TPU v7x, 32 devices: a whole 2x2x4 slice. The times are simulated.
32 devices in a mesh: slab: 8 (over z, y), sub: 4 (over x, core).
Axes of the slice: x: 2, y: 2, z: 4, core: 2. Of those that a mesh axis runs over, the one named last changes fastest.
Arguments:
- mode_shapes: bfloat16 [32, 6, 64, 512], P(None, None, 'slab', 'sub')
- span_stiff: float32 [6, 64, 512], P(None, 'slab', 'sub'), may hold values from -4 to 4
- chord_stiff: float32 [6, 64, 512], P(None, 'slab', 'sub'), may hold values from -4 to 4
- span_geo: float32 [64, 512], P('slab', 'sub'), may hold values from 0.2 to 2
- chord_geo: float32 [64, 512], P('slab', 'sub'), may hold values from 0.2 to 2
- ground: float32 [6, 64, 512], P(None, 'slab', 'sub'), may hold values from 0.2 to 2
- chord_len: int32 [64], replicated, may hold values from 192 to 512, as said below
Outputs:
- adjoint: float32 [32, 6, 64, 512], P(None, None, 'slab', 'sub')
- residual: float32 [32, 6, 64, 512], P(None, None, 'slab', 'sub')
Inputs may be any that keep to these rules, and one draw needn't show every extreme that they name: chord_len[0] = 512.
All inputs are finite; a program needn't handle non-finite values.
Results may differ from a plain program's by a relative error of at most 0.0003.
Values sent between devices are 32-bit elements; how exact they have to be, the bound alone decides.
No kernel may reach another device: no remote copies, remote signals or barrier semaphores. Data moves between devices by JAX's collectives and lax.ppermute only.
A program may use at most 64 MiB of HBM per device.

v0:
```python
import jax
import jax.numpy as jnp
from jax import lax
from jax.sharding import PartitionSpec as P

ITERS = 2


def from_behind(value, axis, steps):
    count = lax.axis_size(axis)
    initial, last = (max(0, -steps), min(count, count - steps))
    return lax.ppermute(value, axis, [(source, source + steps) for source in range(initial, last)])


def factor_blocks(blocks):
    count = len(blocks)
    factor = [[None] * count for i in range(count)]
    inverse = [None] * count
    for j in range(count):
        running = blocks[j][j]
        for k in range(j):
            running = running - factor[j][k] * factor[j][k]
        diag_root = jnp.sqrt(running)
        factor[j][j] = diag_root
        inverse[j] = 1.0 / diag_root
        for i in range(j + 1, count):
            running = blocks[i][j]
            for k in range(j):
                running = running - factor[i][k] * factor[j][k]
            factor[i][j] = running * inverse[j]
    return (factor, inverse)


def solve_blocks(factor, inverse, vector):
    count = len(inverse)
    forward = []
    for i in range(count):
        running = vector[:, i]
        for j in range(i):
            running = running - factor[i][j][None] * forward[j]
        forward.append(running * inverse[i][None])
    backward = [None] * count
    for i in reversed(range(count)):
        running = forward[i]
        for j in range(i + 1, count):
            running = running - factor[j][i][None] * backward[j]
        backward[i] = running * inverse[i][None]
    return jnp.stack(backward, axis=1)


def neighbours_ahead(field):
    next_station = from_behind(field[:, :, :1, :], "slab", -1)
    next_column = from_behind(field[:, :, :, :1], "sub", -1)
    span_next = jnp.concatenate([field[:, :, 1:, :], next_station], axis=2)
    chord_next = jnp.concatenate([field[:, :, :, 1:], next_column], axis=3)
    return (span_next, chord_next)


def forces_behind(span_forces, chord_forces):
    from_span = from_behind(span_forces[:, :, -1:, :], "slab", 1)
    from_chord = from_behind(chord_forces[:, :, :, -1:], "sub", 1)
    span_part = jnp.concatenate([from_span, span_forces[:, :, :-1, :]], axis=2)
    chord_part = jnp.concatenate([from_chord, chord_forces[:, :, :, :-1]], axis=3)
    return span_part + chord_part


def edge_forces(stiffness, jump, live_mask):
    strain = jnp.sum(stiffness[None] * jump, axis=1) * live_mask[None]
    return stiffness[None] * strain[:, None]


def operate_sent(field, span_stiff, chord_stiff, span_live, chord_live, ground):
    span_next, chord_next = neighbours_ahead(field)
    span_forces = edge_forces(span_stiff, span_next - field, span_live)
    chord_forces = edge_forces(chord_stiff, chord_next - field, chord_live)
    return (
        ground[None] * field - span_forces - chord_forces + forces_behind(span_forces, chord_forces)
    )


def inner_rz(first, second):
    return lax.psum(jnp.sum(first * second, axis=(1, 2, 3)), ("slab", "sub"))


def inner_pq(first, second):
    return lax.psum(jnp.sum(first * second, axis=(1, 2, 3)), ("slab", "sub"))


def body(mode_shapes, span_stiff, chord_stiff, span_geo, chord_geo, ground, chord_len):
    count = ground.shape[0]
    stations = ground.shape[1]
    columns = ground.shape[2]
    row_start = lax.axis_index("slab") * stations
    col_start = lax.axis_index("sub") * columns
    padded_len = jnp.concatenate(
        [jnp.zeros((1,), jnp.int32), chord_len, jnp.zeros((2,), jnp.int32)]
    )
    window = lax.dynamic_slice_in_dim(padded_len, row_start, stations + 2)
    col_global = (col_start + jnp.arange(columns, dtype=jnp.int32))[None, :]
    span_mask_wide = ((col_global < window[:-1, None]) & (col_global < window[1:, None])).astype(
        jnp.float32
    )
    col_wide = (col_start - 1 + jnp.arange(columns + 1, dtype=jnp.int32))[None, :]
    own_len = window[1 : stations + 1, None]
    chord_mask_wide = ((col_wide + 1 < own_len) & (col_wide >= 0)).astype(jnp.float32)
    span_live = span_mask_wide[1:]
    chord_live = chord_mask_wide[:, 1:]
    ghost_span = from_behind(span_stiff[:, stations - 1 :, :], "slab", 1)
    ghost_chord = from_behind(chord_stiff[:, :, columns - 1 :], "sub", 1)
    span_wide = jnp.concatenate([ghost_span, span_stiff], axis=1)
    chord_wide = jnp.concatenate([ghost_chord, chord_stiff], axis=2)
    blocks = []
    for i in range(count):
        block_row = []
        for j in range(count):
            span_pair = span_wide[i] * span_wide[j] * span_mask_wide
            chord_pair = chord_wide[i] * chord_wide[j] * chord_mask_wide
            entry = span_pair[1:] + span_pair[:-1] + chord_pair[:, 1:] + chord_pair[:, :-1]
            if i == j:
                entry = entry + ground[i]
            block_row.append(entry)
        blocks.append(block_row)
    factor, inverse = factor_blocks(blocks)
    mode_field = mode_shapes.astype(jnp.float32)
    span_next, chord_next = neighbours_ahead(mode_field)
    span_jump = span_next - mode_field
    chord_jump = chord_next - mode_field
    span_weight = jnp.sum(span_jump * span_jump, axis=1) * (span_geo * span_live)[None]
    chord_weight = jnp.sum(chord_jump * chord_jump, axis=1) * (chord_geo * chord_live)[None]
    span_load = span_stiff[None] * span_weight[:, None]
    chord_load = chord_stiff[None] * chord_weight[:, None]
    load = forces_behind(span_load, chord_load) - span_load - chord_load
    solution = jnp.zeros_like(load)
    residual = load
    precond = solve_blocks(factor, inverse, residual)
    direction = precond
    precond_norm = inner_rz(residual, precond)
    for step in range(ITERS):
        image = operate_sent(direction, span_stiff, chord_stiff, span_live, chord_live, ground)
        step_size = precond_norm / inner_pq(direction, image)
        solution = solution + step_size[:, None, None, None] * direction
        residual = residual - step_size[:, None, None, None] * image
        if step + 1 < ITERS:
            precond = solve_blocks(factor, inverse, residual)
            norm_next = inner_rz(residual, precond)
            direction = precond + (norm_next / precond_norm)[:, None, None, None] * direction
            precond_norm = norm_next
    return (solution, residual)


def solution(mesh):
    return jax.shard_map(
        body,
        mesh=mesh,
        in_specs=(
            P(None, None, "slab", "sub"),
            P(None, "slab", "sub"),
            P(None, "slab", "sub"),
            P("slab", "sub"),
            P("slab", "sub"),
            P(None, "slab", "sub"),
            P(),
        ),
        out_specs=(P(None, None, "slab", "sub"), P(None, None, "slab", "sub")),
        check_vma=False,
    )
```

profile of v0, /device:TPU:0, one launch (start us, length us, event | category | flops | bytes accessed | tf_op | source)
XLA Modules:
  0.0 225.4 jit_solution(9852049154017646248)
XLA Ops:
  1.4 4.9 %collective-permute-start.4 = (f32[6,1,128]{2,1,0:T(1,128)S(1)}, f32[6,1,128]{2,1,0:T(1,128)S(1)}, u32[]{:S(2)}, u32[]{:S(2)}) collective-permute-start(f32[6,1,128]{2,1,0:T(1,128)S(1)} %slice.527), channel_id=1, source_target_pairs={{0,4},{4,8},{8,12},{12,16},{16,20},{20,24},{24,28},{1,5},{5,9},{9,... | collective-permute-start | bytes 9224 | tf_op jit(solution)/shard_map/ppermute | solution.py:12
  7.1 1.5 collective-permute-start.5
  10.0 1.3 collective-permute-start.2
  11.3 1.3 collective-permute-start
  24.0 5.2 %collective-permute-start.1 = (f32[32,6,1,128]{3,0,2,1:T(8,128)S(1)}, f32[32,6,1,128]{3,0,2,1:T(8,128)}, u32[]{:S(2)}, u32[]{:S(2)}) collective-permute-start(f32[32,6,1,128]{3,0,2,1:T(8,128)S(1)} %slice.663), channel_id=1, source_target_pairs={{0,4},{4,8},{8,12},{12,16},{16,20},{20,24},{24,28},{1,5},{5,9},{9,... | collective-permute-start | bytes 294920 | tf_op jit(solution)/shard_map/ppermute | solution.py:12
  30.0 4.0 %collective-permute-start.3 = (f32[32,6,8,1]{0,2,3,1:T(8,128)S(1)}, f32[32,6,8,1]{0,2,3,1:T(8,128)S(1)}, u32[]{:S(2)}, u32[]{:S(2)}) collective-permute-start(f32[32,6,8,1]{0,2,3,1:T(8,128)S(1)} %copy.12), channel_id=1, source_target_pairs={{0,1},{1,2},{2,3},{4,5},{5,6},{6,7},{8,9},{9,10},{10,11},{12,13},{... | collective-permute-start | bytes 18440 | tf_op jit(solution)/shard_map/ppermute | solution.py:12
  35.3 1.3 fusion.3
  38.3 1.3 collective-permute-start.7
  39.6 1.3 collective-permute-start.6
  43.6 2.5 %collective-permute-done.6 = f32[32,6,1,128]{3,0,2,1:T(8,128)S(1)} collective-permute-done((f32[32,6,1,128]{3,0,2,1:T(8,128)S(1)}, f32[32,6,1,128]{3,0,2,1:T(8,128)S(1)}, u32[]{:S(2)}, u32[]{:S(2)}) %collective-permute-start.6) | collective-permute-done | bytes 98336 | tf_op jit(solution)/shard_map/ppermute | solution.py:12
  46.1 1.6 fusion.9
  48.5 5.2 %collective-permute-start.8 = (f32[32,6,1,128]{3,0,2,1:T(8,128)}, f32[32,6,1,128]{3,0,2,1:T(8,128)}, u32[]{:S(2)}, u32[]{:S(2)}) collective-permute-start(f32[32,6,1,128]{3,0,2,1:T(8,128)} %slice.784), channel_id=1, source_target_pairs={{0,4},{4,8},{8,12},{12,16},{16,20},{20,24},{24,28},{1,5},{5,9},{9,... | collective-permute-start | bytes 294920 | tf_op jit(solution)/shard_map/ppermute | solution.py:12
  55.0 2.1 copy.16
  57.1 4.1 %collective-permute-start.9 = (f32[32,6,8,1]{0,2,3,1:T(8,128)}, f32[32,6,8,1]{0,2,3,1:T(8,128)}, u32[]{:S(2)}, u32[]{:S(2)}) collective-permute-start(f32[32,6,8,1]{0,2,3,1:T(8,128)} %copy.16), channel_id=1, source_target_pairs={{0,1},{1,2},{2,3},{4,5},{5,6},{6,7},{8,9},{9,10},{10,11},{12,13},{... | collective-permute-start | bytes 18440 | tf_op jit(solution)/shard_map/ppermute | solution.py:12
  61.8 2.0 copy.17
  63.8 2.6 %multiply_reduce_fusion.2 = (f32[32]{0:T(128)S(1)}, f32[32]{0:T(128)S(1)}, f32[32,6,8,128]{3,0,2,1:T(8,128)}) fusion(f32[32,6,8,128]{3,0,2,1:T(8,128)S(1)} %constant_dynamic-update-slice_fusion, f32[32,6,8,128]{3,0,2,1:T(8,128)S(1)} %fusion.3, f32[32,6,8,127]{3,0,2,1:T(8,128)S(1)} %bitcast.117, f32[32,6,8,1]{3,0,2,1:T(8,128)} %copy.17, ...), kind=kLoop, calls=%fused_computation.31 | loop fusion | flops 2555840 | bytes 4268288 | tf_op jit(solution)/shard_map/reduce_sum | solution.py:86
  66.4 43.7 %all-reduce = (f32[32]{0:T(128)S(1)}, f32[32]{0:T(128)S(1)}) all-reduce(f32[32]{0:T(128)S(1)} %get-tuple-element.7, f32[32]{0:T(128)S(1)} %get-tuple-element.6), channel_id=1, replica_groups=mesh['slab'=8,'sub'=4] {'slab','sub'}, use_global_device_ids=true, to_apply=%region_3.0 | all-reduce | flops 64 | bytes 512 | tf_op jit(solution)/shard_map/psum | solution.py:82
  110.7 1.3 multiply_subtract_fusion.1
  113.0 40.6 %psum.30 = f32[32]{0:T(128)S(1)} all-reduce(f32[32]{0:T(128)S(1)} %multiply_reduce_fusion.1), channel_id=1, replica_groups=mesh['slab'=8,'sub'=4] {'slab','sub'}, use_global_device_ids=true, to_apply=%region_9.0 | all-reduce | flops 32 | bytes 256 | tf_op jit(solution)/shard_map/psum | solution.py:82
  153.9 1.3 collective-permute-start.10
  155.5 1.3 collective-permute-start.11
  160.7 1.8 fusion.14
  164.2 5.4 %collective-permute-start.12 = (f32[32,6,1,128]{3,0,2,1:T(8,128)}, f32[32,6,1,128]{3,0,2,1:T(8,128)}, u32[]{:S(2)}, u32[]{:S(2)}) collective-permute-start(f32[32,6,1,128]{3,0,2,1:T(8,128)} %slice.798), channel_id=1, source_target_pairs={{0,4},{4,8},{8,12},{12,16},{16,20},{20,24},{24,28},{1,5},{5,9},{9,... | collective-permute-start | bytes 294920 | tf_op jit(solution)/shard_map/ppermute | solution.py:12
  170.9 1.5 copy.20
  172.3 3.5 %collective-permute-start.13 = (f32[32,6,8,1]{0,2,3,1:T(8,128)S(1)}, f32[32,6,8,1]{0,2,3,1:T(8,128)S(1)}, u32[]{:S(2)}, u32[]{:S(2)}) collective-permute-start(f32[32,6,8,1]{0,2,3,1:T(8,128)S(1)} %copy.20), channel_id=1, source_target_pairs={{0,1},{1,2},{2,3},{4,5},{5,6},{6,7},{8,9},{9,10},{10,11},{12,13},{... | collective-permute-start | bytes 18440 | tf_op jit(solution)/shard_map/ppermute | solution.py:12
  175.8 2.0 slice.799
  177.8 1.2 copy.21
  179.1 2.7 %multiply_reduce_fusion = (f32[32]{0:T(128)S(1)}, f32[32,6,8,128]{3,0,2,1:T(8,128)}) fusion(f32[32,6,8,128]{3,0,2,1:T(8,128)S(1)} %multiply_add_fusion.1, f32[32,6,8,127]{3,0,2,1:T(8,128)S(1)} %bitcast.115, f32[32,6,8,1]{3,0,2,1:T(8,128)} %copy.21, f32[32,6,7,128]{3,0,2,1:T(8,128)} %slice.799, f32[32,6,1,128]{3,0,2,1:T(8,128)} %collective-permute-done.12, ...), kind=kLoop, calls=%fused_computation.27 | loop fusion | flops 2162656 | bytes 3481728 | tf_op jit(solution)/shard_map/reduce_sum | solution.py:86
  181.8 38.7 %psum.31 = f32[32]{0:T(128)S(1)} all-reduce(f32[32]{0:T(128)S(1)} %get-tuple-element.14), channel_id=1, replica_groups=mesh['slab'=8,'sub'=4] {'slab','sub'}, use_global_device_ids=true, to_apply=%region_13.0 | all-reduce | flops 32 | bytes 256 | tf_op jit(solution)/shard_map/psum | solution.py:86
  221.1 1.5 multiply_subtract_fusion
  222.7 1.3 copy.23
  224.0 1.3 copy.22
  (159 shorter events, 32.8 us)
Async XLA Ops:
  1.4 16.4 %collective-permute-start.4 = (f32[6,1,128]{2,1,0:T(1,128)S(1)}, f32[6,1,128]{2,1,0:T(1,128)S(1)}, u32[]{:S(2)}, u32[]{:S(2)}) collective-permute-start(f32[6,1,128]{2,1,0:T(1,128)S(1)} %slice.527), channel_id=1, source_target_pairs={{0,4},{4,8},{8,12},{12,16},{16,20},{20,24},{24,28},{1,5},{5,9},{9,... | collective-permute-start | bytes 9224 | tf_op jit(solution)/shard_map/ppermute | solution.py:12
  7.1 10.0 %collective-permute-start.5 = (f32[6,8,1]{2,1,0:T(8,128)S(1)}, f32[6,8,1]{2,1,0:T(8,128)S(1)}, u32[]{:S(2)}, u32[]{:S(2)}) collective-permute-start(f32[6,8,1]{2,1,0:T(8,128)S(1)} %slice.531), channel_id=1, source_target_pairs={{0,1},{1,2},{2,3},{4,5},{5,6},{6,7},{8,9},{9,10},{10,11},{12,13},{... | collective-permute-start | bytes 584 | tf_op jit(solution)/shard_map/ppermute | solution.py:12
  10.0 12.3 %collective-permute-start.2 = (f32[32,6,8,1]{0,2,3,1:T(8,128)S(1)}, f32[32,6,8,1]{0,2,3,1:T(8,128)S(1)}, u32[]{:S(2)}, u32[]{:S(2)}) collective-permute-start(f32[32,6,8,1]{0,2,3,1:T(8,128)S(1)} %copy.10), channel_id=1, source_target_pairs={{1,0},{2,1},{3,2},{5,4},{6,5},{7,6},{9,8},{10,9},{11,10},{13,12},{... | collective-permute-start | bytes 18440 | tf_op jit(solution)/shard_map/ppermute | solution.py:12
  11.3 11.3 %collective-permute-start = (f32[32,6,1,128]{3,0,2,1:T(8,128)S(1)}, f32[32,6,1,128]{3,0,2,1:T(8,128)S(1)}, u32[]{:S(2)}, u32[]{:S(2)}) collective-permute-start(f32[32,6,1,128]{3,0,2,1:T(8,128)S(1)} %slice.661), channel_id=1, source_target_pairs={{4,0},{8,4},{12,8},{16,12},{20,16},{24,20},{28,24},{5,1},{9,5},{13... | collective-permute-start | bytes 294920 | tf_op jit(solution)/shard_map/ppermute | solution.py:12
  17.8 3.2 %copy-start.7 = (f32[8,129]{1,0:T(8,128)}, f32[8,129]{1,0:T(8,128)S(1)}, u32[]{:S(2)}) copy-start(f32[8,129]{1,0:T(8,128)S(1)} %get-tuple-element.95) | copy-start | bytes 12388
  22.2 1.0 copy-start.5
  24.0 10.1 %copy-start = (f32[32,6,8,128]{3,0,2,1:T(8,128)}, f32[32,6,8,128]{3,0,2,1:T(8,128)S(1)}, u32[]{:S(2)}) copy-start(f32[32,6,8,128]{3,0,2,1:T(8,128)S(1)} %broadcast_multiply_fusion.5) | copy-start | bytes 2359300
  24.0 5.2 %copy-start.21 = (f32[8,128]{1,0:T(8,128)S(1)}, f32[8,128]{1,0:T(8,128)}, u32[]{:S(2)}) copy-start(f32[8,128]{1,0:T(8,128)} %slice_select_fusion) | copy-start | bytes 12292
  24.0 11.2 %collective-permute-start.1 = (f32[32,6,1,128]{3,0,2,1:T(8,128)S(1)}, f32[32,6,1,128]{3,0,2,1:T(8,128)}, u32[]{:S(2)}, u32[]{:S(2)}) collective-permute-start(f32[32,6,1,128]{3,0,2,1:T(8,128)S(1)} %slice.663), channel_id=1, source_target_pairs={{0,4},{4,8},{8,12},{12,16},{16,20},{20,24},{24,28},{1,5},{5,9},{9,... | collective-permute-start | bytes 294920 | tf_op jit(solution)/shard_map/ppermute | solution.py:12
  29.6 4.4 %copy-start.8 = (f32[8,129]{1,0:T(8,128)S(1)}, f32[8,129]{1,0:T(8,128)}, u32[]{:S(2)}) copy-start(f32[8,129]{1,0:T(8,128)} %copy-done.7) | copy-start | bytes 12388
  29.6 4.4 %copy-start.20 = (f32[8,128]{1,0:T(8,128)S(1)}, f32[8,128]{1,0:T(8,128)}, u32[]{:S(2)}) copy-start(f32[8,128]{1,0:T(8,128)} %copy-done.19) | copy-start | bytes 12292
  30.0 4.9 %collective-permute-start.3 = (f32[32,6,8,1]{0,2,3,1:T(8,128)S(1)}, f32[32,6,8,1]{0,2,3,1:T(8,128)S(1)}, u32[]{:S(2)}, u32[]{:S(2)}) collective-permute-start(f32[32,6,8,1]{0,2,3,1:T(8,128)S(1)} %copy.12), channel_id=1, source_target_pairs={{0,1},{1,2},{2,3},{4,5},{5,6},{6,7},{8,9},{9,10},{10,11},{12,13},{... | collective-permute-start | bytes 18440 | tf_op jit(solution)/shard_map/ppermute | solution.py:12
  34.1 1.1 slice-start
  35.2 1.3 copy-start.15
  37.9 3.0 %copy-start.24 = (pred[9,128]{1,0:T(8,128)(4,1)S(1)}, pred[9,128]{1,0:T(8,128)(4,1)}, u32[]{:S(2)}) copy-start(pred[9,128]{1,0:T(8,128)(4,1)} %copy-done.23) | copy-start | bytes 3460
  38.3 5.0 %collective-permute-start.7 = (f32[32,6,8,1]{0,2,3,1:T(8,128)S(1)}, f32[32,6,8,1]{0,2,3,1:T(8,128)S(1)}, u32[]{:S(2)}, u32[]{:S(2)}) collective-permute-start(f32[32,6,8,1]{0,2,3,1:T(8,128)S(1)} %copy.14), channel_id=1, source_target_pairs={{1,0},{2,1},{3,2},{5,4},{6,5},{7,6},{9,8},{10,9},{11,10},{13,12},{... | collective-permute-start | bytes 18440 | tf_op jit(solution)/shard_map/ppermute | solution.py:12
  39.6 6.5 %collective-permute-start.6 = (f32[32,6,1,128]{3,0,2,1:T(8,128)S(1)}, f32[32,6,1,128]{3,0,2,1:T(8,128)S(1)}, u32[]{:S(2)}, u32[]{:S(2)}) collective-permute-start(f32[32,6,1,128]{3,0,2,1:T(8,128)S(1)} %slice.781), channel_id=1, source_target_pairs={{4,0},{8,4},{12,8},{16,12},{20,16},{24,20},{28,24},{5,1},{9,5},{13... | collective-permute-start | bytes 294920 | tf_op jit(solution)/shard_map/ppermute | solution.py:12
  40.9 6.7 %copy-start.17 = (f32[8,128]{1,0:T(8,128)}, f32[8,128]{1,0:T(8,128)S(1)}, u32[]{:S(2)}) copy-start(f32[8,128]{1,0:T(8,128)S(1)} %slice_convert_fusion.1) | copy-start | bytes 12292
  47.8 13.4 %copy-start.1 = (f32[32,6,8,128]{3,0,2,1:T(8,128)}, f32[32,6,8,128]{3,0,2,1:T(8,128)S(1)}, u32[]{:S(2)}) copy-start(f32[32,6,8,128]{3,0,2,1:T(8,128)S(1)} %broadcast_multiply_fusion.3) | copy-start | bytes 2359300
  47.8 6.0 %copy-start.9 = (f32[8,128]{1,0:T(8,128)S(1)}, f32[8,128]{1,0:T(8,128)}, u32[]{:S(2)}) copy-start(f32[8,128]{1,0:T(8,128)} %slice_convert_fusion) | copy-start | bytes 12292
  48.5 15.2 %collective-permute-start.8 = (f32[32,6,1,128]{3,0,2,1:T(8,128)}, f32[32,6,1,128]{3,0,2,1:T(8,128)}, u32[]{:S(2)}, u32[]{:S(2)}) collective-permute-start(f32[32,6,1,128]{3,0,2,1:T(8,128)} %slice.784), channel_id=1, source_target_pairs={{0,4},{4,8},{8,12},{12,16},{16,20},{20,24},{24,28},{1,5},{5,9},{9,... | collective-permute-start | bytes 294920 | tf_op jit(solution)/shard_map/ppermute | solution.py:12
  57.1 4.7 %collective-permute-start.9 = (f32[32,6,8,1]{0,2,3,1:T(8,128)}, f32[32,6,8,1]{0,2,3,1:T(8,128)}, u32[]{:S(2)}, u32[]{:S(2)}) collective-permute-start(f32[32,6,8,1]{0,2,3,1:T(8,128)} %copy.16), channel_id=1, source_target_pairs={{0,1},{1,2},{2,3},{4,5},{5,6},{6,7},{8,9},{9,10},{10,11},{12,13},{... | collective-permute-start | bytes 18440 | tf_op jit(solution)/shard_map/ppermute | solution.py:12
  61.2 2.6 %slice-start.1 = ((f32[32,6,8,128]{3,0,2,1:T(8,128)}), f32[32,6,7,128]{3,0,2,1:T(8,128)S(1)}, s32[]{:S(2)}) async-start(f32[32,6,8,128]{3,0,2,1:T(8,128)} %copy-done.1), calls=%async_computation.1 | async-start | bytes 1376256 | tf_op jit(solution)/shard_map/slice | solution.py:62
  110.7 1.4 copy-start.12
  110.7 1.4 copy-start.14
  110.7 1.4 copy-start.16
  153.9 6.8 %collective-permute-start.10 = (f32[32,6,1,128]{3,0,2,1:T(8,128)S(1)}, f32[32,6,1,128]{3,0,2,1:T(8,128)S(1)}, u32[]{:S(2)}, u32[]{:S(2)}) collective-permute-start(f32[32,6,1,128]{3,0,2,1:T(8,128)S(1)} %slice.795), channel_id=1, source_target_pairs={{4,0},{8,4},{12,8},{16,12},{20,16},{24,20},{28,24},{5,1},{9,5},{13... | collective-permute-start | bytes 294920 | tf_op jit(solution)/shard_map/ppermute | solution.py:12
  155.5 3.1 %collective-permute-start.11 = (f32[32,6,8,1]{0,2,3,1:T(8,128)S(1)}, f32[32,6,8,1]{0,2,3,1:T(8,128)S(1)}, u32[]{:S(2)}, u32[]{:S(2)}) collective-permute-start(f32[32,6,8,1]{0,2,3,1:T(8,128)S(1)} %copy.18), channel_id=1, source_target_pairs={{1,0},{2,1},{3,2},{5,4},{6,5},{7,6},{9,8},{10,9},{11,10},{13,12},{... | collective-permute-start | bytes 18440 | tf_op jit(solution)/shard_map/ppermute | solution.py:12
  160.7 1.8 copy-start.10
  163.2 0.9 copy-start.2
  164.2 14.9 %collective-permute-start.12 = (f32[32,6,1,128]{3,0,2,1:T(8,128)}, f32[32,6,1,128]{3,0,2,1:T(8,128)}, u32[]{:S(2)}, u32[]{:S(2)}) collective-permute-start(f32[32,6,1,128]{3,0,2,1:T(8,128)} %slice.798), channel_id=1, source_target_pairs={{0,4},{4,8},{8,12},{12,16},{16,20},{20,24},{24,28},{1,5},{5,9},{9,... | collective-permute-start | bytes 294920 | tf_op jit(solution)/shard_map/ppermute | solution.py:12
  172.3 5.5 %collective-permute-start.13 = (f32[32,6,8,1]{0,2,3,1:T(8,128)S(1)}, f32[32,6,8,1]{0,2,3,1:T(8,128)S(1)}, u32[]{:S(2)}, u32[]{:S(2)}) collective-permute-start(f32[32,6,8,1]{0,2,3,1:T(8,128)S(1)} %copy.20), channel_id=1, source_target_pairs={{0,1},{1,2},{2,3},{4,5},{5,6},{6,7},{8,9},{9,10},{10,11},{12,13},{... | collective-permute-start | bytes 18440 | tf_op jit(solution)/shard_map/ppermute | solution.py:12
  (14 other events, 9.4 us)
where the time goes:
time: 227 us; the launch traced here: 225 us
  blocking collectives  123 us (54%)
  starting transfers between devices  41.5 us (18%)
  local copies, waits for them, and re-layouts  31.6 us (14%)
  other arithmetic  21.6 us (10%)
  waiting for transfers between devices  6.4 us (3%)
    psum x2, blocking collectives, inner_rz(): return lax.psum(jnp.sum(first * second, axis=(1, 2, 3)), ('slab', 'sub'))  84.3 us
    ppermute x14, starting transfers between devices, from_behind(): lax.ppermute(value, axis, [(source, source + steps) for source in range(i...  41.5 us
    psum x1, blocking collectives, inner_pq(): return lax.psum(jnp.sum(first * second, axis=(1, 2, 3)), ('slab', 'sub'))  38.7 us
    unnamed x64, local copies, waits for them, and re-layouts  10.6 us
    slice x6, local copies, waits for them, and re-layouts, forces_behind(): from_chord = from_behind(chord_forces[:, :, :, -1:], 'sub', 1)  6.48 us
    ppermute x14, waiting for transfers between devices, from_behind(): lax.ppermute(value, axis, [(source, source + steps) for source in range(i...  6.4 us
    ppermute x6, local copies, waits for them, and re-layouts, from_behind(): lax.ppermute(value, axis, [(source, source + steps) for source in range(i...  5.55 us
    reduce_sum x2, other arithmetic, inner_pq(): return lax.psum(jnp.sum(first * second, axis=(1, 2, 3)), ('slab', 'sub'))  5.36 us
  transfers between devices with their start and end apart: 14, of which 6 were waited for; matrix products, arithmetic and copies ran while one was open for 11% of the time, Pallas kernels for 0%

commit v1 on v0

v1 whole, which is shorter than its diff:
```python
import jax
import jax.numpy as jnp
from jax import lax
from jax.experimental import pallas as pl
from jax.experimental.pallas import tpu as pltpu
from jax.sharding import PartitionSpec as P

F32 = jnp.float32
VMEM_LIMIT = 24 * 1024 * 1024


def matching(slabs, subs, along_slab, parity):
    pairs = []
    for s in range(slabs):
        for c in range(subs):
            here, count = (s, slabs) if along_slab else (c, subs)
            there = here + 1 if here % 2 == parity else here - 1
            if 0 <= there < count:
                target = (there, c) if along_slab else (s, there)
            elif along_slab:
                target = (s, c ^ 1) if subs % 2 == 0 else None
            else:
                target = (s, subs - 1 - c) if subs % 2 == 0 else None
            if target is not None:
                pairs.append((s * subs + c, target[0] * subs + target[1]))
    return pairs


def roll(value, shift, axis):
    size = value.shape[axis]
    if isinstance(shift, int):
        return pltpu.roll(value, shift % size, axis)
    return pltpu.roll(value, lax.rem(shift + size, size), axis)


def dot(left, right):
    total = left[0] * right[0]
    for k in range(1, len(left)):
        total = total + left[k] * right[k]
    return total


def axpy4(coefs, values):
    total = coefs[0] * values[0]
    for k in range(1, len(coefs)):
        total = total + coefs[k] * values[k]
    return total


def tile_iota(shape):
    return lax.broadcasted_iota(jnp.int32, shape, 0), lax.broadcasted_iota(jnp.int32, shape, 1)


def parities():
    return lax.rem(lax.axis_index("slab"), 2) == 0, lax.rem(lax.axis_index("sub"), 2) == 0


def pack_kernel(dims, modes_ref, span_ref, chord_ref, span_geo_ref, chord_geo_ref,
                row_even, row_odd, col_even, col_odd, field):
    modes, dof, rows, cols = dims
    row, lane = tile_iota((rows, cols))
    slab_even, sub_even = parities()
    per = dof * rows

    def body(m, carry):
        start = pl.multiple_of(m * per, per)
        block = modes_ref[pl.ds(start, per), :].astype(F32)
        field[pl.ds(start, per), :] = block
        mine = (lane >> 1) == m
        return tuple(
            jnp.where(mine, roll(block[k * rows:(k + 1) * rows], 2 * m + 1, 1), carry[k]) for k in range(dof)
        )

    packed = lax.fori_loop(0, modes, body, tuple(jnp.zeros((rows, cols), F32) for k in range(dof)))
    coef = jnp.zeros((rows, cols), F32)
    edge = jnp.zeros((rows, cols), F32)
    for k in range(dof + 1):
        span_plane = span_ref[k] if k < dof else span_geo_ref[...]
        chord_plane = chord_ref[k] if k < dof else chord_geo_ref[...]
        coef = jnp.where(row == k, span_plane[rows - 1:rows], coef)
        edge = jnp.where(lane == 2 * k, roll(chord_plane, 2 * k + 1, 1), edge)
    for k in range(dof):
        behind = roll(packed[k], -1, 1)
        col_even[k * rows:(k + 1) * rows, :] = jnp.where(sub_even, packed[k], behind)
        col_odd[k * rows:(k + 1) * rows, :] = jnp.where(sub_even, behind, packed[k])
        for block in range(modes // 8):
            base = block * 8 * per + k * rows
            first = field[pl.ds(base, 8, stride=per), :]
            last = field[pl.ds(base + rows - 1, 8, stride=per), :]
            out = k * modes + block * 8
            row_even[out:out + 8, :] = jnp.where(slab_even, last, first)
            row_odd[out:out + 8, :] = jnp.where(slab_even, first, last)
    row_even[dof * modes:dof * modes + rows, :] = coef
    row_odd[dof * modes:dof * modes + rows, :] = coef
    col_even[dof * rows:(dof + 1) * rows, :] = edge
    col_odd[dof * rows:(dof + 1) * rows, :] = edge


def factor_blocks(blocks):
    count = len(blocks)
    factor = [[None] * count for i in range(count)]
    inverse = [None] * count
    for j in range(count):
        running = blocks[j][j]
        for k in range(j):
            running = running - factor[j][k] * factor[j][k]
        diag_root = jnp.sqrt(running)
        factor[j][j] = diag_root
        inverse[j] = 1.0 / diag_root
        for i in range(j + 1, count):
            running = blocks[i][j]
            for k in range(j):
                running = running - factor[i][k] * factor[j][k]
            factor[i][j] = running * inverse[j]
    return (factor, inverse)


def invert_blocks(blocks):
    count = len(blocks)
    factor, inverse = factor_blocks(blocks)
    lower = [[None] * count for i in range(count)]
    for j in range(count):
        lower[j][j] = inverse[j]
        for i in range(j + 1, count):
            running = factor[i][j] * lower[j][j]
            for k in range(j + 1, i):
                running = running + factor[i][k] * lower[k][j]
            lower[i][j] = -(running * inverse[i])
    result = [[None] * count for i in range(count)]
    for i in range(count):
        for j in range(i + 1):
            running = lower[i][i] * lower[i][j]
            for k in range(i + 1, count):
                running = running + lower[k][i] * lower[k][j]
            result[i][j] = running
    return result


def apply_inverse(entry, vector):
    count = len(vector)
    return [dot([entry(max(i, j), min(i, j)) for j in range(count)], vector) for i in range(count)]


def first_kernel(dims, sizes, modes_ref, span_ref, chord_ref, span_geo_ref, chord_geo_ref, ground_ref, len_ref,
                 row_even_out, row_odd_out, col_even_out, col_odd_out,
                 row_even_in, row_odd_in, col_even_in, col_odd_in,
                 load_ref, z_ref, q_ref, g_ref, coef_ref, row_even, row_odd, col_even, col_odd,
                 inv_ref, up_ref, down_ref, rim_ref, rim2_ref):
    modes, dof, rows, cols = dims
    slabs, subs = sizes
    row, lane = tile_iota((rows, cols))
    slab_even, sub_even = parities()
    per = dof * rows
    stations = slabs * rows
    row_start = lax.axis_index("slab") * rows
    col_start = lax.axis_index("sub") * cols
    column = col_start + lane

    def length(index):
        value = len_ref[jnp.clip(index, 0, stations - 1)]
        return jnp.where((index >= 0) & (index < stations), value, 0)

    own = jnp.zeros((rows, cols), jnp.int32)
    ahead = jnp.zeros((rows, cols), jnp.int32)
    for r in range(rows):
        own = jnp.where(row == r, length(row_start + r), own)
        ahead = jnp.where(row == r, length(row_start + r + 1), ahead)
    span_live = (column < own) & (column < ahead)
    chord_live = column + 1 < own
    up_live = (column < length(row_start - 1)) & (column < length(row_start))
    left_live = (col_start < own) & (col_start > 0)

    def row_weight(arrived, sent):
        total = None
        for k in range(dof):
            jump = arrived[k * modes:(k + 1) * modes, :] - sent[k * modes:(k + 1) * modes, :]
            total = jump * jump if total is None else total + jump * jump
        return total

    def col_weight(arrived, sent):
        total = None
        for k in range(dof):
            jump = arrived[k * rows:(k + 1) * rows, :] - sent[k * rows:(k + 1) * rows, :]
            total = jump * jump if total is None else total + jump * jump
        return total

    even_weight = row_weight(row_even_in, row_even_out)
    odd_weight = row_weight(row_odd_in, row_odd_out)
    up_weight = jnp.where(slab_even, odd_weight, even_weight)
    down_weight = jnp.where(slab_even, even_weight, odd_weight)
    tail = dof * modes
    up_coef = jnp.where(slab_even, row_odd_in[tail:tail + rows, :], row_even_in[tail:tail + rows, :])
    up_ref[...] = jnp.where(up_live[0:1], up_weight * up_coef[dof:dof + 1], 0.0)
    down_ref[...] = jnp.where(span_live[rows - 1:rows], down_weight * span_geo_ref[rows - 1:rows, :], 0.0)
    even_col = col_weight(col_even_in, col_even_out)
    odd_col = col_weight(col_odd_in, col_odd_out)
    left_coef = jnp.where(sub_even, col_odd_in[per:per + rows, :], col_even_in[per:per + rows, :])
    left_weight = jnp.where(sub_even, odd_col, even_col) * left_coef[:, 2 * dof:2 * dof + 1]
    right_weight = jnp.where(sub_even, even_col, odd_col) * chord_geo_ref[:, cols - 1:cols]
    left_weight = jnp.where(left_live, left_weight, 0.0)
    right_weight = jnp.where(chord_live[:, cols - 1:cols], right_weight, 0.0)
    lane_even = (lane & 1) == 0
    rim_weight = jnp.where(lane_even, left_weight, roll(right_weight, -1, 1))

    first_row, last_row = row == 0, row == rows - 1
    first_col, last_col = lane == 0, lane == cols - 1

    zero = jnp.zeros((rows, cols), F32)
    span, span_b, chord, chord_b = [], [], [], []
    for k in range(dof):
        span.append(jnp.where(span_live, span_ref[k], zero))
        up = jnp.where(up_live, up_coef[k:k + 1], zero)
        span_b.append(jnp.where(first_row, up, roll(span[k], 1, 0)))
        chord.append(jnp.where(chord_live, chord_ref[k], zero))
        left = jnp.where(left_live, left_coef[:, 2 * k:2 * k + 1], zero)
        chord_b.append(jnp.where(first_col, left, roll(chord[k], 1, 1)))
    blocks = [[None] * dof for i in range(dof)]
    for i in range(dof):
        for j in range(i + 1):
            entry = span[i] * span[j] + span_b[i] * span_b[j] + chord[i] * chord[j] + chord_b[i] * chord_b[j]
            blocks[i][j] = entry + ground_ref[i] if i == j else entry
    inv = invert_blocks(blocks)
    place = {}
    for i in range(dof):
        for j in range(i + 1):
            place[i, j] = len(place)
            inv_ref[place[i, j]] = inv[i][j]
    row_rim = [jnp.where(last_row, span[k], jnp.where(first_row, span_b[k], zero)) for k in range(dof)]
    col_rim = [jnp.where(last_col, chord[k], jnp.where(first_col, chord_b[k], zero)) for k in range(dof)]
    row_inv = apply_inverse(lambda i, j: inv[i][j], row_rim)
    col_inv = apply_inverse(lambda i, j: inv[i][j], col_rim)
    for group, planes in enumerate((span, span_b, chord, chord_b, row_rim, col_rim, row_inv, col_inv)):
        for k in range(dof):
            coef_ref[group * dof + k] = planes[k]
    row_kappa = dot(row_rim, row_inv)
    col_kappa = dot(col_rim, col_inv)
    coef_ref[8 * dof] = dot(row_rim, col_inv)

    def planes_of(group):
        return [coef_ref[group * dof + k] for k in range(dof)]

    def body(m, carry):
        start = pl.multiple_of(m * per, per)
        block = modes_ref[pl.ds(start, per), :].astype(F32)
        v = [block[k * rows:(k + 1) * rows] for k in range(dof)]
        down = down_ref[pl.ds(m, 1), :]
        up = up_ref[pl.ds(m, 1), :]
        rim = roll(rim_weight, -2 * m, 1)
        jumps = [roll(v[k], -1, 0) - v[k] for k in range(dof)]
        span_w = jnp.where(last_row, down, dot(jumps, jumps) * span_geo_ref[...])
        jumps = [roll(v[k], -1, 1) - v[k] for k in range(dof)]
        chord_w = jnp.where(last_col, rim, dot(jumps, jumps) * chord_geo_ref[...])
        span_wb = jnp.where(first_row, up, roll(span_w, 1, 0))
        chord_wb = jnp.where(first_col, rim, roll(chord_w, 1, 1))
        span, span_b, chord, chord_b = (planes_of(i) for i in range(4))
        load = [
            (span_b[k] * span_wb - span[k] * span_w) + (chord_b[k] * chord_wb - chord[k] * chord_w)
            for k in range(dof)
        ]
        entry = lambda i, j: inv_ref[place[i, j]]
        z = apply_inverse(entry, load)
        fwd_s, bwd_s, fwd_c, bwd_c = dot(span, z), dot(span_b, z), dot(chord, z), dot(chord_b, z)
        near = [
            jnp.where(last_row, zero, roll(bwd_s, -1, 0)),
            jnp.where(first_row, zero, roll(fwd_s, 1, 0)),
            jnp.where(last_col, zero, roll(bwd_c, -1, 1)),
            jnp.where(first_col, zero, roll(fwd_c, 1, 1)),
        ]
        q = [axpy4([span[k], span_b[k], chord[k], chord_b[k]], near) for k in range(dof)]
        g = apply_inverse(entry, q)
        for k in range(dof):
            at = pl.ds(pl.multiple_of(start + k * rows, rows), rows)
            load_ref[at, :] = load[k]
            z_ref[at, :] = z[k]
            q_ref[at, :] = q[k]
            g_ref[at, :] = g[k]
        at = pl.ds(pl.multiple_of(m * rows, rows), rows)
        rim_ref[at, :] = jnp.where(last_row, fwd_s, bwd_s)
        rim2_ref[at, :] = dot(planes_of(4), g)
        mine = (lane >> 1) == m
        col_z = roll(jnp.where(last_col, fwd_c, bwd_c), 2 * m + 1, 1)
        col_g = roll(dot(planes_of(5), g), 2 * m + 1, 1)
        return jnp.where(mine, col_z, carry[0]), jnp.where(mine, col_g, carry[1])

    col_z, col_g = lax.fori_loop(0, modes, body, (zero, zero))
    for which, packed in enumerate((col_z, col_g, roll(col_kappa, 1, 1))):
        behind = roll(packed, -1, 1)
        col_even[which * rows:(which + 1) * rows, :] = jnp.where(sub_even, packed, behind)
        col_odd[which * rows:(which + 1) * rows, :] = jnp.where(sub_even, behind, packed)
    for which, ref in enumerate((rim_ref, rim2_ref)):
        for block in range(modes // 8):
            first = ref[pl.ds(block * 8 * rows, 8, stride=rows), :]
            last = ref[pl.ds(block * 8 * rows + rows - 1, 8, stride=rows), :]
            out = which * modes + block * 8
            row_even[out:out + 8, :] = jnp.where(slab_even, last, first)
            row_odd[out:out + 8, :] = jnp.where(slab_even, first, last)
    first = jnp.where(first_row, row_kappa[0:1], zero)
    last = jnp.where(first_row, row_kappa[rows - 1:rows], zero)
    row_even[2 * modes:2 * modes + rows, :] = jnp.where(slab_even, last, first)
    row_odd[2 * modes:2 * modes + rows, :] = jnp.where(slab_even, first, last)


def second_kernel(dims, devices, load_ref, z_ref, qp_ref, gp_ref, coef_ref,
                  row_even_out, row_odd_out, col_even_out, col_odd_out,
                  row_even_in, row_odd_in, col_even_in, col_odd_in,
                  q_ref, g_ref, q2_ref, chunk_ref,
                  up_ref, down_ref, up2_ref, down2_ref, sum_ref):
    modes, dof, rows, cols = dims
    row, lane = tile_iota((rows, cols))
    slab_even, sub_even = parities()
    per = dof * rows
    first_row, last_row = row == 0, row == rows - 1
    first_col, last_col = lane == 0, lane == cols - 1
    lane_even = (lane & 1) == 0
    zero = jnp.zeros((rows, cols), F32)

    def pick(flag, even, odd, start, size):
        return jnp.where(flag, even[start:start + size, :], odd[start:start + size, :])

    up_flag = jnp.logical_not(slab_even)
    left_flag = jnp.logical_not(sub_even)
    up_ref[...] = pick(up_flag, row_even_in, row_odd_in, 0, modes)
    down_ref[...] = pick(slab_even, row_even_in, row_odd_in, 0, modes)
    up2_ref[...] = (
        pick(up_flag, row_even_in, row_odd_in, modes, modes)
        + pick(up_flag, row_even_in, row_odd_in, 2 * modes, 1) * pick(up_flag, row_even_out, row_odd_out, 0, modes)
    )
    down2_ref[...] = (
        pick(slab_even, row_even_in, row_odd_in, modes, modes)
        + pick(slab_even, row_even_in, row_odd_in, 2 * modes, 1) * pick(slab_even, row_even_out, row_odd_out, 0, modes)
    )

    def merge(left, right):
        return jnp.where(lane_even, left, roll(right, -1, 1))

    def second_col(flag):
        kappa = pick(flag, col_even_in, col_odd_in, 2 * rows, rows)[:, 0:1]
        return pick(flag, col_even_in, col_odd_in, rows, rows) + kappa * pick(flag, col_even_out, col_odd_out, 0, rows)

    rim = merge(pick(left_flag, col_even_in, col_odd_in, 0, rows), pick(sub_even, col_even_in, col_odd_in, 0, rows))
    rim2 = merge(second_col(left_flag), second_col(sub_even))
    corner_kappa = coef_ref[8 * dof]

    def planes_of(group):
        return [coef_ref[group * dof + k] for k in range(dof)]

    def body(m, carry):
        start = pl.multiple_of(m * per, per)
        at = [pl.ds(pl.multiple_of(start + k * rows, rows), rows) for k in range(dof)]
        row_ghost = jnp.where(last_row, down_ref[pl.ds(m, 1), :], up_ref[pl.ds(m, 1), :])
        col_ghost = roll(rim, -2 * m, 1)
        col_ghost2 = roll(rim2, -2 * m, 1)
        row_rim, col_rim, row_inv, col_inv = (planes_of(i) for i in range(4, 8))
        q = [qp_ref[at[k], :] + (row_rim[k] * row_ghost + col_rim[k] * col_ghost) for k in range(dof)]
        g = [gp_ref[at[k], :] + (row_inv[k] * row_ghost + col_inv[k] * col_ghost) for k in range(dof)]
        span, span_b, chord, chord_b = (planes_of(i) for i in range(4))
        fwd_s, bwd_s, fwd_c, bwd_c = dot(span, g), dot(span_b, g), dot(chord, g), dot(chord_b, g)
        near = [
            jnp.where(last_row, down2_ref[pl.ds(m, 1), :], roll(bwd_s, -1, 0)),
            jnp.where(first_row, up2_ref[pl.ds(m, 1), :], roll(fwd_s, 1, 0)),
            jnp.where(last_col, col_ghost2, roll(bwd_c, -1, 1)),
            jnp.where(first_col, col_ghost2, roll(fwd_c, 1, 1)),
        ]
        q2 = [axpy4([span[k], span_b[k], chord[k], chord_b[k]], near) for k in range(dof)]
        z = [z_ref[at[k], :] for k in range(dof)]
        load = [load_ref[at[k], :] for k in range(dof)]
        for which, (left, right) in enumerate(((z, load), (z, q), (g, q), (g, q2))):
            spot = pl.multiple_of((which * modes + m) * rows, rows)
            sum_ref[pl.ds(spot, rows), :] = dot(left, right)
        for k in range(dof):
            q_ref[at[k], :] = q[k]
            g_ref[at[k], :] = g[k]
            q2_ref[at[k], :] = q2[k]
        corners = (
            jnp.where(last_row, fwd_s, bwd_s),
            jnp.where(last_col, fwd_c, bwd_c),
            corner_kappa * col_ghost,
            corner_kappa * row_ghost,
        )
        mine = (lane >> 1) == m
        return tuple(jnp.where(mine, roll(new, 2 * m + 1, 1), old) for new, old in zip(corners, carry))

    corners = lax.fori_loop(0, modes, body, (zero,) * 4)
    sums = []
    for block in range(4 * modes // 8):
        base = block * 8 * rows
        total = sum_ref[pl.ds(base, 8, stride=rows), :]
        for r in range(1, rows):
            total = total + sum_ref[pl.ds(base + r, 8, stride=rows), :]
        sums.append(total)
    sums = jnp.concatenate(sums, axis=0)
    sums = lax.dot_general(
        jnp.ones((8, cols), F32), sums, (((1,), (1,)), ((), ())),
        precision=lax.Precision.HIGHEST, preferred_element_type=F32,
    )
    chunk = jnp.where(first_row, sums[0:1], zero)
    for which, corner in enumerate(corners):
        line = jnp.where(lane < cols // 2, corner[0:1], roll(jnp.broadcast_to(corner[rows - 1:rows], (rows, cols)), cols // 2, 1))
        chunk = jnp.where(row == which + 1, line, chunk)

    def send(d, carry):
        chunk_ref[pl.ds(pl.multiple_of(d * rows, rows), rows), :] = chunk
        return carry

    lax.fori_loop(0, devices, send, 0)


def last_kernel(dims, sizes, steps, part_ref, coef_ref, load_ref, z_ref, q_ref, g_ref, q2_ref,
                adjoint_ref, residual_ref, a_ref, b_ref, fix_ref):
    modes, dof, rows, cols = dims
    slabs, subs = sizes
    devices = slabs * subs
    row, lane = tile_iota((rows, cols))
    per = dof * rows
    half = cols // 2

    @pl.when(pl.program_id(0) == 0)
    def scalars():
        def lines(which):
            return part_ref[pl.ds(which, devices, stride=8), :]

        own_row, own_col, miss_row, miss_col = (lines(i) for i in range(1, 5))
        wide = lax.broadcasted_iota(jnp.int32, (devices, cols), 1)
        swapped = roll(miss_row, half, 1)
        met_row = jnp.where(wide >= half, roll(swapped, -subs, 0), roll(swapped, subs, 0))
        met_col = jnp.where((wide & 1) == 0, roll(roll(miss_col, -1, 1), -1, 0), roll(roll(miss_col, 1, 1), 1, 0))
        total = jnp.sum(lines(0), axis=0, keepdims=True)
        missed = jnp.sum(own_row * met_row + own_col * met_col, axis=0, keepdims=True)
        big_row, big_lane = tile_iota((4 * modes, cols))
        spread = jnp.where(big_row == big_lane, total, 0.0)
        spread = spread + jnp.where(((big_lane & (half - 1)) >> 1) == big_row - 3 * modes, missed, 0.0)
        spread = lax.dot_general(
            spread, jnp.ones((cols, cols), F32), (((1,), (0,)), ((), ())),
            precision=lax.Precision.HIGHEST, preferred_element_type=F32,
        )
        m0, m1, m2, m3 = (spread[i * modes:(i + 1) * modes] for i in range(4))
        step0 = m0 / (m0 - m1)
        rest = 1.0 - step0
        rz1 = rest * rest * m0 + 2.0 * rest * step0 * m1 + step0 * step0 * m2
        c0 = rest + rz1 / m0
        pq1 = c0 * c0 * (m0 - m1) + 2.0 * c0 * step0 * (m1 - m2) + step0 * step0 * (m2 - m3)
        step1 = rz1 / pq1
        a_ref[...] = step0 + step1 * c0
        b_ref[...] = step1 * step0

        here = lax.axis_index("slab") * subs + lax.axis_index("sub")

        def line_of(device, which):
            device = lax.rem(device + devices, devices)
            line = part_ref[pl.ds(device * 8 + which, 1), :]
            return jnp.broadcast_to(line, (rows, cols))

        fix_ref[0:rows, :] = jnp.where(row == rows - 1, line_of(here + subs, 3), roll(line_of(here - subs, 3), half, 1))
        fix = jnp.where((lane & 1) == 0, roll(line_of(here + 1, 4), -1, 1), roll(line_of(here - 1, 4), 1, 1))
        fix_ref[rows:2 * rows, :] = jnp.where(row == rows - 1, roll(fix, half, 1), fix)

    corner = ((row == 0) | (row == rows - 1)) & ((lane == 0) | (lane == cols - 1))
    count = modes // steps

    def body(i, carry):
        m = pl.program_id(0) * count + i
        a = a_ref[pl.ds(m, 1), :]
        b = b_ref[pl.ds(m, 1), :]
        row_fix = b * jnp.where(corner, roll(fix_ref[0:rows, :], cols - 1 - 2 * m, 1), 0.0)
        col_fix = b * jnp.where(corner, roll(fix_ref[rows:2 * rows, :], cols - 1 - 2 * m, 1), 0.0)
        for k in range(dof):
            at = pl.ds(pl.multiple_of(i * per + k * rows, rows), rows)
            adjoint_ref[at, :] = a * z_ref[at, :] + b * g_ref[at, :]
            residual_ref[at, :] = (
                ((1.0 - a) * load_ref[at, :] + (a - b) * q_ref[at, :])
                + (b * q2_ref[at, :] + (coef_ref[4 * dof + k] * row_fix + coef_ref[5 * dof + k] * col_fix))
            )
        return carry

    lax.fori_loop(0, count, body, 0)


def body_of(sizes):
    slabs, subs = sizes
    devices = slabs * subs
    axes = ("slab", "sub")
    paths = [matching(slabs, subs, along, parity) for along in (True, False) for parity in (0, 1)]

    def exchange(arrays):
        return [lax.ppermute(array, axes, path) for array, path in zip(arrays, paths)]

    vmem = pl.BlockSpec(memory_space=pltpu.VMEM)
    smem = pl.BlockSpec(memory_space=pltpu.SMEM)
    params = pltpu.CompilerParams(vmem_limit_bytes=VMEM_LIMIT)

    def body(mode_shapes, span_stiff, chord_stiff, span_geo, chord_geo, ground, chord_len):
        modes, dof, rows, cols = mode_shapes.shape
        dims = mode_shapes.shape
        count = modes * dof * rows
        field = mode_shapes.reshape(count, cols)

        def call(kernel, name, inputs, specs, outs, scratch):
            return pl.pallas_call(
                kernel,
                out_shape=[jax.ShapeDtypeStruct(shape, F32) for shape in outs],
                in_specs=specs,
                out_specs=[vmem] * len(outs),
                scratch_shapes=[pltpu.VMEM(shape, F32) for shape in scratch],
                compiler_params=params,
                name=name,
            )(*inputs)

        row_shape, col_shape = (modes * dof + rows, cols), ((dof + 1) * rows, cols)
        rims = call(
            lambda *refs: pack_kernel(dims, *refs), "pack_rim",
            (field, span_stiff, chord_stiff, span_geo, chord_geo), [vmem] * 5,
            [row_shape, row_shape, col_shape, col_shape], [(count, cols)],
        )
        met = exchange(rims)
        full = (count, cols)
        row_shape, col_shape = (2 * modes + rows, cols), (3 * rows, cols)
        load, z, qp, gp, coef, *rims2 = call(
            lambda *refs: first_kernel(dims, sizes, *refs), "load_and_first",
            (field, span_stiff, chord_stiff, span_geo, chord_geo, ground, chord_len, *rims, *met),
            [vmem] * 6 + [smem] + [vmem] * 8,
            [full] * 4 + [(8 * dof + 1, rows, cols)] + [row_shape, row_shape, col_shape, col_shape],
            [(dof * (dof + 1) // 2, rows, cols), (modes, cols), (modes, cols), (modes * rows, cols), (modes * rows, cols)],
        )
        met2 = exchange(rims2)
        q, g, q2, chunk = call(
            lambda *refs: second_kernel(dims, devices, *refs), "second_and_sums",
            (load, z, qp, gp, coef, *rims2, *met2), [vmem] * 13,
            [full] * 3 + [(devices * 8, cols)],
            [(modes, cols)] * 4 + [(4 * modes * rows, cols)],
        )
        parts = lax.all_to_all(chunk.reshape(devices, 8, cols), axes, 0, 0).reshape(devices * 8, cols)
        steps = 4
        cut = pl.BlockSpec((count // steps, cols), lambda i: (i, 0))
        whole = lambda shape: pl.BlockSpec(shape, lambda i: (0,) * len(shape))
        adjoint, residual = pl.pallas_call(
            lambda *refs: last_kernel(dims, sizes, steps, *refs),
            grid=(steps,),
            out_shape=[jax.ShapeDtypeStruct(full, F32)] * 2,
            in_specs=[whole(parts.shape), whole(coef.shape)] + [cut] * 5,
            out_specs=[cut] * 2,
            scratch_shapes=[pltpu.VMEM((modes, cols), F32), pltpu.VMEM((modes, cols), F32), pltpu.VMEM((2 * rows, cols), F32)],
            compiler_params=params,
            name="combine",
        )(parts, coef, load, z, q, g, q2)
        return adjoint.reshape(dims), residual.reshape(dims)

    return body


def solution(mesh):
    return jax.shard_map(
        body_of((mesh.shape["slab"], mesh.shape["sub"])),
        mesh=mesh,
        in_specs=(
            P(None, None, "slab", "sub"),
            P(None, "slab", "sub"),
            P(None, "slab", "sub"),
            P("slab", "sub"),
            P("slab", "sub"),
            P(None, "slab", "sub"),
            P(),
        ),
        out_specs=(P(None, None, "slab", "sub"), P(None, None, "slab", "sub")),
        check_vma=False,
    )
```

time: 227 us -> 55 us (0.24)
  blocking collectives: 123 us -> 13.3 us
  starting transfers between devices: 41.5 us -> 8.77 us
  local copies, waits for them, and re-layouts: 31.6 us -> 3.84 us
  Pallas kernels: 0 us -> 23.3 us
  other arithmetic: 21.6 us -> 0 us
    psum x3 -> x0, blocking collectives: 123 us -> none  [the longest x2 84.3 us: inner_rz(): return lax.psum(jnp.sum(first * second, axis=(1, 2, 3)), ('slab', 'sub'))]
    ppermute x14 -> x8, starting transfers between devices: 41.5 us -> 8.77 us  [exchange(): lax.ppermute(array, axes, path)]
    pallas_call x0 -> x4, Pallas kernels: none -> 23.3 us  [the longest x3 19.5 us: call(): pl.pallas_call(kernel, out_shape=[jax.ShapeDtypeStruct(shape, F32) for sh...]
    slice x30 -> x0, local copies, waits for them, and re-layouts: 15.4 us -> none  [the longest x6 6.48 us: forces_behind(): from_chord = from_behind(chord_forces[:, :, :, -1:], 'sub', 1)]
    all_to_all x0 -> x1, blocking collectives: none -> 13.3 us  [body(): lax.all_to_all(chunk.reshape(devices, 8, cols), axes, 0, 0)]
    reduce_sum x6 -> x0, other arithmetic: 9.34 us -> none  [the longest x2 5.36 us: inner_pq(): return lax.psum(jnp.sum(first * second, axis=(1, 2, 3)), ('slab', 'sub'))]
    unnamed x64 -> x14, local copies, waits for them, and re-layouts: 10.6 us -> 3.84 us
    ppermute x6 -> x0, local copies, waits for them, and re-layouts: 5.55 us -> none  [from_behind(): lax.ppermute(value, axis, [(source, source + steps) for source in range(i...]
  transfers between devices with their start and end apart: 14 -> 8, of which waited for: 6 -> 3; matrix products, arithmetic and copies ran while one was open for 11% -> 0% of each run, Pallas kernels for 0% -> 0%
where the time goes in v1:
time: 55 us; the launch traced here: 54.6 us
  Pallas kernels  23.3 us (42%)
  blocking collectives  13.3 us (24%)
  starting transfers between devices  8.77 us (16%)
  waiting for transfers between devices  4.72 us (9%)
  local copies, waits for them, and re-layouts  3.84 us (7%)
  between operations  0.66 us (1%)
    pallas_call x3, Pallas kernels, call(): pl.pallas_call(kernel, out_shape=[jax.ShapeDtypeStruct(shape, F32) for sh...  19.5 us
    all_to_all x1, blocking collectives, body(): lax.all_to_all(chunk.reshape(devices, 8, cols), axes, 0, 0)  13.3 us
    ppermute x8, starting transfers between devices, exchange(): lax.ppermute(array, axes, path)  8.77 us
    ppermute x8, waiting for transfers between devices, exchange(): lax.ppermute(array, axes, path)  4.72 us
    unnamed x14, local copies, waits for them, and re-layouts  3.84 us
    pallas_call x1, Pallas kernels, body(): pl.pallas_call(lambda *refs: last_kernel(dims, sizes, steps, *refs), grid...  3.8 us
  transfers between devices with their start and end apart: 8, of which 3 were waited for; matrix products, arithmetic and copies ran while one was open for 0% of the time, Pallas kernels for 0%

profile of v1, /device:TPU:0, one launch (start us, length us, event | category | flops | bytes accessed | tf_op | source)
XLA Modules:
  0.0 54.6 jit_solution(243505676230807614)
XLA Ops:
  0.6 0.0 copy-start
  0.6 1.0 %copy-done = bf16[32,6,8,128]{3,2,1,0:T(8,128)(2,1)S(1)} copy-done((bf16[32,6,8,128]{3,2,1,0:T(8,128)(2,1)S(1)}, bf16[32,6,8,128]{3,2,1,0:T(8,128)(2,1)}, u32[]{:S(2)}) %copy-start) | copy-done | bytes 393240
  1.6 0.0 copy-start.1
  1.6 0.7 %copy-done.1 = f32[6,8,128]{2,1,0:T(8,128)S(1)} copy-done((f32[6,8,128]{2,1,0:T(8,128)S(1)}, f32[6,8,128]{2,1,0:T(8,128)}, u32[]{:S(2)}) %copy-start.1) | copy-done | bytes 24600
  2.4 0.0 copy-start.2
  2.4 0.7 %copy-done.2 = f32[6,8,128]{2,1,0:T(8,128)S(1)} copy-done((f32[6,8,128]{2,1,0:T(8,128)S(1)}, f32[6,8,128]{2,1,0:T(8,128)}, u32[]{:S(2)}) %copy-start.2) | copy-done | bytes 24600
  3.1 0.0 copy-start.4
  3.1 0.7 %copy-done.4 = f32[8,128]{1,0:T(8,128)S(1)} copy-done((f32[8,128]{1,0:T(8,128)S(1)}, f32[8,128]{1,0:T(8,128)}, u32[]{:S(2)}) %copy-start.4) | copy-done | bytes 4120
  3.8 0.7 %copy-done.5 = f32[8,128]{1,0:T(8,128)S(1)} copy-done((f32[8,128]{1,0:T(8,128)S(1)}, f32[8,128]{1,0:T(8,128)}, u32[]{:S(2)}) %copy-start.5) | copy-done | bytes 4120
  4.5 2.5 %pack_rim.1 = (f32[200,128]{1,0:T(8,128)S(1)}, f32[200,128]{1,0:T(8,128)S(1)}, f32[56,128]{1,0:T(8,128)S(1)}, f32[56,128]{1,0:T(8,128)S(1)}) custom-call(bf16[1536,128]{1,0:T(8,128)(2,1)S(1)} %bitcast.5, f32[6,8,128]{2,1,0:T(8,128)S(1)} %copy-done.1, f32[6,8,128]{2,1,0:T(8,128)S(1)} %copy-done.2, f32[8,128]{1,0:T(8,128)S(1)} %copy-done.4, f32[8,128]{1,0:T(8,128)S(1)} %copy-done.5), custom_call_target="tpu_custom_call" | custom-call | tf_op jit(solution)/shard_map/pack_rim/pallas_call | solution.py:498
  7.0 3.0 %collective-permute-start = (f32[200,128]{1,0:T(8,128)S(1)}, f32[200,128]{1,0:T(8,128)S(1)}, u32[]{:S(2)}, u32[]{:S(2)}) collective-permute-start(f32[200,128]{1,0:T(8,128)S(1)} %get-tuple-element.21.refs_7_), channel_id=1, source_target_pairs={{0,4},{1,5},{2,6},{3,7},{4,0},{5,1},{6,2},{7,3},{8,12},{9,13},{10,... | collective-permute-start | bytes 307208 | tf_op jit(solution)/shard_map/ppermute | solution.py:485
  10.0 0.0 collective-permute-start.1
  10.0 0.5 collective-permute-start.2
  10.5 1.1 %collective-permute-start.3 = (f32[56,128]{1,0:T(8,128)S(1)}, f32[56,128]{1,0:T(8,128)S(1)}, u32[]{:S(2)}, u32[]{:S(2)}) collective-permute-start(f32[56,128]{1,0:T(8,128)S(1)} %get-tuple-element.24.refs_10_), channel_id=1, source_target_pairs={{0,3},{1,2},{2,1},{3,0},{4,7},{5,6},{6,5},{7,4},{8,11},{9,10},{10,... | collective-permute-start | bytes 86024 | tf_op jit(solution)/shard_map/ppermute | solution.py:485
  11.6 0.0 collective-permute-done.2.refs_13_
  11.6 2.3 %collective-permute-done.3.refs_14_ = f32[56,128]{1,0:T(8,128)S(1)} collective-permute-done((f32[56,128]{1,0:T(8,128)S(1)}, f32[56,128]{1,0:T(8,128)S(1)}, u32[]{:S(2)}, u32[]{:S(2)}) %collective-permute-start.3) | collective-permute-done | bytes 28704 | tf_op jit(solution)/shard_map/ppermute | solution.py:485
  13.9 0.4 collective-permute-done.refs_11_
  14.4 0.0 collective-permute-done.1.refs_12_
  14.4 0.0 copy-done.3
  14.4 0.0 copy-done.6
  14.4 11.2 %load_and_first.1 = (f32[1536,128]{1,0:T(8,128)S(1)}, f32[1536,128]{1,0:T(8,128)S(1)}, f32[1536,128]{1,0:T(8,128)S(1)}, f32[1536,128]{1,0:T(8,128)S(1)}, f32[49,...) custom-call(bf16[1536,128]{1,0:T(8,128)(2,1)S(1)} %bitcast.6, ...), custom_call_target="tpu_custom_call" | custom-call | tf_op jit(solution)/shard_map/load_and_first/pallas_call | solution.py:498
  25.6 2.5 %collective-permute-start.4 = (f32[72,128]{1,0:T(8,128)S(1)}, f32[72,128]{1,0:T(8,128)S(1)}, u32[]{:S(2)}, u32[]{:S(2)}) collective-permute-start(f32[72,128]{1,0:T(8,128)S(1)} %get-tuple-element.30.refs_5_), channel_id=1, source_target_pairs={{0,4},{1,5},{2,6},{3,7},{4,0},{5,1},{6,2},{7,3},{8,12},{9,13},{10,... | collective-permute-start | bytes 110600 | tf_op jit(solution)/shard_map/ppermute | solution.py:485
  28.1 0.0 collective-permute-start.5
  28.1 0.5 collective-permute-start.6
  28.6 1.1 %collective-permute-start.7 = (f32[24,128]{1,0:T(8,128)S(1)}, f32[24,128]{1,0:T(8,128)S(1)}, u32[]{:S(2)}, u32[]{:S(2)}) collective-permute-start(f32[24,128]{1,0:T(8,128)S(1)} %get-tuple-element.33.refs_8_), channel_id=1, source_target_pairs={{0,3},{1,2},{2,1},{3,0},{4,7},{5,6},{6,5},{7,4},{8,11},{9,10},{10,... | collective-permute-start | bytes 36872 | tf_op jit(solution)/shard_map/ppermute | solution.py:485
  29.7 0.0 collective-permute-done.6.refs_11_
  29.7 2.0 %collective-permute-done.7.refs_12_ = f32[24,128]{1,0:T(8,128)S(1)} collective-permute-done((f32[24,128]{1,0:T(8,128)S(1)}, f32[24,128]{1,0:T(8,128)S(1)}, u32[]{:S(2)}, u32[]{:S(2)}) %collective-permute-start.7) | collective-permute-done | bytes 12320 | tf_op jit(solution)/shard_map/ppermute | solution.py:485
  31.7 0.0 collective-permute-done.4.refs_9_
  31.7 0.0 collective-permute-done.5.refs_10_
  31.7 5.8 %second_and_sums.1 = (f32[1536,128]{1,0:T(8,128)S(1)}, f32[1536,128]{1,0:T(8,128)S(1)}, f32[1536,128]{1,0:T(8,128)S(1)}, f32[256,128]{1,0:T(8,128)S(1)}) custom-call(f32[1536,128]{1,0:T(8,128)S(1)} %get-tuple-element.25.refs_0_.refs_2_, f32[1536,128]{1,0:T(8,128)S(1)} %get-tuple-element.26.refs_1_.refs_3_, f32[1536,128]{1,0:T(8,128)S(1)} %get-tuple-element.27.refs_2_, ...), custom_call_target="tpu_custom_call" | custom-call | tf_op jit(solution)/shard_map/second_and_sums/pallas_call | solution.py:498
  37.5 13.3 %all_to_all.5 = f32[32,8,128]{2,1,0:T(8,128)S(1)} all-to-all(f32[32,8,128]{2,1,0:T(8,128)S(1)} %bitcast.8), channel_id=1, replica_groups=mesh['slab'=8,'sub'=4] {'slab','sub'}, dimensions={0} | all-to-all | bytes 262144 | tf_op jit(solution)/shard_map/all_to_all | solution.py:531
  50.8 3.8 %combine.1 = (f32[1536,128]{1,0:T(8,128)}, f32[1536,128]{1,0:T(8,128)}) custom-call(f32[256,128]{1,0:T(8,128)S(1)} %bitcast.7, f32[49,8,128]{2,1,0:T(8,128)S(1)} %get-tuple-element.29.refs_4_.refs_1_, f32[1536,128]{1,0:T(8,128)S(1)} %get-tuple-element.25.refs_0_.refs_2_, f32[1536,128]{1,0:T(8,128)S(1)} %get-tuple-element.26.refs_1_.refs_3_, ...), custom_call_target="tpu_custom_call" | custom-call | tf_op jit(solution)/shard_map/combine/pallas_call | solution.py:535
  (3 shorter events, 0.0 us)
Async XLA Ops:
  0.6 1.0 %copy-start = (bf16[32,6,8,128]{3,2,1,0:T(8,128)(2,1)S(1)}, bf16[32,6,8,128]{3,2,1,0:T(8,128)(2,1)}, u32[]{:S(2)}) copy-start(bf16[32,6,8,128]{3,2,1,0:T(8,128)(2,1)} %param.7) | copy-start | bytes 1179652
  1.6 0.7 %copy-start.1 = (f32[6,8,128]{2,1,0:T(8,128)S(1)}, f32[6,8,128]{2,1,0:T(8,128)}, u32[]{:S(2)}) copy-start(f32[6,8,128]{2,1,0:T(8,128)} %refs_1_.3) | copy-start | bytes 73732
  2.4 0.7 %copy-start.2 = (f32[6,8,128]{2,1,0:T(8,128)S(1)}, f32[6,8,128]{2,1,0:T(8,128)}, u32[]{:S(2)}) copy-start(f32[6,8,128]{2,1,0:T(8,128)} %refs_2_.3) | copy-start | bytes 73732
  3.1 0.7 %copy-start.4 = (f32[8,128]{1,0:T(8,128)S(1)}, f32[8,128]{1,0:T(8,128)}, u32[]{:S(2)}) copy-start(f32[8,128]{1,0:T(8,128)} %refs_3_.3) | copy-start | bytes 12292
  3.8 0.7 %copy-start.5 = (f32[8,128]{1,0:T(8,128)S(1)}, f32[8,128]{1,0:T(8,128)}, u32[]{:S(2)}) copy-start(f32[8,128]{1,0:T(8,128)} %refs_4_.3) | copy-start | bytes 12292
  4.5 9.9 %copy-start.3 = (f32[6,8,128]{2,1,0:T(8,128)S(1)}, f32[6,8,128]{2,1,0:T(8,128)}, u32[]{:S(2)}) copy-start(f32[6,8,128]{2,1,0:T(8,128)} %refs_5_.1) | copy-start | bytes 73732
  7.0 7.4 %collective-permute-start = (f32[200,128]{1,0:T(8,128)S(1)}, f32[200,128]{1,0:T(8,128)S(1)}, u32[]{:S(2)}, u32[]{:S(2)}) collective-permute-start(f32[200,128]{1,0:T(8,128)S(1)} %get-tuple-element.21.refs_7_), channel_id=1, source_target_pairs={{0,4},{1,5},{2,6},{3,7},{4,0},{5,1},{6,2},{7,3},{8,12},{9,13},{10,... | collective-permute-start | bytes 307208 | tf_op jit(solution)/shard_map/ppermute | solution.py:485
  10.0 4.3 %collective-permute-start.1 = (f32[200,128]{1,0:T(8,128)S(1)}, f32[200,128]{1,0:T(8,128)S(1)}, u32[]{:S(2)}, u32[]{:S(2)}) collective-permute-start(f32[200,128]{1,0:T(8,128)S(1)} %get-tuple-element.22.refs_8_), channel_id=1, source_target_pairs={{0,1},{1,0},{2,3},{3,2},{4,8},{5,9},{6,10},{7,11},{8,4},{9,5},{10,... | collective-permute-start | bytes 307208 | tf_op jit(solution)/shard_map/ppermute | solution.py:485
  10.0 4.3 %copy-start.6 = (s32[64]{0:T(128)S(1)}, s32[64]{0:T(128)}, u32[]{:S(2)}) copy-start(s32[64]{0:T(128)} %refs_6_.1) | copy-start | bytes 772
  10.0 1.6 %collective-permute-start.2 = (f32[56,128]{1,0:T(8,128)S(1)}, f32[56,128]{1,0:T(8,128)S(1)}, u32[]{:S(2)}, u32[]{:S(2)}) collective-permute-start(f32[56,128]{1,0:T(8,128)S(1)} %get-tuple-element.23.refs_9_), channel_id=1, source_target_pairs={{0,1},{1,0},{2,3},{3,2},{4,5},{5,4},{6,7},{7,6},{8,9},{9,8},{10,11... | collective-permute-start | bytes 86024 | tf_op jit(solution)/shard_map/ppermute | solution.py:485
  10.5 3.4 %collective-permute-start.3 = (f32[56,128]{1,0:T(8,128)S(1)}, f32[56,128]{1,0:T(8,128)S(1)}, u32[]{:S(2)}, u32[]{:S(2)}) collective-permute-start(f32[56,128]{1,0:T(8,128)S(1)} %get-tuple-element.24.refs_10_), channel_id=1, source_target_pairs={{0,3},{1,2},{2,1},{3,0},{4,7},{5,6},{6,5},{7,4},{8,11},{9,10},{10,... | collective-permute-start | bytes 86024 | tf_op jit(solution)/shard_map/ppermute | solution.py:485
  25.6 6.1 %collective-permute-start.4 = (f32[72,128]{1,0:T(8,128)S(1)}, f32[72,128]{1,0:T(8,128)S(1)}, u32[]{:S(2)}, u32[]{:S(2)}) collective-permute-start(f32[72,128]{1,0:T(8,128)S(1)} %get-tuple-element.30.refs_5_), channel_id=1, source_target_pairs={{0,4},{1,5},{2,6},{3,7},{4,0},{5,1},{6,2},{7,3},{8,12},{9,13},{10,... | collective-permute-start | bytes 110600 | tf_op jit(solution)/shard_map/ppermute | solution.py:485
  28.1 3.6 %collective-permute-start.5 = (f32[72,128]{1,0:T(8,128)S(1)}, f32[72,128]{1,0:T(8,128)S(1)}, u32[]{:S(2)}, u32[]{:S(2)}) collective-permute-start(f32[72,128]{1,0:T(8,128)S(1)} %get-tuple-element.31.refs_6_), channel_id=1, source_target_pairs={{0,1},{1,0},{2,3},{3,2},{4,8},{5,9},{6,10},{7,11},{8,4},{9,5},{10,... | collective-permute-start | bytes 110600 | tf_op jit(solution)/shard_map/ppermute | solution.py:485
  28.1 1.6 %collective-permute-start.6 = (f32[24,128]{1,0:T(8,128)S(1)}, f32[24,128]{1,0:T(8,128)S(1)}, u32[]{:S(2)}, u32[]{:S(2)}) collective-permute-start(f32[24,128]{1,0:T(8,128)S(1)} %get-tuple-element.32.refs_7_), channel_id=1, source_target_pairs={{0,1},{1,0},{2,3},{3,2},{4,5},{5,4},{6,7},{7,6},{8,9},{9,8},{10,11... | collective-permute-start | bytes 36872 | tf_op jit(solution)/shard_map/ppermute | solution.py:485
  28.6 3.1 %collective-permute-start.7 = (f32[24,128]{1,0:T(8,128)S(1)}, f32[24,128]{1,0:T(8,128)S(1)}, u32[]{:S(2)}, u32[]{:S(2)}) collective-permute-start(f32[24,128]{1,0:T(8,128)S(1)} %get-tuple-element.33.refs_8_), channel_id=1, source_target_pairs={{0,3},{1,2},{2,1},{3,0},{4,7},{5,6},{6,5},{7,4},{8,11},{9,10},{10,... | collective-permute-start | bytes 36872 | tf_op jit(solution)/shard_map/ppermute | solution.py:485

commit v2 on v1

--- a/solution.py
+++ b/solution.py
@@ -7,6 +7,7 @@
 
 F32 = jnp.float32
 VMEM_LIMIT = 24 * 1024 * 1024
+LINES = 4
 
 
 def matching(slabs, subs, along_slab, parity):
@@ -55,23 +56,66 @@
     return lax.rem(lax.axis_index("slab"), 2) == 0, lax.rem(lax.axis_index("sub"), 2) == 0
 
 
-def pack_kernel(dims, modes_ref, span_ref, chord_ref, span_geo_ref, chord_geo_ref,
-                row_even, row_odd, col_even, col_odd, field):
+def pack_kernel(dims, sizes, parts, modes_hbm, span_hbm, chord_hbm, span_geo_hbm, chord_geo_hbm, len_hbm,
+                field, live_ref, span_ref, chord_ref, span_geo_ref, chord_geo_ref, row_even, row_odd, col_even, col_odd,
+                raw, len_ref, sems):
     modes, dof, rows, cols = dims
     row, lane = tile_iota((rows, cols))
     slab_even, sub_even = parities()
     per = dof * rows
-
-    def body(m, carry):
-        start = pl.multiple_of(m * per, per)
-        block = modes_ref[pl.ds(start, per), :].astype(F32)
-        field[pl.ds(start, per), :] = block
+    share = modes // parts
+    fetches = [
+        pltpu.make_async_copy(modes_hbm.at[pl.ds(i * share * per, share * per), :],
+                              raw.at[pl.ds(i * share * per, share * per), :], sems.at[i])
+        for i in range(parts)
+    ]
+    small = ((span_hbm, span_ref), (chord_hbm, chord_ref), (span_geo_hbm, span_geo_ref), (chord_geo_hbm, chord_geo_ref),
+             (len_hbm, len_ref))
+    others = [pltpu.make_async_copy(src, dst, sems.at[parts + i]) for i, (src, dst) in enumerate(small)]
+    for copy in others + fetches:
+        copy.start()
+    for copy in others:
+        copy.wait()
+
+    stations = sizes[0] * rows
+    row_start = lax.axis_index("slab") * rows
+    col_start = lax.axis_index("sub") * cols
+
+    def length(index):
+        value = len_ref[jnp.clip(index, 0, stations - 1)]
+        return jnp.where((index >= 0) & (index < stations), value, 0)
+
+    lengths = [length(row_start + r) for r in range(-1, rows + 1)]
+    own = jnp.zeros((rows, cols), jnp.int32)
+    ahead = jnp.zeros((rows, cols), jnp.int32)
+    for r in range(rows):
+        own = jnp.where(row == r, lengths[r + 1], own)
+        ahead = jnp.where(row == r, lengths[r + 2], ahead)
+    column = col_start + lane
+    up_live = (column < lengths[0]) & (column < lengths[1])
+    left_live = (col_start < own) & (col_start > 0)
+    live = ((column < own) & (column < ahead), column + 1 < own, up_live, left_live)
+    for i, flags in enumerate(live):
+        live_ref[i] = flags.astype(F32)
+
+    packed = [jnp.zeros((rows, cols), F32) for k in range(dof)]
+    for m in range(modes):
+        if m % share == 0:
+            fetches[m // share].wait()
+        block = raw[m * per:(m + 1) * per, :].astype(F32)
+        field[m * per:(m + 1) * per, :] = block
         mine = (lane >> 1) == m
-        return tuple(
-            jnp.where(mine, roll(block[k * rows:(k + 1) * rows], 2 * m + 1, 1), carry[k]) for k in range(dof)
-        )
-
-    packed = lax.fori_loop(0, modes, body, tuple(jnp.zeros((rows, cols), F32) for k in range(dof)))
+        for k in range(dof):
+            packed[k] = jnp.where(mine, roll(block[k * rows:(k + 1) * rows], 2 * m + 1, 1), packed[k])
+        if m % 8 == 7:
+            for k in range(dof):
+                base = (m - 7) * per + k * rows
+                first = field[pl.ds(base, 8, stride=per), :]
+                last = field[pl.ds(base + rows - 1, 8, stride=per), :]
+                out = k * modes + m - 7
+                row_even[out:out + 8, :] = jnp.where(slab_even, last, first)
+                row_odd[out:out + 8, :] = jnp.where(slab_even, first, last)
+    field[modes * per:modes * per + rows, :] = jnp.zeros((rows, cols), F32)
     coef = jnp.zeros((rows, cols), F32)
     edge = jnp.zeros((rows, cols), F32)
     for k in range(dof + 1):
@@ -83,13 +127,6 @@
         behind = roll(packed[k], -1, 1)
         col_even[k * rows:(k + 1) * rows, :] = jnp.where(sub_even, packed[k], behind)
         col_odd[k * rows:(k + 1) * rows, :] = jnp.where(sub_even, behind, packed[k])
-        for block in range(modes // 8):
-            base = block * 8 * per + k * rows
-            first = field[pl.ds(base, 8, stride=per), :]
-            last = field[pl.ds(base + rows - 1, 8, stride=per), :]
-            out = k * modes + block * 8
-            row_even[out:out + 8, :] = jnp.where(slab_even, last, first)
-            row_odd[out:out + 8, :] = jnp.where(slab_even, first, last)
     row_even[dof * modes:dof * modes + rows, :] = coef
     row_odd[dof * modes:dof * modes + rows, :] = coef
     col_even[dof * rows:(dof + 1) * rows, :] = edge
@@ -141,34 +178,16 @@
     return [dot([entry(max(i, j), min(i, j)) for j in range(count)], vector) for i in range(count)]
 
 
-def first_kernel(dims, sizes, modes_ref, span_ref, chord_ref, span_geo_ref, chord_geo_ref, ground_ref, len_ref,
+def first_kernel(dims, modes_ref, live_ref, span_ref, chord_ref, span_geo_ref, chord_geo_ref, ground_ref,
                  row_even_out, row_odd_out, col_even_out, col_odd_out,
                  row_even_in, row_odd_in, col_even_in, col_odd_in,
                  load_ref, z_ref, q_ref, g_ref, coef_ref, row_even, row_odd, col_even, col_odd,
                  inv_ref, up_ref, down_ref, rim_ref, rim2_ref):
     modes, dof, rows, cols = dims
-    slabs, subs = sizes
     row, lane = tile_iota((rows, cols))
     slab_even, sub_even = parities()
     per = dof * rows
-    stations = slabs * rows
-    row_start = lax.axis_index("slab") * rows
-    col_start = lax.axis_index("sub") * cols
-    column = col_start + lane
-
-    def length(index):
-        value = len_ref[jnp.clip(index, 0, stations - 1)]
-        return jnp.where((index >= 0) & (index < stations), value, 0)
-
-    own = jnp.zeros((rows, cols), jnp.int32)
-    ahead = jnp.zeros((rows, cols), jnp.int32)
-    for r in range(rows):
-        own = jnp.where(row == r, length(row_start + r), own)
-        ahead = jnp.where(row == r, length(row_start + r + 1), ahead)
-    span_live = (column < own) & (column < ahead)
-    chord_live = column + 1 < own
-    up_live = (column < length(row_start - 1)) & (column < length(row_start))
-    left_live = (col_start < own) & (col_start > 0)
+    span_live, chord_live, up_live, left_live = (live_ref[i] > 0.0 for i in range(4))
 
     def row_weight(arrived, sent):
         total = None
@@ -190,15 +209,15 @@
     down_weight = jnp.where(slab_even, even_weight, odd_weight)
     tail = dof * modes
     up_coef = jnp.where(slab_even, row_odd_in[tail:tail + rows, :], row_even_in[tail:tail + rows, :])
-    up_ref[...] = jnp.where(up_live[0:1], up_weight * up_coef[dof:dof + 1], 0.0)
-    down_ref[...] = jnp.where(span_live[rows - 1:rows], down_weight * span_geo_ref[rows - 1:rows, :], 0.0)
+    up_ref[...] = jnp.where(live_ref[2, 0:1, :] > 0.0, up_weight * up_coef[dof:dof + 1], 0.0)
+    down_ref[...] = jnp.where(live_ref[0, rows - 1:rows, :] > 0.0, down_weight * span_geo_ref[rows - 1:rows, :], 0.0)
     even_col = col_weight(col_even_in, col_even_out)
     odd_col = col_weight(col_odd_in, col_odd_out)
     left_coef = jnp.where(sub_even, col_odd_in[per:per + rows, :], col_even_in[per:per + rows, :])
     left_weight = jnp.where(sub_even, odd_col, even_col) * left_coef[:, 2 * dof:2 * dof + 1]
     right_weight = jnp.where(sub_even, even_col, odd_col) * chord_geo_ref[:, cols - 1:cols]
     left_weight = jnp.where(left_live, left_weight, 0.0)
-    right_weight = jnp.where(chord_live[:, cols - 1:cols], right_weight, 0.0)
+    right_weight = jnp.where(live_ref[1, :, cols - 1:cols] > 0.0, right_weight, 0.0)
     lane_even = (lane & 1) == 0
     rim_weight = jnp.where(lane_even, left_weight, roll(right_weight, -1, 1))
 
@@ -240,13 +259,12 @@
         return [coef_ref[group * dof + k] for k in range(dof)]
 
     def body(m, carry):
-        start = pl.multiple_of(m * per, per)
-        block = modes_ref[pl.ds(start, per), :].astype(F32)
-        v = [block[k * rows:(k + 1) * rows] for k in range(dof)]
+        start = m * per
+        v = [modes_ref[pl.ds(start + k * rows, rows), :] for k in range(dof)]
         down = down_ref[pl.ds(m, 1), :]
         up = up_ref[pl.ds(m, 1), :]
         rim = roll(rim_weight, -2 * m, 1)
-        jumps = [roll(v[k], -1, 0) - v[k] for k in range(dof)]
+        jumps = [modes_ref[pl.ds(start + k * rows + 1, rows), :] - v[k] for k in range(dof)]
         span_w = jnp.where(last_row, down, dot(jumps, jumps) * span_geo_ref[...])
         jumps = [roll(v[k], -1, 1) - v[k] for k in range(dof)]
         chord_w = jnp.where(last_col, rim, dot(jumps, jumps) * chord_geo_ref[...])
@@ -269,12 +287,12 @@
         q = [axpy4([span[k], span_b[k], chord[k], chord_b[k]], near) for k in range(dof)]
         g = apply_inverse(entry, q)
         for k in range(dof):
-            at = pl.ds(pl.multiple_of(start + k * rows, rows), rows)
+            at = pl.ds(start + k * rows, rows)
             load_ref[at, :] = load[k]
             z_ref[at, :] = z[k]
             q_ref[at, :] = q[k]
             g_ref[at, :] = g[k]
-        at = pl.ds(pl.multiple_of(m * rows, rows), rows)
+        at = pl.ds(m * rows, rows)
         rim_ref[at, :] = jnp.where(last_row, fwd_s, bwd_s)
         rim2_ref[at, :] = dot(planes_of(4), g)
         mine = (lane >> 1) == m
@@ -282,7 +300,9 @@
         col_g = roll(dot(planes_of(5), g), 2 * m + 1, 1)
         return jnp.where(mine, col_z, carry[0]), jnp.where(mine, col_g, carry[1])
 
-    col_z, col_g = lax.fori_loop(0, modes, body, (zero, zero))
+    col_z, col_g = zero, zero
+    for m in range(modes):
+        col_z, col_g = body(m, (col_z, col_g))
     for which, packed in enumerate((col_z, col_g, roll(col_kappa, 1, 1))):
         behind = roll(packed, -1, 1)
         col_even[which * rows:(which + 1) * rows, :] = jnp.where(sub_even, packed, behind)
@@ -345,8 +365,8 @@
         return [coef_ref[group * dof + k] for k in range(dof)]
 
     def body(m, carry):
-        start = pl.multiple_of(m * per, per)
-        at = [pl.ds(pl.multiple_of(start + k * rows, rows), rows) for k in range(dof)]
+        start = m * per
+        at = [pl.ds(start + k * rows, rows) for k in range(dof)]
         row_ghost = jnp.where(last_row, down_ref[pl.ds(m, 1), :], up_ref[pl.ds(m, 1), :])
         col_ghost = roll(rim, -2 * m, 1)
         col_ghost2 = roll(rim2, -2 * m, 1)
@@ -364,23 +384,22 @@
         q2 = [axpy4([span[k], span_b[k], chord[k], chord_b[k]], near) for k in range(dof)]
         z = [z_ref[at[k], :] for k in range(dof)]
         load = [load_ref[at[k], :] for k in range(dof)]
+        miss = (corner_kappa * col_ghost, corner_kappa * row_ghost)
+        cross = miss[0] * jnp.where(last_row, near[0], near[1]) + miss[1] * jnp.where(last_col, near[2], near[3])
         for which, (left, right) in enumerate(((z, load), (z, q), (g, q), (g, q2))):
-            spot = pl.multiple_of((which * modes + m) * rows, rows)
-            sum_ref[pl.ds(spot, rows), :] = dot(left, right)
+            spot = (which * modes + m) * rows
+            total = dot(left, right)
+            sum_ref[pl.ds(spot, rows), :] = total + cross if which == 3 else total
         for k in range(dof):
             q_ref[at[k], :] = q[k]
             g_ref[at[k], :] = g[k]
             q2_ref[at[k], :] = q2[k]
-        corners = (
-            jnp.where(last_row, fwd_s, bwd_s),
-            jnp.where(last_col, fwd_c, bwd_c),
-            corner_kappa * col_ghost,
-            corner_kappa * row_ghost,
-        )
         mine = (lane >> 1) == m
-        return tuple(jnp.where(mine, roll(new, 2 * m + 1, 1), old) for new, old in zip(corners, carry))
-
-    corners = lax.fori_loop(0, modes, body, (zero,) * 4)
+        return tuple(jnp.where(mine, roll(new, 2 * m + 1, 1), old) for new, old in zip(miss, carry))
+
+    corners = (zero, zero)
+    for m in range(modes):
+        corners = body(m, corners)
     sums = []
     for block in range(4 * modes // 8):
         base = block * 8 * rows
@@ -393,20 +412,21 @@
         jnp.ones((8, cols), F32), sums, (((1,), (1,)), ((), ())),
         precision=lax.Precision.HIGHEST, preferred_element_type=F32,
     )
-    chunk = jnp.where(first_row, sums[0:1], zero)
+    chunk = jnp.where(row % LINES == 0, sums[0:1], zero)
     for which, corner in enumerate(corners):
-        line = jnp.where(lane < cols // 2, corner[0:1], roll(jnp.broadcast_to(corner[rows - 1:rows], (rows, cols)), cols // 2, 1))
-        chunk = jnp.where(row == which + 1, line, chunk)
+        far = roll(jnp.broadcast_to(corner[rows - 1:rows], (rows, cols)), cols // 2, 1)
+        line = jnp.where(lane < cols // 2, corner[0:1], far)
+        chunk = jnp.where(row % LINES == which + 1, line, chunk)
 
     def send(d, carry):
         chunk_ref[pl.ds(pl.multiple_of(d * rows, rows), rows), :] = chunk
         return carry
 
-    lax.fori_loop(0, devices, send, 0)
+    lax.fori_loop(0, devices * LINES // rows, send, 0, unroll=8)
 
 
 def last_kernel(dims, sizes, steps, part_ref, coef_ref, load_ref, z_ref, q_ref, g_ref, q2_ref,
-                adjoint_ref, residual_ref, a_ref, b_ref, fix_ref):
+                adjoint_hbm, residual_hbm, a_ref, b_ref, adjoint_ref, residual_ref, sems):
     modes, dof, rows, cols = dims
     slabs, subs = sizes
     devices = slabs * subs
@@ -414,65 +434,65 @@
     per = dof * rows
     half = cols // 2
 
-    @pl.when(pl.program_id(0) == 0)
-    def scalars():
-        def lines(which):
-            return part_ref[pl.ds(which, devices, stride=8), :]
-
-        own_row, own_col, miss_row, miss_col = (lines(i) for i in range(1, 5))
-        wide = lax.broadcasted_iota(jnp.int32, (devices, cols), 1)
-        swapped = roll(miss_row, half, 1)
-        met_row = jnp.where(wide >= half, roll(swapped, -subs, 0), roll(swapped, subs, 0))
-        met_col = jnp.where((wide & 1) == 0, roll(roll(miss_col, -1, 1), -1, 0), roll(roll(miss_col, 1, 1), 1, 0))
-        total = jnp.sum(lines(0), axis=0, keepdims=True)
-        missed = jnp.sum(own_row * met_row + own_col * met_col, axis=0, keepdims=True)
-        big_row, big_lane = tile_iota((4 * modes, cols))
-        spread = jnp.where(big_row == big_lane, total, 0.0)
-        spread = spread + jnp.where(((big_lane & (half - 1)) >> 1) == big_row - 3 * modes, missed, 0.0)
-        spread = lax.dot_general(
-            spread, jnp.ones((cols, cols), F32), (((1,), (0,)), ((), ())),
-            precision=lax.Precision.HIGHEST, preferred_element_type=F32,
-        )
-        m0, m1, m2, m3 = (spread[i * modes:(i + 1) * modes] for i in range(4))
-        step0 = m0 / (m0 - m1)
-        rest = 1.0 - step0
-        rz1 = rest * rest * m0 + 2.0 * rest * step0 * m1 + step0 * step0 * m2
-        c0 = rest + rz1 / m0
-        pq1 = c0 * c0 * (m0 - m1) + 2.0 * c0 * step0 * (m1 - m2) + step0 * step0 * (m2 - m3)
-        step1 = rz1 / pq1
-        a_ref[...] = step0 + step1 * c0
-        b_ref[...] = step1 * step0
-
-        here = lax.axis_index("slab") * subs + lax.axis_index("sub")
-
-        def line_of(device, which):
-            device = lax.rem(device + devices, devices)
-            line = part_ref[pl.ds(device * 8 + which, 1), :]
-            return jnp.broadcast_to(line, (rows, cols))
-
-        fix_ref[0:rows, :] = jnp.where(row == rows - 1, line_of(here + subs, 3), roll(line_of(here - subs, 3), half, 1))
-        fix = jnp.where((lane & 1) == 0, roll(line_of(here + 1, 4), -1, 1), roll(line_of(here - 1, 4), 1, 1))
-        fix_ref[rows:2 * rows, :] = jnp.where(row == rows - 1, roll(fix, half, 1), fix)
-
+    def lines(which):
+        return part_ref[pl.ds(which, devices, stride=LINES), :]
+
+    miss_row, miss_col = lines(1), lines(2)
+    wide = lax.broadcasted_iota(jnp.int32, (devices, cols), 1)
+    swapped = roll(miss_row, half, 1)
+    met_row = jnp.where(wide >= half, roll(swapped, -subs, 0), roll(swapped, subs, 0))
+    met_col = jnp.where((wide & 1) == 0, roll(roll(miss_col, -1, 1), -1, 0), roll(roll(miss_col, 1, 1), 1, 0))
+    total = jnp.sum(lines(0), axis=0, keepdims=True)
+    missed = jnp.sum(miss_row * met_row + miss_col * met_col, axis=0, keepdims=True)
+    big_row, big_lane = tile_iota((4 * modes, cols))
+    spread = jnp.where(big_row == big_lane, total, 0.0)
+    spread = spread + jnp.where(((big_lane & (half - 1)) >> 1) == big_row - 3 * modes, missed, 0.0)
+    spread = lax.dot_general(
+        spread, jnp.ones((cols, cols), F32), (((1,), (0,)), ((), ())),
+        precision=lax.Precision.HIGHEST, preferred_element_type=F32,
+    )
+    m0, m1, m2, m3 = (spread[i * modes:(i + 1) * modes] for i in range(4))
+    step0 = m0 / (m0 - m1)
+    rest = 1.0 - step0
+    rz1 = rest * rest * m0 + 2.0 * rest * step0 * m1 + step0 * step0 * m2
+    c0 = rest + rz1 / m0
+    pq1 = c0 * c0 * (m0 - m1) + 2.0 * c0 * step0 * (m1 - m2) + step0 * step0 * (m2 - m3)
+    step1 = rz1 / pq1
+    a_ref[...] = step0 + step1 * c0
+    b_ref[...] = step1 * step0
+
+    here = lax.axis_index("slab") * subs + lax.axis_index("sub")
+
+    def line_of(device, which):
+        device = lax.rem(device + devices, devices)
+        return jnp.broadcast_to(part_ref[pl.ds(device * LINES + which, 1), :], (rows, cols))
+
+    row_fixes = jnp.where(row == rows - 1, line_of(here + subs, 1), roll(line_of(here - subs, 1), half, 1))
+    col_fixes = jnp.where((lane & 1) == 0, roll(line_of(here + 1, 2), -1, 1), roll(line_of(here - 1, 2), 1, 1))
+    col_fixes = jnp.where(row == rows - 1, roll(col_fixes, half, 1), col_fixes)
     corner = ((row == 0) | (row == rows - 1)) & ((lane == 0) | (lane == cols - 1))
     count = modes // steps
-
-    def body(i, carry):
-        m = pl.program_id(0) * count + i
-        a = a_ref[pl.ds(m, 1), :]
-        b = b_ref[pl.ds(m, 1), :]
-        row_fix = b * jnp.where(corner, roll(fix_ref[0:rows, :], cols - 1 - 2 * m, 1), 0.0)
-        col_fix = b * jnp.where(corner, roll(fix_ref[rows:2 * rows, :], cols - 1 - 2 * m, 1), 0.0)
-        for k in range(dof):
-            at = pl.ds(pl.multiple_of(i * per + k * rows, rows), rows)
+    copies = []
+    for m in range(modes):
+        a = a_ref[m:m + 1, :]
+        b = b_ref[m:m + 1, :]
+        row_fix = b * jnp.where(corner, roll(row_fixes, -1 - 2 * m, 1), 0.0)
+        col_fix = b * jnp.where(corner, roll(col_fixes, -1 - 2 * m, 1), 0.0)
+        for k in range(dof):
+            at = pl.ds(m * per + k * rows, rows)
             adjoint_ref[at, :] = a * z_ref[at, :] + b * g_ref[at, :]
             residual_ref[at, :] = (
                 ((1.0 - a) * load_ref[at, :] + (a - b) * q_ref[at, :])
                 + (b * q2_ref[at, :] + (coef_ref[4 * dof + k] * row_fix + coef_ref[5 * dof + k] * col_fix))
             )
-        return carry
-
-    lax.fori_loop(0, count, body, 0)
+        if (m + 1) % count == 0:
+            at = pl.ds((m + 1 - count) * per, count * per)
+            for src, dst in ((adjoint_ref, adjoint_hbm), (residual_ref, residual_hbm)):
+                copy = pltpu.make_async_copy(src.at[at, :], dst.at[at, :], sems.at[len(copies)])
+                copy.start()
+                copies.append(copy)
+    for copy in copies:
+        copy.wait()
 
 
 def body_of(sizes):
@@ -485,63 +505,57 @@
         return [lax.ppermute(array, axes, path) for array, path in zip(arrays, paths)]
 
     vmem = pl.BlockSpec(memory_space=pltpu.VMEM)
-    smem = pl.BlockSpec(memory_space=pltpu.SMEM)
-    params = pltpu.CompilerParams(vmem_limit_bytes=VMEM_LIMIT)
+    hbm = pl.BlockSpec(memory_space=pltpu.HBM)
 
     def body(mode_shapes, span_stiff, chord_stiff, span_geo, chord_geo, ground, chord_len):
         modes, dof, rows, cols = mode_shapes.shape
         dims = mode_shapes.shape
         count = modes * dof * rows
-        field = mode_shapes.reshape(count, cols)
-
-        def call(kernel, name, inputs, specs, outs, scratch):
+
+        def call(kernel, name, inputs, in_specs, outs, scratch, out_spec=vmem):
             return pl.pallas_call(
                 kernel,
                 out_shape=[jax.ShapeDtypeStruct(shape, F32) for shape in outs],
-                in_specs=specs,
-                out_specs=[vmem] * len(outs),
-                scratch_shapes=[pltpu.VMEM(shape, F32) for shape in scratch],
-                compiler_params=params,
+                in_specs=in_specs,
+                out_specs=[out_spec] * len(outs),
+                scratch_shapes=[pltpu.VMEM(s, F32) if isinstance(s, tuple) else s for s in scratch],
+                compiler_params=pltpu.CompilerParams(vmem_limit_bytes=VMEM_LIMIT),
                 name=name,
             )(*inputs)
 
+        plane, planes, full = (rows, cols), (dof, rows, cols), (count, cols)
         row_shape, col_shape = (modes * dof + rows, cols), ((dof + 1) * rows, cols)
-        rims = call(
-            lambda *refs: pack_kernel(dims, *refs), "pack_rim",
-            (field, span_stiff, chord_stiff, span_geo, chord_geo), [vmem] * 5,
-            [row_shape, row_shape, col_shape, col_shape], [(count, cols)],
+        parts = 4
+        inputs = (mode_shapes.reshape(count, cols), span_stiff, chord_stiff, span_geo, chord_geo, chord_len)
+        field, *coefs, row_even, row_odd, col_even, col_odd = call(
+            lambda *refs: pack_kernel(dims, sizes, parts, *refs), "pack_rim",
+            [pltpu.with_memory_space_constraint(x, pltpu.HBM) for x in inputs], [hbm] * 6,
+            [(count + rows, cols), (4, rows, cols), planes, planes, plane, plane, row_shape, row_shape, col_shape, col_shape],
+            [pltpu.VMEM(full, mode_shapes.dtype), pltpu.SMEM(chord_len.shape, jnp.int32), pltpu.SemaphoreType.DMA((parts + 5,))],
         )
+        rims = [row_even, row_odd, col_even, col_odd]
         met = exchange(rims)
-        full = (count, cols)
         row_shape, col_shape = (2 * modes + rows, cols), (3 * rows, cols)
         load, z, qp, gp, coef, *rims2 = call(
-            lambda *refs: first_kernel(dims, sizes, *refs), "load_and_first",
-            (field, span_stiff, chord_stiff, span_geo, chord_geo, ground, chord_len, *rims, *met),
-            [vmem] * 6 + [smem] + [vmem] * 8,
-            [full] * 4 + [(8 * dof + 1, rows, cols)] + [row_shape, row_shape, col_shape, col_shape],
+            lambda *refs: first_kernel(dims, *refs), "load_and_first",
+            (field, *coefs, ground, *rims, *met), [vmem] * 15,
+            [full] * 4 + [(8 * dof + 1, rows, cols), row_shape, row_shape, col_shape, col_shape],
             [(dof * (dof + 1) // 2, rows, cols), (modes, cols), (modes, cols), (modes * rows, cols), (modes * rows, cols)],
         )
         met2 = exchange(rims2)
         q, g, q2, chunk = call(
             lambda *refs: second_kernel(dims, devices, *refs), "second_and_sums",
             (load, z, qp, gp, coef, *rims2, *met2), [vmem] * 13,
-            [full] * 3 + [(devices * 8, cols)],
+            [full] * 3 + [(devices * LINES, cols)],
             [(modes, cols)] * 4 + [(4 * modes * rows, cols)],
         )
-        parts = lax.all_to_all(chunk.reshape(devices, 8, cols), axes, 0, 0).reshape(devices * 8, cols)
+        shares = lax.all_to_all(chunk.reshape(devices, LINES, cols), axes, 0, 0).reshape(devices * LINES, cols)
         steps = 4
-        cut = pl.BlockSpec((count // steps, cols), lambda i: (i, 0))
-        whole = lambda shape: pl.BlockSpec(shape, lambda i: (0,) * len(shape))
-        adjoint, residual = pl.pallas_call(
-            lambda *refs: last_kernel(dims, sizes, steps, *refs),
-            grid=(steps,),
-            out_shape=[jax.ShapeDtypeStruct(full, F32)] * 2,
-            in_specs=[whole(parts.shape), whole(coef.shape)] + [cut] * 5,
-            out_specs=[cut] * 2,
-            scratch_shapes=[pltpu.VMEM((modes, cols), F32), pltpu.VMEM((modes, cols), F32), pltpu.VMEM((2 * rows, cols), F32)],
-            compiler_params=params,
-            name="combine",
-        )(parts, coef, load, z, q, g, q2)
+        adjoint, residual = call(
+            lambda *refs: last_kernel(dims, sizes, steps, *refs), "combine",
+            (shares, coef, load, z, q, g, q2), [vmem] * 7, [full] * 2,
+            [(modes, cols), (modes, cols), full, full, pltpu.SemaphoreType.DMA((2 * steps,))], hbm,
+        )
         return adjoint.reshape(dims), residual.reshape(dims)
 
     return body

time: 55 us -> 33.5 us (0.61)
  Pallas kernels: 23.3 us -> 6.6 us
  local copies, waits for them, and re-layouts: 3.84 us -> 0.01 us
  blocking collectives: 13.3 us -> 12.5 us
    pallas_call x3 -> x4, Pallas kernels: 19.5 us -> 6.6 us  [call(): pl.pallas_call(kernel, out_shape=[jax.ShapeDtypeStruct(shape, F32) for sh...]
    unnamed x14 -> x2, local copies, waits for them, and re-layouts: 3.84 us -> 0.01 us
    pallas_call x1 -> x0, Pallas kernels: 3.8 us -> none  [body(): pl.pallas_call(lambda *refs: last_kernel(dims, sizes, steps, *refs), grid...]
    all_to_all x1, blocking collectives: 13.3 us -> 12.5 us  [body(): lax.all_to_all(chunk.reshape(devices, LINES, cols), axes, 0, 0)]
where the time goes in v2:
time: 33.5 us; the launch traced here: 33.3 us
  blocking collectives  12.5 us (37%)
  starting transfers between devices  8.76 us (26%)
  Pallas kernels  6.6 us (20%)
  waiting for transfers between devices  4.72 us (14%)
  between operations  0.66 us (2%)
    all_to_all x1, blocking collectives, body(): lax.all_to_all(chunk.reshape(devices, LINES, cols), axes, 0, 0)  12.5 us
    ppermute x8, starting transfers between devices, exchange(): lax.ppermute(array, axes, path)  8.76 us
    pallas_call x4, Pallas kernels, call(): pl.pallas_call(kernel, out_shape=[jax.ShapeDtypeStruct(shape, F32) for sh...  6.6 us
    ppermute x8, waiting for transfers between devices, exchange(): lax.ppermute(array, axes, path)  4.72 us
  transfers between devices with their start and end apart: 8, of which 3 were waited for; matrix products, arithmetic and copies ran while one was open for 0% of the time, Pallas kernels for 0%

profile of v2, /device:TPU:0, one launch (start us, length us, event | category | flops | bytes accessed | tf_op | source)
XLA Modules:
  0.0 33.3 jit_solution(10006717340695530452)
XLA Ops:
  0.6 0.0 copy-start
  0.6 1.5 %pack_rim.1 = (f32[1544,128]{1,0:T(8,128)S(1)}, f32[4,8,128]{2,1,0:T(8,128)S(1)}, f32[6,8,128]{2,1,0:T(8,128)S(1)}, f32[6,8,128]{2,1,0:T(8,128)S(1)}, f32[8,128]...) custom-call(bf16[1536,128]{1,0:T(8,128)(2,1)} %bitcast.7, ...), custom_call_target="tpu_custom_call" | custom-call | tf_op jit(solution)/shard_map/pack_rim/pallas_call | solution.py:516
  2.2 3.0 %collective-permute-start = (f32[200,128]{1,0:T(8,128)S(1)}, f32[200,128]{1,0:T(8,128)S(1)}, u32[]{:S(2)}, u32[]{:S(2)}) collective-permute-start(f32[200,128]{1,0:T(8,128)S(1)} %get-tuple-element.33.refs_7_), channel_id=1, source_target_pairs={{0,4},{1,5},{2,6},{3,7},{4,0},{5,1},{6,2},{7,3},{8,12},{9,13},{10,... | collective-permute-start | bytes 307208 | tf_op jit(solution)/shard_map/ppermute | solution.py:505
  5.2 0.0 collective-permute-start.1
  5.2 0.5 %collective-permute-start.2 = (f32[56,128]{1,0:T(8,128)S(1)}, f32[56,128]{1,0:T(8,128)S(1)}, u32[]{:S(2)}, u32[]{:S(2)}) collective-permute-start(f32[56,128]{1,0:T(8,128)S(1)} %get-tuple-element.35.refs_9_), channel_id=1, source_target_pairs={{0,1},{1,0},{2,3},{3,2},{4,5},{5,4},{6,7},{7,6},{8,9},{9,8},{10,11... | collective-permute-start | bytes 86024 | tf_op jit(solution)/shard_map/ppermute | solution.py:505
  5.7 1.1 %collective-permute-start.3 = (f32[56,128]{1,0:T(8,128)S(1)}, f32[56,128]{1,0:T(8,128)S(1)}, u32[]{:S(2)}, u32[]{:S(2)}) collective-permute-start(f32[56,128]{1,0:T(8,128)S(1)} %get-tuple-element.36.refs_10_), channel_id=1, source_target_pairs={{0,3},{1,2},{2,1},{3,0},{4,7},{5,6},{6,5},{7,4},{8,11},{9,10},{10,... | collective-permute-start | bytes 86024 | tf_op jit(solution)/shard_map/ppermute | solution.py:505
  6.8 0.0 collective-permute-done.2.refs_13_
  6.8 2.3 %collective-permute-done.3.refs_14_ = f32[56,128]{1,0:T(8,128)S(1)} collective-permute-done((f32[56,128]{1,0:T(8,128)S(1)}, f32[56,128]{1,0:T(8,128)S(1)}, u32[]{:S(2)}, u32[]{:S(2)}) %collective-permute-start.3) | collective-permute-done | bytes 28704 | tf_op jit(solution)/shard_map/ppermute | solution.py:505
  9.1 0.4 %collective-permute-done.refs_11_ = f32[200,128]{1,0:T(8,128)S(1)} collective-permute-done((f32[200,128]{1,0:T(8,128)S(1)}, f32[200,128]{1,0:T(8,128)S(1)}, u32[]{:S(2)}, u32[]{:S(2)}) %collective-permute-start) | collective-permute-done | bytes 102432 | tf_op jit(solution)/shard_map/ppermute | solution.py:505
  9.5 0.0 collective-permute-done.1.refs_12_
  9.5 0.0 copy-done
  9.5 1.9 %load_and_first.1 = (f32[1536,128]{1,0:T(8,128)S(1)}, f32[1536,128]{1,0:T(8,128)S(1)}, f32[1536,128]{1,0:T(8,128)S(1)}, f32[1536,128]{1,0:T(8,128)S(1)}, f32[49,...) custom-call(f32[1544,128]{1,0:T(8,128)S(1)} %get-tuple-element.27.re, ...), custom_call_target="tpu_custom_call" | custom-call | tf_op jit(solution)/shard_map/load_and_first/pallas_call | solution.py:516
  11.5 2.5 %collective-permute-start.4 = (f32[72,128]{1,0:T(8,128)S(1)}, f32[72,128]{1,0:T(8,128)S(1)}, u32[]{:S(2)}, u32[]{:S(2)}) collective-permute-start(f32[72,128]{1,0:T(8,128)S(1)} %get-tuple-element.42.refs_5_), channel_id=1, source_target_pairs={{0,4},{1,5},{2,6},{3,7},{4,0},{5,1},{6,2},{7,3},{8,12},{9,13},{10,... | collective-permute-start | bytes 110600 | tf_op jit(solution)/shard_map/ppermute | solution.py:505
  14.0 0.0 collective-permute-start.5
  14.0 0.5 %collective-permute-start.6 = (f32[24,128]{1,0:T(8,128)S(1)}, f32[24,128]{1,0:T(8,128)S(1)}, u32[]{:S(2)}, u32[]{:S(2)}) collective-permute-start(f32[24,128]{1,0:T(8,128)S(1)} %get-tuple-element.44.refs_7_), channel_id=1, source_target_pairs={{0,1},{1,0},{2,3},{3,2},{4,5},{5,4},{6,7},{7,6},{8,9},{9,8},{10,11... | collective-permute-start | bytes 36872 | tf_op jit(solution)/shard_map/ppermute | solution.py:505
  14.5 1.1 %collective-permute-start.7 = (f32[24,128]{1,0:T(8,128)S(1)}, f32[24,128]{1,0:T(8,128)S(1)}, u32[]{:S(2)}, u32[]{:S(2)}) collective-permute-start(f32[24,128]{1,0:T(8,128)S(1)} %get-tuple-element.45.refs_8_), channel_id=1, source_target_pairs={{0,3},{1,2},{2,1},{3,0},{4,7},{5,6},{6,5},{7,4},{8,11},{9,10},{10,... | collective-permute-start | bytes 36872 | tf_op jit(solution)/shard_map/ppermute | solution.py:505
  15.6 0.0 collective-permute-done.6.refs_11_
  15.6 2.0 %collective-permute-done.7.refs_12_ = f32[24,128]{1,0:T(8,128)S(1)} collective-permute-done((f32[24,128]{1,0:T(8,128)S(1)}, f32[24,128]{1,0:T(8,128)S(1)}, u32[]{:S(2)}, u32[]{:S(2)}) %collective-permute-start.7) | collective-permute-done | bytes 12320 | tf_op jit(solution)/shard_map/ppermute | solution.py:505
  17.6 0.0 collective-permute-done.4.refs_9_
  17.6 0.0 collective-permute-done.5.refs_10_
  17.6 1.4 %second_and_sums.1 = (f32[1536,128]{1,0:T(8,128)S(1)}, f32[1536,128]{1,0:T(8,128)S(1)}, f32[1536,128]{1,0:T(8,128)S(1)}, f32[128,128]{1,0:T(8,128)S(1)}) custom-call(f32[1536,128]{1,0:T(8,128)S(1)} %get-tuple-element.37.refs_0_.refs_2_, f32[1536,128]{1,0:T(8,128)S(1)} %get-tuple-element.38.refs_1_.refs_3_, f32[1536,128]{1,0:T(8,128)S(1)} %get-tuple-element.39.refs_2_, ...), custom_call_target="tpu_custom_call" | custom-call | tf_op jit(solution)/shard_map/second_and_sums/pallas_call | solution.py:516
  19.0 12.5 %all_to_all.5 = f32[32,4,128]{2,1,0:T(4,128)S(1)} all-to-all(f32[32,4,128]{2,1,0:T(4,128)S(1)} %bitcast.6), channel_id=1, replica_groups=mesh['slab'=8,'sub'=4] {'slab','sub'}, dimensions={0} | all-to-all | bytes 131072 | tf_op jit(solution)/shard_map/all_to_all | solution.py:552
  31.5 1.8 %combine.1 = (f32[1536,128]{1,0:T(8,128)}, f32[1536,128]{1,0:T(8,128)}) custom-call(f32[128,128]{1,0:T(8,128)S(1)} %bitcast.5, f32[49,8,128]{2,1,0:T(8,128)S(1)} %get-tuple-element.41.refs_4_.refs_1_, f32[1536,128]{1,0:T(8,128)S(1)} %get-tuple-element.37.refs_0_.refs_2_, f32[1536,128]{1,0:T(8,128)S(1)} %get-tuple-element.38.refs_1_.refs_3_, ...), custom_call_target="tpu_custom_call" | custom-call | tf_op jit(solution)/shard_map/combine/pallas_call | solution.py:516
Async XLA Ops:
  0.6 8.9 %copy-start = (f32[6,8,128]{2,1,0:T(8,128)S(1)}, f32[6,8,128]{2,1,0:T(8,128)}, u32[]{:S(2)}) copy-start(f32[6,8,128]{2,1,0:T(8,128)} %refs_6_.1) | copy-start | bytes 73732
  2.2 7.4 %collective-permute-start = (f32[200,128]{1,0:T(8,128)S(1)}, f32[200,128]{1,0:T(8,128)S(1)}, u32[]{:S(2)}, u32[]{:S(2)}) collective-permute-start(f32[200,128]{1,0:T(8,128)S(1)} %get-tuple-element.33.refs_7_), channel_id=1, source_target_pairs={{0,4},{1,5},{2,6},{3,7},{4,0},{5,1},{6,2},{7,3},{8,12},{9,13},{10,... | collective-permute-start | bytes 307208 | tf_op jit(solution)/shard_map/ppermute | solution.py:505
  5.2 4.3 %collective-permute-start.1 = (f32[200,128]{1,0:T(8,128)S(1)}, f32[200,128]{1,0:T(8,128)S(1)}, u32[]{:S(2)}, u32[]{:S(2)}) collective-permute-start(f32[200,128]{1,0:T(8,128)S(1)} %get-tuple-element.34.refs_8_), channel_id=1, source_target_pairs={{0,1},{1,0},{2,3},{3,2},{4,8},{5,9},{6,10},{7,11},{8,4},{9,5},{10,... | collective-permute-start | bytes 307208 | tf_op jit(solution)/shard_map/ppermute | solution.py:505
  5.2 1.6 %collective-permute-start.2 = (f32[56,128]{1,0:T(8,128)S(1)}, f32[56,128]{1,0:T(8,128)S(1)}, u32[]{:S(2)}, u32[]{:S(2)}) collective-permute-start(f32[56,128]{1,0:T(8,128)S(1)} %get-tuple-element.35.refs_9_), channel_id=1, source_target_pairs={{0,1},{1,0},{2,3},{3,2},{4,5},{5,4},{6,7},{7,6},{8,9},{9,8},{10,11... | collective-permute-start | bytes 86024 | tf_op jit(solution)/shard_map/ppermute | solution.py:505
  5.7 3.4 %collective-permute-start.3 = (f32[56,128]{1,0:T(8,128)S(1)}, f32[56,128]{1,0:T(8,128)S(1)}, u32[]{:S(2)}, u32[]{:S(2)}) collective-permute-start(f32[56,128]{1,0:T(8,128)S(1)} %get-tuple-element.36.refs_10_), channel_id=1, source_target_pairs={{0,3},{1,2},{2,1},{3,0},{4,7},{5,6},{6,5},{7,4},{8,11},{9,10},{10,... | collective-permute-start | bytes 86024 | tf_op jit(solution)/shard_map/ppermute | solution.py:505
  11.5 6.1 %collective-permute-start.4 = (f32[72,128]{1,0:T(8,128)S(1)}, f32[72,128]{1,0:T(8,128)S(1)}, u32[]{:S(2)}, u32[]{:S(2)}) collective-permute-start(f32[72,128]{1,0:T(8,128)S(1)} %get-tuple-element.42.refs_5_), channel_id=1, source_target_pairs={{0,4},{1,5},{2,6},{3,7},{4,0},{5,1},{6,2},{7,3},{8,12},{9,13},{10,... | collective-permute-start | bytes 110600 | tf_op jit(solution)/shard_map/ppermute | solution.py:505
  14.0 3.6 %collective-permute-start.5 = (f32[72,128]{1,0:T(8,128)S(1)}, f32[72,128]{1,0:T(8,128)S(1)}, u32[]{:S(2)}, u32[]{:S(2)}) collective-permute-start(f32[72,128]{1,0:T(8,128)S(1)} %get-tuple-element.43.refs_6_), channel_id=1, source_target_pairs={{0,1},{1,0},{2,3},{3,2},{4,8},{5,9},{6,10},{7,11},{8,4},{9,5},{10,... | collective-permute-start | bytes 110600 | tf_op jit(solution)/shard_map/ppermute | solution.py:505
  14.0 1.6 %collective-permute-start.6 = (f32[24,128]{1,0:T(8,128)S(1)}, f32[24,128]{1,0:T(8,128)S(1)}, u32[]{:S(2)}, u32[]{:S(2)}) collective-permute-start(f32[24,128]{1,0:T(8,128)S(1)} %get-tuple-element.44.refs_7_), channel_id=1, source_target_pairs={{0,1},{1,0},{2,3},{3,2},{4,5},{5,4},{6,7},{7,6},{8,9},{9,8},{10,11... | collective-permute-start | bytes 36872 | tf_op jit(solution)/shard_map/ppermute | solution.py:505
  14.5 3.1 %collective-permute-start.7 = (f32[24,128]{1,0:T(8,128)S(1)}, f32[24,128]{1,0:T(8,128)S(1)}, u32[]{:S(2)}, u32[]{:S(2)}) collective-permute-start(f32[24,128]{1,0:T(8,128)S(1)} %get-tuple-element.45.refs_8_), channel_id=1, source_target_pairs={{0,3},{1,2},{2,1},{3,0},{4,7},{5,6},{6,5},{7,4},{8,11},{9,10},{10,... | collective-permute-start | bytes 36872 | tf_op jit(solution)/shard_map/ppermute | solution.py:505

commit v3 on v2

--- a/solution.py
+++ b/solution.py
@@ -133,44 +133,54 @@
     col_odd[dof * rows:(dof + 1) * rows, :] = edge
 
 
-def factor_blocks(blocks):
+def invert_blocks(blocks):
     count = len(blocks)
+    scaled = [[None] * count for i in range(count)]
     factor = [[None] * count for i in range(count)]
     inverse = [None] * count
     for j in range(count):
         running = blocks[j][j]
         for k in range(j):
-            running = running - factor[j][k] * factor[j][k]
-        diag_root = jnp.sqrt(running)
-        factor[j][j] = diag_root
-        inverse[j] = 1.0 / diag_root
+            running = running - scaled[j][k] * factor[j][k]
+        inverse[j] = 1.0 / running
         for i in range(j + 1, count):
             running = blocks[i][j]
             for k in range(j):
-                running = running - factor[i][k] * factor[j][k]
+                running = running - scaled[i][k] * factor[j][k]
+            scaled[i][j] = running
             factor[i][j] = running * inverse[j]
-    return (factor, inverse)
-
-
-def invert_blocks(blocks):
-    count = len(blocks)
-    factor, inverse = factor_blocks(blocks)
     lower = [[None] * count for i in range(count)]
     for j in range(count):
-        lower[j][j] = inverse[j]
         for i in range(j + 1, count):
-            running = factor[i][j] * lower[j][j]
+            running = factor[i][j]
             for k in range(j + 1, i):
                 running = running + factor[i][k] * lower[k][j]
-            lower[i][j] = -(running * inverse[i])
+            lower[i][j] = -running
     result = [[None] * count for i in range(count)]
     for i in range(count):
         for j in range(i + 1):
-            running = lower[i][i] * lower[i][j]
+            running = inverse[i] if i == j else inverse[i] * lower[i][j]
             for k in range(i + 1, count):
-                running = running + lower[k][i] * lower[k][j]
+                running = running + (lower[k][i] * inverse[k]) * lower[k][j]
             result[i][j] = running
     return result
+
+
+def times_ones(value, transposed):
+    high = value.astype(jnp.bfloat16)
+    rest = value - high.astype(F32)
+    middle = rest.astype(jnp.bfloat16)
+    low = (rest - middle.astype(F32)).astype(jnp.bfloat16)
+    pieces = jnp.concatenate([high, middle, low], axis=1)
+    if transposed:
+        ones = jnp.ones((8, pieces.shape[1]), jnp.bfloat16)
+        return lax.dot_general(ones, pieces, (((1,), (1,)), ((), ())), preferred_element_type=F32)
+    ones = jnp.ones((pieces.shape[1], value.shape[1]), jnp.bfloat16)
+    return lax.dot_general(pieces, ones, (((1,), (0,)), ((), ())), preferred_element_type=F32)
+
+
+def inverse_place(dof, i, j):
+    return 8 * dof + 1 + i * (i + 1) // 2 + j
 
 
 def apply_inverse(entry, vector):
@@ -178,11 +188,40 @@
     return [dot([entry(max(i, j), min(i, j)) for j in range(count)], vector) for i in range(count)]
 
 
-def first_kernel(dims, modes_ref, live_ref, span_ref, chord_ref, span_geo_ref, chord_geo_ref, ground_ref,
+def inner_kernel(dims, modes_ref, live_ref, span_ref, chord_ref, span_geo_ref, chord_geo_ref, load_ref):
+    modes, dof, rows, cols = dims
+    row, lane = tile_iota((rows, cols))
+    per = dof * rows
+    first_row, last_row = row == 0, row == rows - 1
+    first_col, last_col = lane == 0, lane == cols - 1
+    zero = jnp.zeros((rows, cols), F32)
+    span_inner = (live_ref[0] > 0.0) & jnp.logical_not(last_row)
+    chord_inner = (live_ref[1] > 0.0) & jnp.logical_not(last_col)
+    span = [jnp.where(span_inner, span_ref[k], zero) for k in range(dof)]
+    chord = [jnp.where(chord_inner, chord_ref[k], zero) for k in range(dof)]
+    span_b = [jnp.where(first_row, zero, roll(span[k], 1, 0)) for k in range(dof)]
+    chord_b = [jnp.where(first_col, zero, roll(chord[k], 1, 1)) for k in range(dof)]
+    span_geo = jnp.where(span_inner, span_geo_ref[...], zero)
+    chord_geo = jnp.where(chord_inner, chord_geo_ref[...], zero)
+    for m in range(modes):
+        start = m * per
+        v = [modes_ref[pl.ds(start + k * rows, rows), :] for k in range(dof)]
+        jumps = [modes_ref[pl.ds(start + k * rows + 1, rows), :] - v[k] for k in range(dof)]
+        span_w = jnp.where(last_row, zero, dot(jumps, jumps) * span_geo)
+        jumps = [roll(v[k], -1, 1) - v[k] for k in range(dof)]
+        chord_w = jnp.where(last_col, zero, dot(jumps, jumps) * chord_geo)
+        span_wb, chord_wb = roll(span_w, 1, 0), roll(chord_w, 1, 1)
+        for k in range(dof):
+            load_ref[pl.ds(start + k * rows, rows), :] = (
+                (span_b[k] * span_wb - span[k] * span_w) + (chord_b[k] * chord_wb - chord[k] * chord_w)
+            )
+
+
+def first_kernel(dims, inner_ref, live_ref, span_ref, chord_ref, span_geo_ref, chord_geo_ref, ground_ref,
                  row_even_out, row_odd_out, col_even_out, col_odd_out,
                  row_even_in, row_odd_in, col_even_in, col_odd_in,
-                 load_ref, z_ref, q_ref, g_ref, coef_ref, row_even, row_odd, col_even, col_odd,
-                 inv_ref, up_ref, down_ref, rim_ref, rim2_ref):
+                 load_ref, z_ref, q_ref, coef_ref, row_even, row_odd, col_even, col_odd,
+                 up_ref, down_ref, rim_ref, rim2_ref):
     modes, dof, rows, cols = dims
     row, lane = tile_iota((rows, cols))
     slab_even, sub_even = parities()
@@ -239,13 +278,13 @@
             entry = span[i] * span[j] + span_b[i] * span_b[j] + chord[i] * chord[j] + chord_b[i] * chord_b[j]
             blocks[i][j] = entry + ground_ref[i] if i == j else entry
     inv = invert_blocks(blocks)
-    place = {}
     for i in range(dof):
         for j in range(i + 1):
-            place[i, j] = len(place)
-            inv_ref[place[i, j]] = inv[i][j]
+            coef_ref[inverse_place(dof, i, j)] = inv[i][j]
     row_rim = [jnp.where(last_row, span[k], jnp.where(first_row, span_b[k], zero)) for k in range(dof)]
     col_rim = [jnp.where(last_col, chord[k], jnp.where(first_col, chord_b[k], zero)) for k in range(dof)]
+    row_sign = [jnp.where(last_row, -row_rim[k], row_rim[k]) for k in range(dof)]
+    col_sign = [jnp.where(last_col, -col_rim[k], col_rim[k]) for k in range(dof)]
     row_inv = apply_inverse(lambda i, j: inv[i][j], row_rim)
     col_inv = apply_inverse(lambda i, j: inv[i][j], col_rim)
     for group, planes in enumerate((span, span_b, chord, chord_b, row_rim, col_rim, row_inv, col_inv)):
@@ -260,23 +299,14 @@
 
     def body(m, carry):
         start = m * per
-        v = [modes_ref[pl.ds(start + k * rows, rows), :] for k in range(dof)]
-        down = down_ref[pl.ds(m, 1), :]
-        up = up_ref[pl.ds(m, 1), :]
-        rim = roll(rim_weight, -2 * m, 1)
-        jumps = [modes_ref[pl.ds(start + k * rows + 1, rows), :] - v[k] for k in range(dof)]
-        span_w = jnp.where(last_row, down, dot(jumps, jumps) * span_geo_ref[...])
-        jumps = [roll(v[k], -1, 1) - v[k] for k in range(dof)]
-        chord_w = jnp.where(last_col, rim, dot(jumps, jumps) * chord_geo_ref[...])
-        span_wb = jnp.where(first_row, up, roll(span_w, 1, 0))
-        chord_wb = jnp.where(first_col, rim, roll(chord_w, 1, 1))
+        row_w = jnp.where(last_row, down_ref[pl.ds(m, 1), :], up_ref[pl.ds(m, 1), :])
+        col_w = roll(rim_weight, -2 * m, 1)
         span, span_b, chord, chord_b = (planes_of(i) for i in range(4))
         load = [
-            (span_b[k] * span_wb - span[k] * span_w) + (chord_b[k] * chord_wb - chord[k] * chord_w)
+            inner_ref[pl.ds(start + k * rows, rows), :] + (row_sign[k] * row_w + col_sign[k] * col_w)
             for k in range(dof)
         ]
-        entry = lambda i, j: inv_ref[place[i, j]]
-        z = apply_inverse(entry, load)
+        z = apply_inverse(lambda i, j: coef_ref[inverse_place(dof, i, j)], load)
         fwd_s, bwd_s, fwd_c, bwd_c = dot(span, z), dot(span_b, z), dot(chord, z), dot(chord_b, z)
         near = [
             jnp.where(last_row, zero, roll(bwd_s, -1, 0)),
@@ -285,19 +315,17 @@
             jnp.where(first_col, zero, roll(fwd_c, 1, 1)),
         ]
         q = [axpy4([span[k], span_b[k], chord[k], chord_b[k]], near) for k in range(dof)]
-        g = apply_inverse(entry, q)
         for k in range(dof):
             at = pl.ds(start + k * rows, rows)
             load_ref[at, :] = load[k]
             z_ref[at, :] = z[k]
             q_ref[at, :] = q[k]
-            g_ref[at, :] = g[k]
         at = pl.ds(m * rows, rows)
         rim_ref[at, :] = jnp.where(last_row, fwd_s, bwd_s)
-        rim2_ref[at, :] = dot(planes_of(4), g)
+        rim2_ref[at, :] = dot(planes_of(6), q)
         mine = (lane >> 1) == m
         col_z = roll(jnp.where(last_col, fwd_c, bwd_c), 2 * m + 1, 1)
-        col_g = roll(dot(planes_of(5), g), 2 * m + 1, 1)
+        col_g = roll(dot(planes_of(7), q), 2 * m + 1, 1)
         return jnp.where(mine, col_z, carry[0]), jnp.where(mine, col_g, carry[1])
 
     col_z, col_g = zero, zero
@@ -320,7 +348,28 @@
     row_odd[2 * modes:2 * modes + rows, :] = jnp.where(slab_even, first, last)
 
 
-def second_kernel(dims, devices, load_ref, z_ref, qp_ref, gp_ref, coef_ref,
+def solve_kernel(dims, load_ref, z_ref, q_ref, coef_ref, g_ref, first_ref, sum_ref):
+    modes, dof, rows, cols = dims
+    for m in range(modes):
+        at = [pl.ds((m * dof + k) * rows, rows) for k in range(dof)]
+        q = [q_ref[at[k], :] for k in range(dof)]
+        g = apply_inverse(lambda i, j: coef_ref[inverse_place(dof, i, j)], q)
+        for k in range(dof):
+            g_ref[at[k], :] = g[k]
+        z, load = [z_ref[at[k], :] for k in range(dof)], [load_ref[at[k], :] for k in range(dof)]
+        sum_ref[pl.ds(m * rows, rows), :] = dot(z, load)
+    for block in range(modes // 8):
+        first_ref[block * 8:block * 8 + 8, :] = sum_of_rows(sum_ref, block * 8 * rows, rows)
+
+
+def sum_of_rows(ref, base, rows):
+    total = ref[pl.ds(base, 8, stride=rows), :]
+    for r in range(1, rows):
+        total = total + ref[pl.ds(base + r, 8, stride=rows), :]
+    return total
+
+
+def second_kernel(dims, devices, first_ref, z_ref, qp_ref, gp_ref, coef_ref,
                   row_even_out, row_odd_out, col_even_out, col_odd_out,
                   row_even_in, row_odd_in, col_even_in, col_odd_in,
                   q_ref, g_ref, q2_ref, chunk_ref,
@@ -383,13 +432,12 @@
         ]
         q2 = [axpy4([span[k], span_b[k], chord[k], chord_b[k]], near) for k in range(dof)]
         z = [z_ref[at[k], :] for k in range(dof)]
-        load = [load_ref[at[k], :] for k in range(dof)]
         miss = (corner_kappa * col_ghost, corner_kappa * row_ghost)
         cross = miss[0] * jnp.where(last_row, near[0], near[1]) + miss[1] * jnp.where(last_col, near[2], near[3])
-        for which, (left, right) in enumerate(((z, load), (z, q), (g, q), (g, q2))):
+        for which, (left, right) in enumerate(((z, q), (g, q), (g, q2))):
             spot = (which * modes + m) * rows
             total = dot(left, right)
-            sum_ref[pl.ds(spot, rows), :] = total + cross if which == 3 else total
+            sum_ref[pl.ds(spot, rows), :] = total + cross if which == 2 else total
         for k in range(dof):
             q_ref[at[k], :] = q[k]
             g_ref[at[k], :] = g[k]
@@ -400,18 +448,9 @@
     corners = (zero, zero)
     for m in range(modes):
         corners = body(m, corners)
-    sums = []
-    for block in range(4 * modes // 8):
-        base = block * 8 * rows
-        total = sum_ref[pl.ds(base, 8, stride=rows), :]
-        for r in range(1, rows):
-            total = total + sum_ref[pl.ds(base + r, 8, stride=rows), :]
-        sums.append(total)
+    sums = [first_ref[...]] + [sum_of_rows(sum_ref, block * 8 * rows, rows) for block in range(3 * modes // 8)]
     sums = jnp.concatenate(sums, axis=0)
-    sums = lax.dot_general(
-        jnp.ones((8, cols), F32), sums, (((1,), (1,)), ((), ())),
-        precision=lax.Precision.HIGHEST, preferred_element_type=F32,
-    )
+    sums = times_ones(sums, True)
     chunk = jnp.where(row % LINES == 0, sums[0:1], zero)
     for which, corner in enumerate(corners):
         far = roll(jnp.broadcast_to(corner[rows - 1:rows], (rows, cols)), cols // 2, 1)
@@ -447,10 +486,7 @@
     big_row, big_lane = tile_iota((4 * modes, cols))
     spread = jnp.where(big_row == big_lane, total, 0.0)
     spread = spread + jnp.where(((big_lane & (half - 1)) >> 1) == big_row - 3 * modes, missed, 0.0)
-    spread = lax.dot_general(
-        spread, jnp.ones((cols, cols), F32), (((1,), (0,)), ((), ())),
-        precision=lax.Precision.HIGHEST, preferred_element_type=F32,
-    )
+    spread = times_ones(spread, False)
     m0, m1, m2, m3 = (spread[i * modes:(i + 1) * modes] for i in range(4))
     step0 = m0 / (m0 - m1)
     rest = 1.0 - step0
@@ -525,7 +561,7 @@
 
         plane, planes, full = (rows, cols), (dof, rows, cols), (count, cols)
         row_shape, col_shape = (modes * dof + rows, cols), ((dof + 1) * rows, cols)
-        parts = 4
+        parts = 2
         inputs = (mode_shapes.reshape(count, cols), span_stiff, chord_stiff, span_geo, chord_geo, chord_len)
         field, *coefs, row_even, row_odd, col_even, col_odd = call(
             lambda *refs: pack_kernel(dims, sizes, parts, *refs), "pack_rim",
@@ -535,19 +571,26 @@
         )
         rims = [row_even, row_odd, col_even, col_odd]
         met = exchange(rims)
+        (inner,) = call(
+            lambda *refs: inner_kernel(dims, *refs), "inner_load", (field, *coefs), [vmem] * 6, [full], [],
+        )
         row_shape, col_shape = (2 * modes + rows, cols), (3 * rows, cols)
-        load, z, qp, gp, coef, *rims2 = call(
+        load, z, qp, coef, *rims2 = call(
             lambda *refs: first_kernel(dims, *refs), "load_and_first",
-            (field, *coefs, ground, *rims, *met), [vmem] * 15,
-            [full] * 4 + [(8 * dof + 1, rows, cols), row_shape, row_shape, col_shape, col_shape],
-            [(dof * (dof + 1) // 2, rows, cols), (modes, cols), (modes, cols), (modes * rows, cols), (modes * rows, cols)],
+            (inner, *coefs, ground, *rims, *met), [vmem] * 15,
+            [full] * 3 + [(inverse_place(dof, dof, 0), rows, cols), row_shape, row_shape, col_shape, col_shape],
+            [(modes, cols), (modes, cols), (modes * rows, cols), (modes * rows, cols)],
         )
         met2 = exchange(rims2)
+        gp, first = call(
+            lambda *refs: solve_kernel(dims, *refs), "solve_inner", (load, z, qp, coef), [vmem] * 4,
+            [full, (modes, cols)], [(modes * rows, cols)],
+        )
         q, g, q2, chunk = call(
             lambda *refs: second_kernel(dims, devices, *refs), "second_and_sums",
-            (load, z, qp, gp, coef, *rims2, *met2), [vmem] * 13,
+            (first, z, qp, gp, coef, *rims2, *met2), [vmem] * 13,
             [full] * 3 + [(devices * LINES, cols)],
-            [(modes, cols)] * 4 + [(4 * modes * rows, cols)],
+            [(modes, cols)] * 4 + [(3 * modes * rows, cols)],
         )
         shares = lax.all_to_all(chunk.reshape(devices, LINES, cols), axes, 0, 0).reshape(devices * LINES, cols)
         steps = 4

time: 33.5 us -> 32.4 us (0.967)
  waiting for transfers between devices: 4.72 us -> 3.04 us
  Pallas kernels: 6.6 us -> 7.24 us
    ppermute x8, waiting for transfers between devices: 4.72 us -> 3.04 us  [exchange(): lax.ppermute(array, axes, path)]
    pallas_call x4 -> x6, Pallas kernels: 6.6 us -> 7.24 us  [call(): pl.pallas_call(kernel, out_shape=[jax.ShapeDtypeStruct(shape, F32) for sh...]
  transfers between devices with their start and end apart: 8 -> 8, of which waited for: 3 -> 3; matrix products, arithmetic and copies ran while one was open for 0% -> 0% of each run, Pallas kernels for 0% -> 5%
where the time goes in v3:
time: 32.4 us; the launch traced here: 32.2 us
  blocking collectives  12.5 us (39%)
  starting transfers between devices  8.76 us (27%)
  Pallas kernels  7.24 us (22%)
  waiting for transfers between devices  3.04 us (9%)
  between operations  0.68 us (2%)
    all_to_all x1, blocking collectives, body(): lax.all_to_all(chunk.reshape(devices, LINES, cols), axes, 0, 0)  12.5 us
    ppermute x8, starting transfers between devices, exchange(): lax.ppermute(array, axes, path)  8.76 us
    pallas_call x6, Pallas kernels, call(): pl.pallas_call(kernel, out_shape=[jax.ShapeDtypeStruct(shape, F32) for sh...  7.24 us
    ppermute x8, waiting for transfers between devices, exchange(): lax.ppermute(array, axes, path)  3.04 us
  transfers between devices with their start and end apart: 8, of which 3 were waited for; matrix products, arithmetic and copies ran while one was open for 0% of the time, Pallas kernels for 5%

profile of v3, /device:TPU:0, one launch (start us, length us, event | category | flops | bytes accessed | tf_op | source)
XLA Modules:
  0.0 32.2 jit_solution(8736642173028953281)
XLA Ops:
  0.6 1.4 %pack_rim.1 = (f32[1544,128]{1,0:T(8,128)S(1)}, f32[4,8,128]{2,1,0:T(8,128)S(1)}, f32[6,8,128]{2,1,0:T(8,128)S(1)}, f32[6,8,128]{2,1,0:T(8,128)S(1)}, f32[8,128]...) custom-call(bf16[1536,128]{1,0:T(8,128)(2,1)} %bitcast.7, ...), custom_call_target="tpu_custom_call" | custom-call | tf_op jit(solution)/shard_map/pack_rim/pallas_call | solution.py:552
  2.0 3.0 %collective-permute-start = (f32[200,128]{1,0:T(8,128)S(1)}, f32[200,128]{1,0:T(8,128)S(1)}, u32[]{:S(2)}, u32[]{:S(2)}) collective-permute-start(f32[200,128]{1,0:T(8,128)S(1)} %get-tuple-element.34.refs_7_), channel_id=1, source_target_pairs={{0,4},{1,5},{2,6},{3,7},{4,0},{5,1},{6,2},{7,3},{8,12},{9,13},{10,... | collective-permute-start | bytes 307208 | tf_op jit(solution)/shard_map/ppermute | solution.py:541
  5.1 0.0 collective-permute-start.1
  5.1 0.5 %collective-permute-start.2 = (f32[56,128]{1,0:T(8,128)S(1)}, f32[56,128]{1,0:T(8,128)S(1)}, u32[]{:S(2)}, u32[]{:S(2)}) collective-permute-start(f32[56,128]{1,0:T(8,128)S(1)} %get-tuple-element.36.refs_9_), channel_id=1, source_target_pairs={{0,1},{1,0},{2,3},{3,2},{4,5},{5,4},{6,7},{7,6},{8,9},{9,8},{10,11... | collective-permute-start | bytes 86024 | tf_op jit(solution)/shard_map/ppermute | solution.py:541
  5.6 1.1 %collective-permute-start.3 = (f32[56,128]{1,0:T(8,128)S(1)}, f32[56,128]{1,0:T(8,128)S(1)}, u32[]{:S(2)}, u32[]{:S(2)}) collective-permute-start(f32[56,128]{1,0:T(8,128)S(1)} %get-tuple-element.37.refs_10_), channel_id=1, source_target_pairs={{0,3},{1,2},{2,1},{3,0},{4,7},{5,6},{6,5},{7,4},{8,11},{9,10},{10,... | collective-permute-start | bytes 86024 | tf_op jit(solution)/shard_map/ppermute | solution.py:541
  6.7 0.0 copy-start
  6.7 1.3 %inner_load.1.refs_0_ = f32[1536,128]{1,0:T(8,128)S(1)} custom-call(f32[1544,128]{1,0:T(8,128)S(1)} %get-tuple-element.28.refs_0_, f32[4,8,128]{2,1,0:T(8,128)S(1)} %get-tuple-element.29.refs_1_, f32[6,8,128]{2,1,0:T(8,128)S(1)} %get-tuple-element.30.refs_2_, f32[6,8,128]{2,1,0:T(8,128)S(1)} %get-tuple-element.31.refs_3_, ...), custom_call_target="tpu_custom_call" | custom-call | tf_op jit(solution)/shard_map/inner_load/pallas_call | solution.py:552
  8.0 0.0 collective-permute-done.2.refs_13_
  8.0 1.0 %collective-permute-done.3.refs_14_ = f32[56,128]{1,0:T(8,128)S(1)} collective-permute-done((f32[56,128]{1,0:T(8,128)S(1)}, f32[56,128]{1,0:T(8,128)S(1)}, u32[]{:S(2)}, u32[]{:S(2)}) %collective-permute-start.3) | collective-permute-done | bytes 28704 | tf_op jit(solution)/shard_map/ppermute | solution.py:541
  9.0 0.4 %collective-permute-done.refs_11_ = f32[200,128]{1,0:T(8,128)S(1)} collective-permute-done((f32[200,128]{1,0:T(8,128)S(1)}, f32[200,128]{1,0:T(8,128)S(1)}, u32[]{:S(2)}, u32[]{:S(2)}) %collective-permute-start) | collective-permute-done | bytes 102432 | tf_op jit(solution)/shard_map/ppermute | solution.py:541
  9.4 0.0 collective-permute-done.1.refs_12_
  9.4 0.0 copy-done
  9.4 1.3 %load_and_first.1 = (f32[1536,128]{1,0:T(8,128)S(1)}, f32[1536,128]{1,0:T(8,128)S(1)}, f32[1536,128]{1,0:T(8,128)S(1)}, f32[70,8,128]{2,1,0:T(8,128)S(1)}, f32[7...) custom-call(f32[1536,128]{1,0:T(8,128)S(1)} %inner_load.1.refs_0_, ...), custom_call_target="tpu_custom_call" | custom-call | tf_op jit(solution)/shard_map/load_and_first/pallas_call | solution.py:552
  10.7 2.5 %collective-permute-start.4 = (f32[72,128]{1,0:T(8,128)S(1)}, f32[72,128]{1,0:T(8,128)S(1)}, u32[]{:S(2)}, u32[]{:S(2)}) collective-permute-start(f32[72,128]{1,0:T(8,128)S(1)} %get-tuple-element.44.refs_5_), channel_id=1, source_target_pairs={{0,4},{1,5},{2,6},{3,7},{4,0},{5,1},{6,2},{7,3},{8,12},{9,13},{10,... | collective-permute-start | bytes 110600 | tf_op jit(solution)/shard_map/ppermute | solution.py:541
  13.2 0.0 collective-permute-start.5
  13.2 0.5 %collective-permute-start.6 = (f32[24,128]{1,0:T(8,128)S(1)}, f32[24,128]{1,0:T(8,128)S(1)}, u32[]{:S(2)}, u32[]{:S(2)}) collective-permute-start(f32[24,128]{1,0:T(8,128)S(1)} %get-tuple-element.46.refs_7_), channel_id=1, source_target_pairs={{0,1},{1,0},{2,3},{3,2},{4,5},{5,4},{6,7},{7,6},{8,9},{9,8},{10,11... | collective-permute-start | bytes 36872 | tf_op jit(solution)/shard_map/ppermute | solution.py:541
  13.7 1.1 %collective-permute-start.7 = (f32[24,128]{1,0:T(8,128)S(1)}, f32[24,128]{1,0:T(8,128)S(1)}, u32[]{:S(2)}, u32[]{:S(2)}) collective-permute-start(f32[24,128]{1,0:T(8,128)S(1)} %get-tuple-element.47.refs_8_), channel_id=1, source_target_pairs={{0,3},{1,2},{2,1},{3,0},{4,7},{5,6},{6,5},{7,4},{8,11},{9,10},{10,... | collective-permute-start | bytes 36872 | tf_op jit(solution)/shard_map/ppermute | solution.py:541
  14.9 0.3 %solve_inner.1 = (f32[1536,128]{1,0:T(8,128)S(1)}, f32[32,128]{1,0:T(8,128)S(1)}) custom-call(f32[1536,128]{1,0:T(8,128)S(1)} %get-tuple-element.38.refs_0_.refs_2_, f32[1536,128]{1,0:T(8,128)S(1)} %get-tuple-element.39.refs_1_.refs_3_, f32[1536,128]{1,0:T(8,128)S(1)} %get-tuple-element.40.refs_2_, f32[70,8,128]{2,1,0:T(8,128)S(1)} %get-tuple-element.41.refs_3_.refs_4_.refs_1_), custom_call_target="tpu_custom_call" | custom-call | tf_op jit(solution)/shard_map/solve_inner/pallas_call | solution.py:552
  15.2 0.0 collective-permute-done.6.refs_11_
  15.2 1.6 %collective-permute-done.7.refs_12_ = f32[24,128]{1,0:T(8,128)S(1)} collective-permute-done((f32[24,128]{1,0:T(8,128)S(1)}, f32[24,128]{1,0:T(8,128)S(1)}, u32[]{:S(2)}, u32[]{:S(2)}) %collective-permute-start.7) | collective-permute-done | bytes 12320 | tf_op jit(solution)/shard_map/ppermute | solution.py:541
  16.9 0.0 collective-permute-done.4.refs_9_
  16.9 0.0 collective-permute-done.5.refs_10_
  16.9 1.3 %second_and_sums.1 = (f32[1536,128]{1,0:T(8,128)S(1)}, f32[1536,128]{1,0:T(8,128)S(1)}, f32[1536,128]{1,0:T(8,128)S(1)}, f32[128,128]{1,0:T(8,128)S(1)}) custom-call(f32[32,128]{1,0:T(8,128)S(1)} %get-tuple-element.42.refs_0_, f32[1536,128]{1,0:T(8,128)S(1)} %get-tuple-element.39.refs_1_.refs_3_, f32[1536,128]{1,0:T(8,128)S(1)} %get-tuple-element.40.refs_2_, ...), custom_call_target="tpu_custom_call" | custom-call | tf_op jit(solution)/shard_map/second_and_sums/pallas_call | solution.py:552
  18.2 12.5 %all_to_all.5 = f32[32,4,128]{2,1,0:T(4,128)S(1)} all-to-all(f32[32,4,128]{2,1,0:T(4,128)S(1)} %bitcast.6), channel_id=1, replica_groups=mesh['slab'=8,'sub'=4] {'slab','sub'}, dimensions={0} | all-to-all | bytes 131072 | tf_op jit(solution)/shard_map/all_to_all | solution.py:595
  30.7 1.6 %combine.1 = (f32[1536,128]{1,0:T(8,128)}, f32[1536,128]{1,0:T(8,128)}) custom-call(f32[128,128]{1,0:T(8,128)S(1)} %bitcast.5, f32[70,8,128]{2,1,0:T(8,128)S(1)} %get-tuple-element.41.refs_3_.refs_4_.refs_1_, f32[1536,128]{1,0:T(8,128)S(1)} %get-tuple-element.38.refs_0_.refs_2_, f32[1536,128]{1,0:T(8,128)S(1)} %get-tuple-element.39.refs_1_.refs_3_, ...), custom_call_target="tpu_custom_call" | custom-call | tf_op jit(solution)/shard_map/combine/pallas_call | solution.py:552
Async XLA Ops:
  2.0 7.4 %collective-permute-start = (f32[200,128]{1,0:T(8,128)S(1)}, f32[200,128]{1,0:T(8,128)S(1)}, u32[]{:S(2)}, u32[]{:S(2)}) collective-permute-start(f32[200,128]{1,0:T(8,128)S(1)} %get-tuple-element.34.refs_7_), channel_id=1, source_target_pairs={{0,4},{1,5},{2,6},{3,7},{4,0},{5,1},{6,2},{7,3},{8,12},{9,13},{10,... | collective-permute-start | bytes 307208 | tf_op jit(solution)/shard_map/ppermute | solution.py:541
  5.1 4.3 %collective-permute-start.1 = (f32[200,128]{1,0:T(8,128)S(1)}, f32[200,128]{1,0:T(8,128)S(1)}, u32[]{:S(2)}, u32[]{:S(2)}) collective-permute-start(f32[200,128]{1,0:T(8,128)S(1)} %get-tuple-element.35.refs_8_), channel_id=1, source_target_pairs={{0,1},{1,0},{2,3},{3,2},{4,8},{5,9},{6,10},{7,11},{8,4},{9,5},{10,... | collective-permute-start | bytes 307208 | tf_op jit(solution)/shard_map/ppermute | solution.py:541
  5.1 2.9 %collective-permute-start.2 = (f32[56,128]{1,0:T(8,128)S(1)}, f32[56,128]{1,0:T(8,128)S(1)}, u32[]{:S(2)}, u32[]{:S(2)}) collective-permute-start(f32[56,128]{1,0:T(8,128)S(1)} %get-tuple-element.36.refs_9_), channel_id=1, source_target_pairs={{0,1},{1,0},{2,3},{3,2},{4,5},{5,4},{6,7},{7,6},{8,9},{9,8},{10,11... | collective-permute-start | bytes 86024 | tf_op jit(solution)/shard_map/ppermute | solution.py:541
  5.6 3.4 %collective-permute-start.3 = (f32[56,128]{1,0:T(8,128)S(1)}, f32[56,128]{1,0:T(8,128)S(1)}, u32[]{:S(2)}, u32[]{:S(2)}) collective-permute-start(f32[56,128]{1,0:T(8,128)S(1)} %get-tuple-element.37.refs_10_), channel_id=1, source_target_pairs={{0,3},{1,2},{2,1},{3,0},{4,7},{5,6},{6,5},{7,4},{8,11},{9,10},{10,... | collective-permute-start | bytes 86024 | tf_op jit(solution)/shard_map/ppermute | solution.py:541
  6.7 2.7 %copy-start = (f32[6,8,128]{2,1,0:T(8,128)S(1)}, f32[6,8,128]{2,1,0:T(8,128)}, u32[]{:S(2)}) copy-start(f32[6,8,128]{2,1,0:T(8,128)} %refs_6_.1) | copy-start | bytes 73732
  10.7 6.1 %collective-permute-start.4 = (f32[72,128]{1,0:T(8,128)S(1)}, f32[72,128]{1,0:T(8,128)S(1)}, u32[]{:S(2)}, u32[]{:S(2)}) collective-permute-start(f32[72,128]{1,0:T(8,128)S(1)} %get-tuple-element.44.refs_5_), channel_id=1, source_target_pairs={{0,4},{1,5},{2,6},{3,7},{4,0},{5,1},{6,2},{7,3},{8,12},{9,13},{10,... | collective-permute-start | bytes 110600 | tf_op jit(solution)/shard_map/ppermute | solution.py:541
  13.2 3.6 %collective-permute-start.5 = (f32[72,128]{1,0:T(8,128)S(1)}, f32[72,128]{1,0:T(8,128)S(1)}, u32[]{:S(2)}, u32[]{:S(2)}) collective-permute-start(f32[72,128]{1,0:T(8,128)S(1)} %get-tuple-element.45.refs_6_), channel_id=1, source_target_pairs={{0,1},{1,0},{2,3},{3,2},{4,8},{5,9},{6,10},{7,11},{8,4},{9,5},{10,... | collective-permute-start | bytes 110600 | tf_op jit(solution)/shard_map/ppermute | solution.py:541
  13.2 2.0 %collective-permute-start.6 = (f32[24,128]{1,0:T(8,128)S(1)}, f32[24,128]{1,0:T(8,128)S(1)}, u32[]{:S(2)}, u32[]{:S(2)}) collective-permute-start(f32[24,128]{1,0:T(8,128)S(1)} %get-tuple-element.46.refs_7_), channel_id=1, source_target_pairs={{0,1},{1,0},{2,3},{3,2},{4,5},{5,4},{6,7},{7,6},{8,9},{9,8},{10,11... | collective-permute-start | bytes 36872 | tf_op jit(solution)/shard_map/ppermute | solution.py:541
  13.7 3.1 %collective-permute-start.7 = (f32[24,128]{1,0:T(8,128)S(1)}, f32[24,128]{1,0:T(8,128)S(1)}, u32[]{:S(2)}, u32[]{:S(2)}) collective-permute-start(f32[24,128]{1,0:T(8,128)S(1)} %get-tuple-element.47.refs_8_), channel_id=1, source_target_pairs={{0,3},{1,2},{2,1},{3,0},{4,7},{5,6},{6,5},{7,4},{8,11},{9,10},{10,... | collective-permute-start | bytes 36872 | tf_op jit(solution)/shard_map/ppermute | solution.py:541

commit v4 on v3

--- a/solution.py
+++ b/solution.py
@@ -133,37 +133,22 @@
     col_odd[dof * rows:(dof + 1) * rows, :] = edge
 
 
-def invert_blocks(blocks):
+def factor_blocks(blocks):
     count = len(blocks)
     scaled = [[None] * count for i in range(count)]
     factor = [[None] * count for i in range(count)]
-    inverse = [None] * count
     for j in range(count):
         running = blocks[j][j]
         for k in range(j):
             running = running - scaled[j][k] * factor[j][k]
-        inverse[j] = 1.0 / running
+        factor[j][j] = 1.0 / running
         for i in range(j + 1, count):
             running = blocks[i][j]
             for k in range(j):
                 running = running - scaled[i][k] * factor[j][k]
             scaled[i][j] = running
-            factor[i][j] = running * inverse[j]
-    lower = [[None] * count for i in range(count)]
-    for j in range(count):
-        for i in range(j + 1, count):
-            running = factor[i][j]
-            for k in range(j + 1, i):
-                running = running + factor[i][k] * lower[k][j]
-            lower[i][j] = -running
-    result = [[None] * count for i in range(count)]
-    for i in range(count):
-        for j in range(i + 1):
-            running = inverse[i] if i == j else inverse[i] * lower[i][j]
-            for k in range(i + 1, count):
-                running = running + (lower[k][i] * inverse[k]) * lower[k][j]
-            result[i][j] = running
-    return result
+            factor[i][j] = running * factor[j][j]
+    return factor
 
 
 def times_ones(value, transposed):
@@ -179,13 +164,25 @@
     return lax.dot_general(pieces, ones, (((1,), (0,)), ((), ())), preferred_element_type=F32)
 
 
-def inverse_place(dof, i, j):
+def factor_place(dof, i, j):
     return 8 * dof + 1 + i * (i + 1) // 2 + j
 
 
-def apply_inverse(entry, vector):
+def solve_blocks(factor, vector):
     count = len(vector)
-    return [dot([entry(max(i, j), min(i, j)) for j in range(count)], vector) for i in range(count)]
+    forward = []
+    for i in range(count):
+        running = vector[i]
+        for j in range(i):
+            running = running - factor(i, j) * forward[j]
+        forward.append(running)
+    backward = [None] * count
+    for i in reversed(range(count)):
+        running = forward[i] * factor(i, i)
+        for j in range(i + 1, count):
+            running = running - factor(j, i) * backward[j]
+        backward[i] = running
+    return backward
 
 
 def inner_kernel(dims, modes_ref, live_ref, span_ref, chord_ref, span_geo_ref, chord_geo_ref, load_ref):
@@ -277,16 +274,16 @@
         for j in range(i + 1):
             entry = span[i] * span[j] + span_b[i] * span_b[j] + chord[i] * chord[j] + chord_b[i] * chord_b[j]
             blocks[i][j] = entry + ground_ref[i] if i == j else entry
-    inv = invert_blocks(blocks)
+    factor = factor_blocks(blocks)
     for i in range(dof):
         for j in range(i + 1):
-            coef_ref[inverse_place(dof, i, j)] = inv[i][j]
+            coef_ref[factor_place(dof, i, j)] = factor[i][j]
     row_rim = [jnp.where(last_row, span[k], jnp.where(first_row, span_b[k], zero)) for k in range(dof)]
     col_rim = [jnp.where(last_col, chord[k], jnp.where(first_col, chord_b[k], zero)) for k in range(dof)]
     row_sign = [jnp.where(last_row, -row_rim[k], row_rim[k]) for k in range(dof)]
     col_sign = [jnp.where(last_col, -col_rim[k], col_rim[k]) for k in range(dof)]
-    row_inv = apply_inverse(lambda i, j: inv[i][j], row_rim)
-    col_inv = apply_inverse(lambda i, j: inv[i][j], col_rim)
+    row_inv = solve_blocks(lambda i, j: factor[i][j], row_rim)
+    col_inv = solve_blocks(lambda i, j: factor[i][j], col_rim)
     for group, planes in enumerate((span, span_b, chord, chord_b, row_rim, col_rim, row_inv, col_inv)):
         for k in range(dof):
             coef_ref[group * dof + k] = planes[k]
@@ -306,7 +303,7 @@
             inner_ref[pl.ds(start + k * rows, rows), :] + (row_sign[k] * row_w + col_sign[k] * col_w)
             for k in range(dof)
         ]
-        z = apply_inverse(lambda i, j: coef_ref[inverse_place(dof, i, j)], load)
+        z = solve_blocks(lambda i, j: coef_ref[factor_place(dof, i, j)], load)
         fwd_s, bwd_s, fwd_c, bwd_c = dot(span, z), dot(span_b, z), dot(chord, z), dot(chord_b, z)
         near = [
             jnp.where(last_row, zero, roll(bwd_s, -1, 0)),
@@ -353,7 +350,7 @@
     for m in range(modes):
         at = [pl.ds((m * dof + k) * rows, rows) for k in range(dof)]
         q = [q_ref[at[k], :] for k in range(dof)]
-        g = apply_inverse(lambda i, j: coef_ref[inverse_place(dof, i, j)], q)
+        g = solve_blocks(lambda i, j: coef_ref[factor_place(dof, i, j)], q)
         for k in range(dof):
             g_ref[at[k], :] = g[k]
         z, load = [z_ref[at[k], :] for k in range(dof)], [load_ref[at[k], :] for k in range(dof)]
@@ -450,7 +447,7 @@
         corners = body(m, corners)
     sums = [first_ref[...]] + [sum_of_rows(sum_ref, block * 8 * rows, rows) for block in range(3 * modes // 8)]
     sums = jnp.concatenate(sums, axis=0)
-    sums = times_ones(sums, True)
+    sums = jnp.sum(jnp.transpose(sums), axis=0, keepdims=True)
     chunk = jnp.where(row % LINES == 0, sums[0:1], zero)
     for which, corner in enumerate(corners):
         far = roll(jnp.broadcast_to(corner[rows - 1:rows], (rows, cols)), cols // 2, 1)
@@ -465,7 +462,7 @@
 
 
 def last_kernel(dims, sizes, steps, part_ref, coef_ref, load_ref, z_ref, q_ref, g_ref, q2_ref,
-                adjoint_hbm, residual_hbm, a_ref, b_ref, adjoint_ref, residual_ref, sems):
+                adjoint_hbm, residual_hbm, a_ref, b_ref, load_share_ref, q_share_ref, shares_ref, adjoint_ref, residual_ref, sems):
     modes, dof, rows, cols = dims
     slabs, subs = sizes
     devices = slabs * subs
@@ -473,8 +470,10 @@
     per = dof * rows
     half = cols // 2
 
+    shares_ref[0:devices * LINES, :] = part_ref[...]
+
     def lines(which):
-        return part_ref[pl.ds(which, devices, stride=LINES), :]
+        return shares_ref[pl.ds(which, devices, stride=LINES), :]
 
     miss_row, miss_col = lines(1), lines(2)
     wide = lax.broadcasted_iota(jnp.int32, (devices, cols), 1)
@@ -488,14 +487,18 @@
     spread = spread + jnp.where(((big_lane & (half - 1)) >> 1) == big_row - 3 * modes, missed, 0.0)
     spread = times_ones(spread, False)
     m0, m1, m2, m3 = (spread[i * modes:(i + 1) * modes] for i in range(4))
-    step0 = m0 / (m0 - m1)
-    rest = 1.0 - step0
-    rz1 = rest * rest * m0 + 2.0 * rest * step0 * m1 + step0 * step0 * m2
-    c0 = rest + rz1 / m0
-    pq1 = c0 * c0 * (m0 - m1) + 2.0 * c0 * step0 * (m1 - m2) + step0 * step0 * (m2 - m3)
-    step1 = rz1 / pq1
+    m1, m2, m3 = m1 / m0, m2 / m0, m3 / m0
+    step0 = 1.0 / (1.0 - m1)
+    square = step0 * step0
+    beta = (m2 - m1 * m1) * square
+    c0 = (m2 - m1) * square
+    excess = beta * beta - (c0 * c0 * m1 + 2.0 * c0 * step0 * m2 + square * m3)
+    inverse = 1.0 / (beta + excess)
+    step1 = beta * inverse
     a_ref[...] = step0 + step1 * c0
     b_ref[...] = step1 * step0
+    load_share_ref[...] = -m1 * step0 - step1 * c0
+    q_share_ref[...] = step0 * (excess * inverse) + step1 * c0
 
     here = lax.axis_index("slab") * subs + lax.axis_index("sub")
 
@@ -512,13 +515,15 @@
     for m in range(modes):
         a = a_ref[m:m + 1, :]
         b = b_ref[m:m + 1, :]
+        load_share = load_share_ref[m:m + 1, :]
+        q_share = q_share_ref[m:m + 1, :]
         row_fix = b * jnp.where(corner, roll(row_fixes, -1 - 2 * m, 1), 0.0)
         col_fix = b * jnp.where(corner, roll(col_fixes, -1 - 2 * m, 1), 0.0)
         for k in range(dof):
             at = pl.ds(m * per + k * rows, rows)
             adjoint_ref[at, :] = a * z_ref[at, :] + b * g_ref[at, :]
             residual_ref[at, :] = (
-                ((1.0 - a) * load_ref[at, :] + (a - b) * q_ref[at, :])
+                (load_share * load_ref[at, :] + q_share * q_ref[at, :])
                 + (b * q2_ref[at, :] + (coef_ref[4 * dof + k] * row_fix + coef_ref[5 * dof + k] * col_fix))
             )
         if (m + 1) % count == 0:
@@ -566,7 +571,7 @@
         field, *coefs, row_even, row_odd, col_even, col_odd = call(
             lambda *refs: pack_kernel(dims, sizes, parts, *refs), "pack_rim",
             [pltpu.with_memory_space_constraint(x, pltpu.HBM) for x in inputs], [hbm] * 6,
-            [(count + rows, cols), (4, rows, cols), planes, planes, plane, plane, row_shape, row_shape, col_shape, col_shape],
+            [(count + 8 * dof * rows, cols), (4, rows, cols), planes, planes, plane, plane, row_shape, row_shape, col_shape, col_shape],
             [pltpu.VMEM(full, mode_shapes.dtype), pltpu.SMEM(chord_len.shape, jnp.int32), pltpu.SemaphoreType.DMA((parts + 5,))],
         )
         rims = [row_even, row_odd, col_even, col_odd]
@@ -578,26 +583,26 @@
         load, z, qp, coef, *rims2 = call(
             lambda *refs: first_kernel(dims, *refs), "load_and_first",
             (inner, *coefs, ground, *rims, *met), [vmem] * 15,
-            [full] * 3 + [(inverse_place(dof, dof, 0), rows, cols), row_shape, row_shape, col_shape, col_shape],
-            [(modes, cols), (modes, cols), (modes * rows, cols), (modes * rows, cols)],
+            [full] * 3 + [(factor_place(dof, dof, 0), rows, cols), row_shape, row_shape, col_shape, col_shape],
+            [(modes, cols), (modes, cols), ((modes + 1) * rows, cols), ((modes + 1) * rows, cols)],
         )
         met2 = exchange(rims2)
         gp, first = call(
             lambda *refs: solve_kernel(dims, *refs), "solve_inner", (load, z, qp, coef), [vmem] * 4,
-            [full, (modes, cols)], [(modes * rows, cols)],
+            [full, (modes, cols)], [((modes + 1) * rows, cols)],
         )
         q, g, q2, chunk = call(
             lambda *refs: second_kernel(dims, devices, *refs), "second_and_sums",
             (first, z, qp, gp, coef, *rims2, *met2), [vmem] * 13,
             [full] * 3 + [(devices * LINES, cols)],
-            [(modes, cols)] * 4 + [(3 * modes * rows, cols)],
+            [(modes, cols)] * 4 + [((3 * modes + 1) * rows, cols)],
         )
         shares = lax.all_to_all(chunk.reshape(devices, LINES, cols), axes, 0, 0).reshape(devices * LINES, cols)
         steps = 4
         adjoint, residual = call(
             lambda *refs: last_kernel(dims, sizes, steps, *refs), "combine",
             (shares, coef, load, z, q, g, q2), [vmem] * 7, [full] * 2,
-            [(modes, cols), (modes, cols), full, full, pltpu.SemaphoreType.DMA((2 * steps,))], hbm,
+            [(modes, cols)] * 4 + [(devices * LINES + 8, cols), full, full, pltpu.SemaphoreType.DMA((2 * steps,))], hbm,
         )
         return adjoint.reshape(dims), residual.reshape(dims)
 

time: 32.4 us -> 32.4 us (level)
  no operation moved by 1% of the time
where the time goes in v4:
time: 32.4 us; the launch traced here: 32.2 us
  blocking collectives  12.5 us (39%)
  starting transfers between devices  8.76 us (27%)
  Pallas kernels  7.22 us (22%)
  waiting for transfers between devices  3.04 us (9%)
  between operations  0.68 us (2%)
    all_to_all x1, blocking collectives, body(): lax.all_to_all(chunk.reshape(devices, LINES, cols), axes, 0, 0)  12.5 us
    ppermute x8, starting transfers between devices, exchange(): lax.ppermute(array, axes, path)  8.76 us
    pallas_call x6, Pallas kernels, call(): pl.pallas_call(kernel, out_shape=[jax.ShapeDtypeStruct(shape, F32) for sh...  7.22 us
    ppermute x8, waiting for transfers between devices, exchange(): lax.ppermute(array, axes, path)  3.04 us
  transfers between devices with their start and end apart: 8, of which 3 were waited for; matrix products, arithmetic and copies ran while one was open for 0% of the time, Pallas kernels for 5%

profile of v4, /device:TPU:0, one launch (start us, length us, event | category | flops | bytes accessed | tf_op | source)
XLA Modules:
  0.0 32.2 jit_solution(12303902980096459220)
XLA Ops:
  0.6 1.4 %pack_rim.1 = (f32[1920,128]{1,0:T(8,128)S(1)}, f32[4,8,128]{2,1,0:T(8,128)S(1)}, f32[6,8,128]{2,1,0:T(8,128)S(1)}, f32[6,8,128]{2,1,0:T(8,128)S(1)}, f32[8,128]...) custom-call(bf16[1536,128]{1,0:T(8,128)(2,1)} %bitcast.7, ...), custom_call_target="tpu_custom_call" | custom-call | tf_op jit(solution)/shard_map/pack_rim/pallas_call | solution.py:557
  2.0 3.0 %collective-permute-start = (f32[200,128]{1,0:T(8,128)S(1)}, f32[200,128]{1,0:T(8,128)S(1)}, u32[]{:S(2)}, u32[]{:S(2)}) collective-permute-start(f32[200,128]{1,0:T(8,128)S(1)} %get-tuple-element.34.refs_7_), channel_id=1, source_target_pairs={{0,4},{1,5},{2,6},{3,7},{4,0},{5,1},{6,2},{7,3},{8,12},{9,13},{10,... | collective-permute-start | bytes 307208 | tf_op jit(solution)/shard_map/ppermute | solution.py:546
  5.1 0.0 collective-permute-start.1
  5.1 0.5 %collective-permute-start.2 = (f32[56,128]{1,0:T(8,128)S(1)}, f32[56,128]{1,0:T(8,128)S(1)}, u32[]{:S(2)}, u32[]{:S(2)}) collective-permute-start(f32[56,128]{1,0:T(8,128)S(1)} %get-tuple-element.36.refs_9_), channel_id=1, source_target_pairs={{0,1},{1,0},{2,3},{3,2},{4,5},{5,4},{6,7},{7,6},{8,9},{9,8},{10,11... | collective-permute-start | bytes 86024 | tf_op jit(solution)/shard_map/ppermute | solution.py:546
  5.6 1.1 %collective-permute-start.3 = (f32[56,128]{1,0:T(8,128)S(1)}, f32[56,128]{1,0:T(8,128)S(1)}, u32[]{:S(2)}, u32[]{:S(2)}) collective-permute-start(f32[56,128]{1,0:T(8,128)S(1)} %get-tuple-element.37.refs_10_), channel_id=1, source_target_pairs={{0,3},{1,2},{2,1},{3,0},{4,7},{5,6},{6,5},{7,4},{8,11},{9,10},{10,... | collective-permute-start | bytes 86024 | tf_op jit(solution)/shard_map/ppermute | solution.py:546
  6.7 0.0 copy-start
  6.7 1.3 %inner_load.1.refs_0_ = f32[1536,128]{1,0:T(8,128)S(1)} custom-call(f32[1920,128]{1,0:T(8,128)S(1)} %get-tuple-element.28.refs_0_, f32[4,8,128]{2,1,0:T(8,128)S(1)} %get-tuple-element.29.refs_1_, f32[6,8,128]{2,1,0:T(8,128)S(1)} %get-tuple-element.30.refs_2_, f32[6,8,128]{2,1,0:T(8,128)S(1)} %get-tuple-element.31.refs_3_, ...), custom_call_target="tpu_custom_call" | custom-call | tf_op jit(solution)/shard_map/inner_load/pallas_call | solution.py:557
  8.0 0.0 collective-permute-done.2.refs_13_
  8.0 1.0 %collective-permute-done.3.refs_14_ = f32[56,128]{1,0:T(8,128)S(1)} collective-permute-done((f32[56,128]{1,0:T(8,128)S(1)}, f32[56,128]{1,0:T(8,128)S(1)}, u32[]{:S(2)}, u32[]{:S(2)}) %collective-permute-start.3) | collective-permute-done | bytes 28704 | tf_op jit(solution)/shard_map/ppermute | solution.py:546
  9.0 0.4 %collective-permute-done.refs_11_ = f32[200,128]{1,0:T(8,128)S(1)} collective-permute-done((f32[200,128]{1,0:T(8,128)S(1)}, f32[200,128]{1,0:T(8,128)S(1)}, u32[]{:S(2)}, u32[]{:S(2)}) %collective-permute-start) | collective-permute-done | bytes 102432 | tf_op jit(solution)/shard_map/ppermute | solution.py:546
  9.4 0.0 collective-permute-done.1.refs_12_
  9.4 0.0 copy-done
  9.4 1.3 %load_and_first.1 = (f32[1536,128]{1,0:T(8,128)S(1)}, f32[1536,128]{1,0:T(8,128)S(1)}, f32[1536,128]{1,0:T(8,128)S(1)}, f32[70,8,128]{2,1,0:T(8,128)S(1)}, f32[7...) custom-call(f32[1536,128]{1,0:T(8,128)S(1)} %inner_load.1.refs_0_, ...), custom_call_target="tpu_custom_call" | custom-call | tf_op jit(solution)/shard_map/load_and_first/pallas_call | solution.py:557
  10.7 2.5 %collective-permute-start.4 = (f32[72,128]{1,0:T(8,128)S(1)}, f32[72,128]{1,0:T(8,128)S(1)}, u32[]{:S(2)}, u32[]{:S(2)}) collective-permute-start(f32[72,128]{1,0:T(8,128)S(1)} %get-tuple-element.44.refs_5_), channel_id=1, source_target_pairs={{0,4},{1,5},{2,6},{3,7},{4,0},{5,1},{6,2},{7,3},{8,12},{9,13},{10,... | collective-permute-start | bytes 110600 | tf_op jit(solution)/shard_map/ppermute | solution.py:546
  13.2 0.0 collective-permute-start.5
  13.2 0.5 %collective-permute-start.6 = (f32[24,128]{1,0:T(8,128)S(1)}, f32[24,128]{1,0:T(8,128)S(1)}, u32[]{:S(2)}, u32[]{:S(2)}) collective-permute-start(f32[24,128]{1,0:T(8,128)S(1)} %get-tuple-element.46.refs_7_), channel_id=1, source_target_pairs={{0,1},{1,0},{2,3},{3,2},{4,5},{5,4},{6,7},{7,6},{8,9},{9,8},{10,11... | collective-permute-start | bytes 36872 | tf_op jit(solution)/shard_map/ppermute | solution.py:546
  13.7 1.1 %collective-permute-start.7 = (f32[24,128]{1,0:T(8,128)S(1)}, f32[24,128]{1,0:T(8,128)S(1)}, u32[]{:S(2)}, u32[]{:S(2)}) collective-permute-start(f32[24,128]{1,0:T(8,128)S(1)} %get-tuple-element.47.refs_8_), channel_id=1, source_target_pairs={{0,3},{1,2},{2,1},{3,0},{4,7},{5,6},{6,5},{7,4},{8,11},{9,10},{10,... | collective-permute-start | bytes 36872 | tf_op jit(solution)/shard_map/ppermute | solution.py:546
  14.9 0.4 %solve_inner.1 = (f32[1536,128]{1,0:T(8,128)S(1)}, f32[32,128]{1,0:T(8,128)S(1)}) custom-call(f32[1536,128]{1,0:T(8,128)S(1)} %get-tuple-element.38.refs_0_.refs_2_, f32[1536,128]{1,0:T(8,128)S(1)} %get-tuple-element.39.refs_1_.refs_3_, f32[1536,128]{1,0:T(8,128)S(1)} %get-tuple-element.40.refs_2_, f32[70,8,128]{2,1,0:T(8,128)S(1)} %get-tuple-element.41.refs_3_.refs_4_.refs_1_), custom_call_target="tpu_custom_call" | custom-call | tf_op jit(solution)/shard_map/solve_inner/pallas_call | solution.py:557
  15.2 0.0 collective-permute-done.6.refs_11_
  15.2 1.6 %collective-permute-done.7.refs_12_ = f32[24,128]{1,0:T(8,128)S(1)} collective-permute-done((f32[24,128]{1,0:T(8,128)S(1)}, f32[24,128]{1,0:T(8,128)S(1)}, u32[]{:S(2)}, u32[]{:S(2)}) %collective-permute-start.7) | collective-permute-done | bytes 12320 | tf_op jit(solution)/shard_map/ppermute | solution.py:546
  16.9 0.0 collective-permute-done.4.refs_9_
  16.9 0.0 collective-permute-done.5.refs_10_
  16.9 1.2 %second_and_sums.1 = (f32[1536,128]{1,0:T(8,128)S(1)}, f32[1536,128]{1,0:T(8,128)S(1)}, f32[1536,128]{1,0:T(8,128)S(1)}, f32[128,128]{1,0:T(8,128)S(1)}) custom-call(f32[32,128]{1,0:T(8,128)S(1)} %get-tuple-element.42.refs_0_, f32[1536,128]{1,0:T(8,128)S(1)} %get-tuple-element.39.refs_1_.refs_3_, f32[1536,128]{1,0:T(8,128)S(1)} %get-tuple-element.40.refs_2_, ...), custom_call_target="tpu_custom_call" | custom-call | tf_op jit(solution)/shard_map/second_and_sums/pallas_call | solution.py:557
  18.1 12.5 %all_to_all.5 = f32[32,4,128]{2,1,0:T(4,128)S(1)} all-to-all(f32[32,4,128]{2,1,0:T(4,128)S(1)} %bitcast.6), channel_id=1, replica_groups=mesh['slab'=8,'sub'=4] {'slab','sub'}, dimensions={0} | all-to-all | bytes 131072 | tf_op jit(solution)/shard_map/all_to_all | solution.py:600
  30.6 1.6 %combine.1 = (f32[1536,128]{1,0:T(8,128)}, f32[1536,128]{1,0:T(8,128)}) custom-call(f32[128,128]{1,0:T(8,128)S(1)} %bitcast.5, f32[70,8,128]{2,1,0:T(8,128)S(1)} %get-tuple-element.41.refs_3_.refs_4_.refs_1_, f32[1536,128]{1,0:T(8,128)S(1)} %get-tuple-element.38.refs_0_.refs_2_, f32[1536,128]{1,0:T(8,128)S(1)} %get-tuple-element.39.refs_1_.refs_3_, ...), custom_call_target="tpu_custom_call" | custom-call | tf_op jit(solution)/shard_map/combine/pallas_call | solution.py:557
Async XLA Ops:
  2.0 7.4 %collective-permute-start = (f32[200,128]{1,0:T(8,128)S(1)}, f32[200,128]{1,0:T(8,128)S(1)}, u32[]{:S(2)}, u32[]{:S(2)}) collective-permute-start(f32[200,128]{1,0:T(8,128)S(1)} %get-tuple-element.34.refs_7_), channel_id=1, source_target_pairs={{0,4},{1,5},{2,6},{3,7},{4,0},{5,1},{6,2},{7,3},{8,12},{9,13},{10,... | collective-permute-start | bytes 307208 | tf_op jit(solution)/shard_map/ppermute | solution.py:546
  5.1 4.3 %collective-permute-start.1 = (f32[200,128]{1,0:T(8,128)S(1)}, f32[200,128]{1,0:T(8,128)S(1)}, u32[]{:S(2)}, u32[]{:S(2)}) collective-permute-start(f32[200,128]{1,0:T(8,128)S(1)} %get-tuple-element.35.refs_8_), channel_id=1, source_target_pairs={{0,1},{1,0},{2,3},{3,2},{4,8},{5,9},{6,10},{7,11},{8,4},{9,5},{10,... | collective-permute-start | bytes 307208 | tf_op jit(solution)/shard_map/ppermute | solution.py:546
  5.1 2.9 %collective-permute-start.2 = (f32[56,128]{1,0:T(8,128)S(1)}, f32[56,128]{1,0:T(8,128)S(1)}, u32[]{:S(2)}, u32[]{:S(2)}) collective-permute-start(f32[56,128]{1,0:T(8,128)S(1)} %get-tuple-element.36.refs_9_), channel_id=1, source_target_pairs={{0,1},{1,0},{2,3},{3,2},{4,5},{5,4},{6,7},{7,6},{8,9},{9,8},{10,11... | collective-permute-start | bytes 86024 | tf_op jit(solution)/shard_map/ppermute | solution.py:546
  5.6 3.4 %collective-permute-start.3 = (f32[56,128]{1,0:T(8,128)S(1)}, f32[56,128]{1,0:T(8,128)S(1)}, u32[]{:S(2)}, u32[]{:S(2)}) collective-permute-start(f32[56,128]{1,0:T(8,128)S(1)} %get-tuple-element.37.refs_10_), channel_id=1, source_target_pairs={{0,3},{1,2},{2,1},{3,0},{4,7},{5,6},{6,5},{7,4},{8,11},{9,10},{10,... | collective-permute-start | bytes 86024 | tf_op jit(solution)/shard_map/ppermute | solution.py:546
  6.7 2.7 %copy-start = (f32[6,8,128]{2,1,0:T(8,128)S(1)}, f32[6,8,128]{2,1,0:T(8,128)}, u32[]{:S(2)}) copy-start(f32[6,8,128]{2,1,0:T(8,128)} %refs_6_.1) | copy-start | bytes 73732
  10.7 6.1 %collective-permute-start.4 = (f32[72,128]{1,0:T(8,128)S(1)}, f32[72,128]{1,0:T(8,128)S(1)}, u32[]{:S(2)}, u32[]{:S(2)}) collective-permute-start(f32[72,128]{1,0:T(8,128)S(1)} %get-tuple-element.44.refs_5_), channel_id=1, source_target_pairs={{0,4},{1,5},{2,6},{3,7},{4,0},{5,1},{6,2},{7,3},{8,12},{9,13},{10,... | collective-permute-start | bytes 110600 | tf_op jit(solution)/shard_map/ppermute | solution.py:546
  13.2 3.6 %collective-permute-start.5 = (f32[72,128]{1,0:T(8,128)S(1)}, f32[72,128]{1,0:T(8,128)S(1)}, u32[]{:S(2)}, u32[]{:S(2)}) collective-permute-start(f32[72,128]{1,0:T(8,128)S(1)} %get-tuple-element.45.refs_6_), channel_id=1, source_target_pairs={{0,1},{1,0},{2,3},{3,2},{4,8},{5,9},{6,10},{7,11},{8,4},{9,5},{10,... | collective-permute-start | bytes 110600 | tf_op jit(solution)/shard_map/ppermute | solution.py:546
  13.2 2.0 %collective-permute-start.6 = (f32[24,128]{1,0:T(8,128)S(1)}, f32[24,128]{1,0:T(8,128)S(1)}, u32[]{:S(2)}, u32[]{:S(2)}) collective-permute-start(f32[24,128]{1,0:T(8,128)S(1)} %get-tuple-element.46.refs_7_), channel_id=1, source_target_pairs={{0,1},{1,0},{2,3},{3,2},{4,5},{5,4},{6,7},{7,6},{8,9},{9,8},{10,11... | collective-permute-start | bytes 36872 | tf_op jit(solution)/shard_map/ppermute | solution.py:546
  13.7 3.1 %collective-permute-start.7 = (f32[24,128]{1,0:T(8,128)S(1)}, f32[24,128]{1,0:T(8,128)S(1)}, u32[]{:S(2)}, u32[]{:S(2)}) collective-permute-start(f32[24,128]{1,0:T(8,128)S(1)} %get-tuple-element.47.refs_8_), channel_id=1, source_target_pairs={{0,3},{1,2},{2,1},{3,0},{4,7},{5,6},{6,5},{7,4},{8,11},{9,10},{10,... | collective-permute-start | bytes 36872 | tf_op jit(solution)/shard_map/ppermute | solution.py:546

commit v5 on v4

--- a/solution.py
+++ b/solution.py
@@ -165,7 +165,7 @@
 
 
 def factor_place(dof, i, j):
-    return 8 * dof + 1 + i * (i + 1) // 2 + j
+    return 8 * dof + 3 + i * (i + 1) // 2 + j
 
 
 def solve_blocks(factor, vector):
@@ -290,6 +290,8 @@
     row_kappa = dot(row_rim, row_inv)
     col_kappa = dot(col_rim, col_inv)
     coef_ref[8 * dof] = dot(row_rim, col_inv)
+    coef_ref[8 * dof + 1] = row_kappa
+    coef_ref[8 * dof + 2] = col_kappa
 
     def planes_of(group):
         return [coef_ref[group * dof + k] for k in range(dof)]
@@ -345,7 +347,7 @@
     row_odd[2 * modes:2 * modes + rows, :] = jnp.where(slab_even, first, last)
 
 
-def solve_kernel(dims, load_ref, z_ref, q_ref, coef_ref, g_ref, first_ref, sum_ref):
+def solve_kernel(dims, load_ref, z_ref, q_ref, coef_ref, g_ref, first_ref, cross_ref, sum_ref):
     modes, dof, rows, cols = dims
     for m in range(modes):
         at = [pl.ds((m * dof + k) * rows, rows) for k in range(dof)]
@@ -354,8 +356,12 @@
         for k in range(dof):
             g_ref[at[k], :] = g[k]
         z, load = [z_ref[at[k], :] for k in range(dof)], [load_ref[at[k], :] for k in range(dof)]
-        sum_ref[pl.ds(m * rows, rows), :] = dot(z, load)
-    for block in range(modes // 8):
+        for which, (left, right) in enumerate(((z, load), (z, q), (g, q))):
+            sum_ref[pl.ds((which * modes + m) * rows, rows), :] = dot(left, right)
+        for which, (group, field) in enumerate(((4, z), (5, z), (6, q), (7, q))):
+            planes = [coef_ref[group * dof + k] for k in range(dof)]
+            cross_ref[pl.ds((which * modes + m) * rows, rows), :] = dot(planes, field)
+    for block in range(3 * modes // 8):
         first_ref[block * 8:block * 8 + 8, :] = sum_of_rows(sum_ref, block * 8 * rows, rows)
 
 
@@ -366,11 +372,11 @@
     return total
 
 
-def second_kernel(dims, devices, first_ref, z_ref, qp_ref, gp_ref, coef_ref,
+def second_kernel(dims, devices, first_ref, cross_ref, gp_ref, coef_ref,
                   row_even_out, row_odd_out, col_even_out, col_odd_out,
                   row_even_in, row_odd_in, col_even_in, col_odd_in,
-                  q_ref, g_ref, q2_ref, chunk_ref,
-                  up_ref, down_ref, up2_ref, down2_ref, sum_ref):
+                  g_ref, q2_ref, chunk_ref, up_ref, down_ref, rim_ref,
+                  up2_ref, down2_ref, sum_ref):
     modes, dof, rows, cols = dims
     row, lane = tile_iota((rows, cols))
     slab_even, sub_even = parities()
@@ -405,7 +411,8 @@
 
     rim = merge(pick(left_flag, col_even_in, col_odd_in, 0, rows), pick(sub_even, col_even_in, col_odd_in, 0, rows))
     rim2 = merge(second_col(left_flag), second_col(sub_even))
-    corner_kappa = coef_ref[8 * dof]
+    corner_kappa, row_kappa, col_kappa = (coef_ref[8 * dof + i] for i in range(3))
+    rim_ref[...] = rim
 
     def planes_of(group):
         return [coef_ref[group * dof + k] for k in range(dof)]
@@ -416,8 +423,7 @@
         row_ghost = jnp.where(last_row, down_ref[pl.ds(m, 1), :], up_ref[pl.ds(m, 1), :])
         col_ghost = roll(rim, -2 * m, 1)
         col_ghost2 = roll(rim2, -2 * m, 1)
-        row_rim, col_rim, row_inv, col_inv = (planes_of(i) for i in range(4, 8))
-        q = [qp_ref[at[k], :] + (row_rim[k] * row_ghost + col_rim[k] * col_ghost) for k in range(dof)]
+        row_inv, col_inv = planes_of(6), planes_of(7)
         g = [gp_ref[at[k], :] + (row_inv[k] * row_ghost + col_inv[k] * col_ghost) for k in range(dof)]
         span, span_b, chord, chord_b = (planes_of(i) for i in range(4))
         fwd_s, bwd_s, fwd_c, bwd_c = dot(span, g), dot(span_b, g), dot(chord, g), dot(chord_b, g)
@@ -428,15 +434,18 @@
             jnp.where(first_col, col_ghost2, roll(fwd_c, 1, 1)),
         ]
         q2 = [axpy4([span[k], span_b[k], chord[k], chord_b[k]], near) for k in range(dof)]
-        z = [z_ref[at[k], :] for k in range(dof)]
         miss = (corner_kappa * col_ghost, corner_kappa * row_ghost)
         cross = miss[0] * jnp.where(last_row, near[0], near[1]) + miss[1] * jnp.where(last_col, near[2], near[3])
-        for which, (left, right) in enumerate(((z, q), (g, q), (g, q2))):
-            spot = (which * modes + m) * rows
-            total = dot(left, right)
-            sum_ref[pl.ds(spot, rows), :] = total + cross if which == 2 else total
-        for k in range(dof):
-            q_ref[at[k], :] = q[k]
+        row_z, col_z, row_q, col_q = (cross_ref[pl.ds((i * modes + m) * rows, rows), :] for i in range(4))
+        products = (
+            row_z * row_ghost + col_z * col_ghost,
+            row_ghost * (2.0 * (row_q + miss[0]) + row_kappa * row_ghost)
+            + col_ghost * (2.0 * col_q + col_kappa * col_ghost),
+            dot(g, q2) + cross,
+        )
+        for which, product in enumerate(products):
+            sum_ref[pl.ds((which * modes + m) * rows, rows), :] = product
+        for k in range(dof):
             g_ref[at[k], :] = g[k]
             q2_ref[at[k], :] = q2[k]
         mine = (lane >> 1) == m
@@ -445,8 +454,10 @@
     corners = (zero, zero)
     for m in range(modes):
         corners = body(m, corners)
-    sums = [first_ref[...]] + [sum_of_rows(sum_ref, block * 8 * rows, rows) for block in range(3 * modes // 8)]
-    sums = jnp.concatenate(sums, axis=0)
+    sums = jnp.concatenate([sum_of_rows(sum_ref, block * 8 * rows, rows) for block in range(3 * modes // 8)], axis=0)
+    sums = jnp.concatenate(
+        [first_ref[0:modes, :], first_ref[modes:3 * modes, :] + sums[0:2 * modes], sums[2 * modes:]], axis=0
+    )
     sums = jnp.sum(jnp.transpose(sums), axis=0, keepdims=True)
     chunk = jnp.where(row % LINES == 0, sums[0:1], zero)
     for which, corner in enumerate(corners):
@@ -461,7 +472,8 @@
     lax.fori_loop(0, devices * LINES // rows, send, 0, unroll=8)
 
 
-def last_kernel(dims, sizes, steps, part_ref, coef_ref, load_ref, z_ref, q_ref, g_ref, q2_ref,
+def last_kernel(dims, sizes, steps, part_ref, coef_ref, up_ref, down_ref, rim_ref,
+                load_ref, z_ref, q_ref, g_ref, q2_ref,
                 adjoint_hbm, residual_hbm, a_ref, b_ref, load_share_ref, q_share_ref, shares_ref, adjoint_ref, residual_ref, sems):
     modes, dof, rows, cols = dims
     slabs, subs = sizes
@@ -517,8 +529,10 @@
         b = b_ref[m:m + 1, :]
         load_share = load_share_ref[m:m + 1, :]
         q_share = q_share_ref[m:m + 1, :]
-        row_fix = b * jnp.where(corner, roll(row_fixes, -1 - 2 * m, 1), 0.0)
-        col_fix = b * jnp.where(corner, roll(col_fixes, -1 - 2 * m, 1), 0.0)
+        row_ghost = jnp.where(row == rows - 1, down_ref[m:m + 1, :], up_ref[m:m + 1, :])
+        col_ghost = roll(rim_ref[...], -2 * m, 1)
+        row_fix = b * jnp.where(corner, roll(row_fixes, -1 - 2 * m, 1), 0.0) + q_share * row_ghost
+        col_fix = b * jnp.where(corner, roll(col_fixes, -1 - 2 * m, 1), 0.0) + q_share * col_ghost
         for k in range(dof):
             at = pl.ds(m * per + k * rows, rows)
             adjoint_ref[at, :] = a * z_ref[at, :] + b * g_ref[at, :]
@@ -587,21 +601,21 @@
             [(modes, cols), (modes, cols), ((modes + 1) * rows, cols), ((modes + 1) * rows, cols)],
         )
         met2 = exchange(rims2)
-        gp, first = call(
+        gp, first, cross = call(
             lambda *refs: solve_kernel(dims, *refs), "solve_inner", (load, z, qp, coef), [vmem] * 4,
-            [full, (modes, cols)], [((modes + 1) * rows, cols)],
+            [full, (3 * modes, cols), (4 * modes * rows, cols)], [((3 * modes + 1) * rows, cols)],
         )
-        q, g, q2, chunk = call(
+        g, q2, chunk, up, down, rim = call(
             lambda *refs: second_kernel(dims, devices, *refs), "second_and_sums",
-            (first, z, qp, gp, coef, *rims2, *met2), [vmem] * 13,
-            [full] * 3 + [(devices * LINES, cols)],
-            [(modes, cols)] * 4 + [((3 * modes + 1) * rows, cols)],
+            (first, cross, gp, coef, *rims2, *met2), [vmem] * 12,
+            [full] * 2 + [(devices * LINES, cols), (modes, cols), (modes, cols), plane],
+            [(modes, cols)] * 2 + [((3 * modes + 1) * rows, cols)],
         )
         shares = lax.all_to_all(chunk.reshape(devices, LINES, cols), axes, 0, 0).reshape(devices * LINES, cols)
         steps = 4
         adjoint, residual = call(
             lambda *refs: last_kernel(dims, sizes, steps, *refs), "combine",
-            (shares, coef, load, z, q, g, q2), [vmem] * 7, [full] * 2,
+            (shares, coef, up, down, rim, load, z, qp, g, q2), [vmem] * 10, [full] * 2,
             [(modes, cols)] * 4 + [(devices * LINES + 8, cols), full, full, pltpu.SemaphoreType.DMA((2 * steps,))], hbm,
         )
         return adjoint.reshape(dims), residual.reshape(dims)

time: 32.4 us -> 32.1 us (level)
  waiting for transfers between devices: 3.04 us -> 2.71 us
    ppermute x8, waiting for transfers between devices: 3.04 us -> 2.71 us  [exchange(): lax.ppermute(array, axes, path)]
  transfers between devices with their start and end apart: 8 -> 8, of which waited for: 3 -> 3; matrix products, arithmetic and copies ran while one was open for 0% -> 0% of each run, Pallas kernels for 5% -> 6%
where the time goes in v5:
time: 32.1 us; the launch traced here: 32 us
  blocking collectives  12.5 us (39%)
  starting transfers between devices  8.76 us (27%)
  Pallas kernels  7.29 us (23%)
  waiting for transfers between devices  2.71 us (8%)
  between operations  0.68 us (2%)
    all_to_all x1, blocking collectives, body(): lax.all_to_all(chunk.reshape(devices, LINES, cols), axes, 0, 0)  12.5 us
    ppermute x8, starting transfers between devices, exchange(): lax.ppermute(array, axes, path)  8.76 us
    pallas_call x6, Pallas kernels, call(): pl.pallas_call(kernel, out_shape=[jax.ShapeDtypeStruct(shape, F32) for sh...  7.29 us
    ppermute x8, waiting for transfers between devices, exchange(): lax.ppermute(array, axes, path)  2.71 us
  transfers between devices with their start and end apart: 8, of which 3 were waited for; matrix products, arithmetic and copies ran while one was open for 0% of the time, Pallas kernels for 6%

profile of v5, /device:TPU:0, one launch (start us, length us, event | category | flops | bytes accessed | tf_op | source)
XLA Modules:
  0.0 32.0 jit_solution(3555812931237079695)
XLA Ops:
  0.6 1.4 %pack_rim.1 = (f32[1920,128]{1,0:T(8,128)S(1)}, f32[4,8,128]{2,1,0:T(8,128)S(1)}, f32[6,8,128]{2,1,0:T(8,128)S(1)}, f32[6,8,128]{2,1,0:T(8,128)S(1)}, f32[8,128]...) custom-call(bf16[1536,128]{1,0:T(8,128)(2,1)} %bitcast.7, ...), custom_call_target="tpu_custom_call" | custom-call | tf_op jit(solution)/shard_map/pack_rim/pallas_call | solution.py:571
  2.0 3.0 %collective-permute-start = (f32[200,128]{1,0:T(8,128)S(1)}, f32[200,128]{1,0:T(8,128)S(1)}, u32[]{:S(2)}, u32[]{:S(2)}) collective-permute-start(f32[200,128]{1,0:T(8,128)S(1)} %get-tuple-element.37.refs_7_), channel_id=1, source_target_pairs={{0,4},{1,5},{2,6},{3,7},{4,0},{5,1},{6,2},{7,3},{8,12},{9,13},{10,... | collective-permute-start | bytes 307208 | tf_op jit(solution)/shard_map/ppermute | solution.py:560
  5.1 0.0 collective-permute-start.1
  5.1 0.5 %collective-permute-start.2 = (f32[56,128]{1,0:T(8,128)S(1)}, f32[56,128]{1,0:T(8,128)S(1)}, u32[]{:S(2)}, u32[]{:S(2)}) collective-permute-start(f32[56,128]{1,0:T(8,128)S(1)} %get-tuple-element.39.refs_9_), channel_id=1, source_target_pairs={{0,1},{1,0},{2,3},{3,2},{4,5},{5,4},{6,7},{7,6},{8,9},{9,8},{10,11... | collective-permute-start | bytes 86024 | tf_op jit(solution)/shard_map/ppermute | solution.py:560
  5.6 1.1 %collective-permute-start.3 = (f32[56,128]{1,0:T(8,128)S(1)}, f32[56,128]{1,0:T(8,128)S(1)}, u32[]{:S(2)}, u32[]{:S(2)}) collective-permute-start(f32[56,128]{1,0:T(8,128)S(1)} %get-tuple-element.40.refs_10_), channel_id=1, source_target_pairs={{0,3},{1,2},{2,1},{3,0},{4,7},{5,6},{6,5},{7,4},{8,11},{9,10},{10,... | collective-permute-start | bytes 86024 | tf_op jit(solution)/shard_map/ppermute | solution.py:560
  6.7 0.0 copy-start
  6.7 1.3 %inner_load.1.refs_0_ = f32[1536,128]{1,0:T(8,128)S(1)} custom-call(f32[1920,128]{1,0:T(8,128)S(1)} %get-tuple-element.31.refs_0_, f32[4,8,128]{2,1,0:T(8,128)S(1)} %get-tuple-element.32.refs_1_, f32[6,8,128]{2,1,0:T(8,128)S(1)} %get-tuple-element.33.refs_2_, f32[6,8,128]{2,1,0:T(8,128)S(1)} %get-tuple-element.34.refs_3_, ...), custom_call_target="tpu_custom_call" | custom-call | tf_op jit(solution)/shard_map/inner_load/pallas_call | solution.py:571
  8.0 0.0 collective-permute-done.2.refs_13_
  8.0 1.0 %collective-permute-done.3.refs_14_ = f32[56,128]{1,0:T(8,128)S(1)} collective-permute-done((f32[56,128]{1,0:T(8,128)S(1)}, f32[56,128]{1,0:T(8,128)S(1)}, u32[]{:S(2)}, u32[]{:S(2)}) %collective-permute-start.3) | collective-permute-done | bytes 28704 | tf_op jit(solution)/shard_map/ppermute | solution.py:560
  9.0 0.4 %collective-permute-done.refs_11_ = f32[200,128]{1,0:T(8,128)S(1)} collective-permute-done((f32[200,128]{1,0:T(8,128)S(1)}, f32[200,128]{1,0:T(8,128)S(1)}, u32[]{:S(2)}, u32[]{:S(2)}) %collective-permute-start) | collective-permute-done | bytes 102432 | tf_op jit(solution)/shard_map/ppermute | solution.py:560
  9.4 0.0 collective-permute-done.1.refs_12_
  9.4 0.0 copy-done
  9.4 1.3 %load_and_first.1 = (f32[1536,128]{1,0:T(8,128)S(1)}, f32[1536,128]{1,0:T(8,128)S(1)}, f32[1536,128]{1,0:T(8,128)S(1)}, f32[72,8,128]{2,1,0:T(8,128)S(1)}, f32[7...) custom-call(f32[1536,128]{1,0:T(8,128)S(1)} %inner_load.1.refs_0_, ...), custom_call_target="tpu_custom_call" | custom-call | tf_op jit(solution)/shard_map/load_and_first/pallas_call | solution.py:571
  10.7 2.5 %collective-permute-start.4 = (f32[72,128]{1,0:T(8,128)S(1)}, f32[72,128]{1,0:T(8,128)S(1)}, u32[]{:S(2)}, u32[]{:S(2)}) collective-permute-start(f32[72,128]{1,0:T(8,128)S(1)} %get-tuple-element.48.refs_4_), channel_id=1, source_target_pairs={{0,4},{1,5},{2,6},{3,7},{4,0},{5,1},{6,2},{7,3},{8,12},{9,13},{10,... | collective-permute-start | bytes 110600 | tf_op jit(solution)/shard_map/ppermute | solution.py:560
  13.2 0.0 collective-permute-start.5
  13.2 0.5 %collective-permute-start.6 = (f32[24,128]{1,0:T(8,128)S(1)}, f32[24,128]{1,0:T(8,128)S(1)}, u32[]{:S(2)}, u32[]{:S(2)}) collective-permute-start(f32[24,128]{1,0:T(8,128)S(1)} %get-tuple-element.50.refs_6_), channel_id=1, source_target_pairs={{0,1},{1,0},{2,3},{3,2},{4,5},{5,4},{6,7},{7,6},{8,9},{9,8},{10,11... | collective-permute-start | bytes 36872 | tf_op jit(solution)/shard_map/ppermute | solution.py:560
  13.7 1.1 %collective-permute-start.7 = (f32[24,128]{1,0:T(8,128)S(1)}, f32[24,128]{1,0:T(8,128)S(1)}, u32[]{:S(2)}, u32[]{:S(2)}) collective-permute-start(f32[24,128]{1,0:T(8,128)S(1)} %get-tuple-element.51.refs_7_), channel_id=1, source_target_pairs={{0,3},{1,2},{2,1},{3,0},{4,7},{5,6},{6,5},{7,4},{8,11},{9,10},{10,... | collective-permute-start | bytes 36872 | tf_op jit(solution)/shard_map/ppermute | solution.py:560
  14.8 0.7 %solve_inner.1 = (f32[1536,128]{1,0:T(8,128)S(1)}, f32[96,128]{1,0:T(8,128)S(1)}, f32[1024,128]{1,0:T(8,128)S(1)}) custom-call(f32[1536,128]{1,0:T(8,128)S(1)} %get-tuple-element.41.refs_0_.refs_5_, f32[1536,128]{1,0:T(8,128)S(1)} %get-tuple-element.42.refs_1_.refs_6_, f32[1536,128]{1,0:T(8,128)S(1)} %get-tuple-element.43.refs_2_.refs_7_, ...), custom_call_target="tpu_custom_call" | custom-call | tf_op jit(solution)/shard_map/solve_inner/pallas_call | solution.py:571
  15.5 0.0 collective-permute-done.6.refs_10_
  15.5 1.3 %collective-permute-done.7.refs_11_ = f32[24,128]{1,0:T(8,128)S(1)} collective-permute-done((f32[24,128]{1,0:T(8,128)S(1)}, f32[24,128]{1,0:T(8,128)S(1)}, u32[]{:S(2)}, u32[]{:S(2)}) %collective-permute-start.7) | collective-permute-done | bytes 12320 | tf_op jit(solution)/shard_map/ppermute | solution.py:560
  16.8 0.0 collective-permute-done.4.refs_8_
  16.8 0.0 collective-permute-done.5.refs_9_
  16.8 0.9 %second_and_sums.1 = (f32[1536,128]{1,0:T(8,128)S(1)}, f32[1536,128]{1,0:T(8,128)S(1)}, f32[128,128]{1,0:T(8,128)S(1)}, f32[32,128]{1,0:T(8,128)S(1)}, f32[32,128]{1,0:T(8,128)S(1)}, /*index=5*/f32[8,128]{1,0:T(8,128)S(1)}) custom-call(f32[96,128]{1,0:T(8,128)S(1)} %get-tuple-element.45.refs_0_, f32[1024,128]{1,0:T(8,128)S(1)} %get-tuple-element.46.refs_1_, ...), custom_call_target="tpu_custom_call" | custom-call | tf_op jit(solution)/shard_map/second_and_sums/pallas_call | solution.py:571
  17.8 12.5 %all_to_all.5 = f32[32,4,128]{2,1,0:T(4,128)S(1)} all-to-all(f32[32,4,128]{2,1,0:T(4,128)S(1)} %bitcast.6), channel_id=1, replica_groups=mesh['slab'=8,'sub'=4] {'slab','sub'}, dimensions={0} | all-to-all | bytes 131072 | tf_op jit(solution)/shard_map/all_to_all | solution.py:614
  30.3 1.7 %combine.1 = (f32[1536,128]{1,0:T(8,128)}, f32[1536,128]{1,0:T(8,128)}) custom-call(f32[128,128]{1,0:T(8,128)S(1)} %bitcast.5, f32[72,8,128]{2,1,0:T(8,128)S(1)} %get-tuple-element.44.refs_3_.refs_1_, f32[32,128]{1,0:T(8,128)S(1)} %get-tuple-element.53.refs_2_, f32[32,128]{1,0:T(8,128)S(1)} %get-tuple-element.54.refs_3_, ...), custom_call_target="tpu_custom_call" | custom-call | tf_op jit(solution)/shard_map/combine/pallas_call | solution.py:571
Async XLA Ops:
  2.0 7.4 %collective-permute-start = (f32[200,128]{1,0:T(8,128)S(1)}, f32[200,128]{1,0:T(8,128)S(1)}, u32[]{:S(2)}, u32[]{:S(2)}) collective-permute-start(f32[200,128]{1,0:T(8,128)S(1)} %get-tuple-element.37.refs_7_), channel_id=1, source_target_pairs={{0,4},{1,5},{2,6},{3,7},{4,0},{5,1},{6,2},{7,3},{8,12},{9,13},{10,... | collective-permute-start | bytes 307208 | tf_op jit(solution)/shard_map/ppermute | solution.py:560
  5.1 4.3 %collective-permute-start.1 = (f32[200,128]{1,0:T(8,128)S(1)}, f32[200,128]{1,0:T(8,128)S(1)}, u32[]{:S(2)}, u32[]{:S(2)}) collective-permute-start(f32[200,128]{1,0:T(8,128)S(1)} %get-tuple-element.38.refs_8_), channel_id=1, source_target_pairs={{0,1},{1,0},{2,3},{3,2},{4,8},{5,9},{6,10},{7,11},{8,4},{9,5},{10,... | collective-permute-start | bytes 307208 | tf_op jit(solution)/shard_map/ppermute | solution.py:560
  5.1 2.9 %collective-permute-start.2 = (f32[56,128]{1,0:T(8,128)S(1)}, f32[56,128]{1,0:T(8,128)S(1)}, u32[]{:S(2)}, u32[]{:S(2)}) collective-permute-start(f32[56,128]{1,0:T(8,128)S(1)} %get-tuple-element.39.refs_9_), channel_id=1, source_target_pairs={{0,1},{1,0},{2,3},{3,2},{4,5},{5,4},{6,7},{7,6},{8,9},{9,8},{10,11... | collective-permute-start | bytes 86024 | tf_op jit(solution)/shard_map/ppermute | solution.py:560
  5.6 3.4 %collective-permute-start.3 = (f32[56,128]{1,0:T(8,128)S(1)}, f32[56,128]{1,0:T(8,128)S(1)}, u32[]{:S(2)}, u32[]{:S(2)}) collective-permute-start(f32[56,128]{1,0:T(8,128)S(1)} %get-tuple-element.40.refs_10_), channel_id=1, source_target_pairs={{0,3},{1,2},{2,1},{3,0},{4,7},{5,6},{6,5},{7,4},{8,11},{9,10},{10,... | collective-permute-start | bytes 86024 | tf_op jit(solution)/shard_map/ppermute | solution.py:560
  6.7 2.7 %copy-start = (f32[6,8,128]{2,1,0:T(8,128)S(1)}, f32[6,8,128]{2,1,0:T(8,128)}, u32[]{:S(2)}) copy-start(f32[6,8,128]{2,1,0:T(8,128)} %refs_6_.1) | copy-start | bytes 73732
  10.7 6.1 %collective-permute-start.4 = (f32[72,128]{1,0:T(8,128)S(1)}, f32[72,128]{1,0:T(8,128)S(1)}, u32[]{:S(2)}, u32[]{:S(2)}) collective-permute-start(f32[72,128]{1,0:T(8,128)S(1)} %get-tuple-element.48.refs_4_), channel_id=1, source_target_pairs={{0,4},{1,5},{2,6},{3,7},{4,0},{5,1},{6,2},{7,3},{8,12},{9,13},{10,... | collective-permute-start | bytes 110600 | tf_op jit(solution)/shard_map/ppermute | solution.py:560
  13.2 3.6 %collective-permute-start.5 = (f32[72,128]{1,0:T(8,128)S(1)}, f32[72,128]{1,0:T(8,128)S(1)}, u32[]{:S(2)}, u32[]{:S(2)}) collective-permute-start(f32[72,128]{1,0:T(8,128)S(1)} %get-tuple-element.49.refs_5_), channel_id=1, source_target_pairs={{0,1},{1,0},{2,3},{3,2},{4,8},{5,9},{6,10},{7,11},{8,4},{9,5},{10,... | collective-permute-start | bytes 110600 | tf_op jit(solution)/shard_map/ppermute | solution.py:560
  13.2 2.3 %collective-permute-start.6 = (f32[24,128]{1,0:T(8,128)S(1)}, f32[24,128]{1,0:T(8,128)S(1)}, u32[]{:S(2)}, u32[]{:S(2)}) collective-permute-start(f32[24,128]{1,0:T(8,128)S(1)} %get-tuple-element.50.refs_6_), channel_id=1, source_target_pairs={{0,1},{1,0},{2,3},{3,2},{4,5},{5,4},{6,7},{7,6},{8,9},{9,8},{10,11... | collective-permute-start | bytes 36872 | tf_op jit(solution)/shard_map/ppermute | solution.py:560
  13.7 3.1 %collective-permute-start.7 = (f32[24,128]{1,0:T(8,128)S(1)}, f32[24,128]{1,0:T(8,128)S(1)}, u32[]{:S(2)}, u32[]{:S(2)}) collective-permute-start(f32[24,128]{1,0:T(8,128)S(1)} %get-tuple-element.51.refs_7_), channel_id=1, source_target_pairs={{0,3},{1,2},{2,1},{3,0},{4,7},{5,6},{6,5},{7,4},{8,11},{9,10},{10,... | collective-permute-start | bytes 36872 | tf_op jit(solution)/shard_map/ppermute | solution.py:560

commit v6 on v5

--- a/solution.py
+++ b/solution.py
@@ -524,8 +524,22 @@
     corner = ((row == 0) | (row == rows - 1)) & ((lane == 0) | (lane == cols - 1))
     count = modes // steps
     copies = []
+
+    def store(m, src, dst):
+        if (m + 1) % count == 0:
+            at = pl.ds((m + 1 - count) * per, count * per)
+            copy = pltpu.make_async_copy(src.at[at, :], dst.at[at, :], sems.at[len(copies)])
+            copy.start()
+            copies.append(copy)
+
     for m in range(modes):
         a = a_ref[m:m + 1, :]
+        b = b_ref[m:m + 1, :]
+        for k in range(dof):
+            at = pl.ds(m * per + k * rows, rows)
+            adjoint_ref[at, :] = a * z_ref[at, :] + b * g_ref[at, :]
+        store(m, adjoint_ref, adjoint_hbm)
+    for m in range(modes):
         b = b_ref[m:m + 1, :]
         load_share = load_share_ref[m:m + 1, :]
         q_share = q_share_ref[m:m + 1, :]
@@ -535,17 +549,11 @@
         col_fix = b * jnp.where(corner, roll(col_fixes, -1 - 2 * m, 1), 0.0) + q_share * col_ghost
         for k in range(dof):
             at = pl.ds(m * per + k * rows, rows)
-            adjoint_ref[at, :] = a * z_ref[at, :] + b * g_ref[at, :]
             residual_ref[at, :] = (
                 (load_share * load_ref[at, :] + q_share * q_ref[at, :])
                 + (b * q2_ref[at, :] + (coef_ref[4 * dof + k] * row_fix + coef_ref[5 * dof + k] * col_fix))
             )
-        if (m + 1) % count == 0:
-            at = pl.ds((m + 1 - count) * per, count * per)
-            for src, dst in ((adjoint_ref, adjoint_hbm), (residual_ref, residual_hbm)):
-                copy = pltpu.make_async_copy(src.at[at, :], dst.at[at, :], sems.at[len(copies)])
-                copy.start()
-                copies.append(copy)
+        store(m, residual_ref, residual_hbm)
     for copy in copies:
         copy.wait()
 

time: 32.1 us -> 32.2 us (level)
  no operation moved by 1% of the time
where the time goes in v6:
time: 32.2 us; the launch traced here: 32 us
  blocking collectives  12.5 us (39%)
  starting transfers between devices  8.76 us (27%)
  Pallas kernels  7.35 us (23%)
  waiting for transfers between devices  2.71 us (8%)
  between operations  0.68 us (2%)
    all_to_all x1, blocking collectives, body(): lax.all_to_all(chunk.reshape(devices, LINES, cols), axes, 0, 0)  12.5 us
    ppermute x8, starting transfers between devices, exchange(): lax.ppermute(array, axes, path)  8.76 us
    pallas_call x6, Pallas kernels, call(): pl.pallas_call(kernel, out_shape=[jax.ShapeDtypeStruct(shape, F32) for sh...  7.35 us
    ppermute x8, waiting for transfers between devices, exchange(): lax.ppermute(array, axes, path)  2.71 us
  transfers between devices with their start and end apart: 8, of which 3 were waited for; matrix products, arithmetic and copies ran while one was open for 0% of the time, Pallas kernels for 6%

profile of v6, /device:TPU:0, one launch (start us, length us, event | category | flops | bytes accessed | tf_op | source)
XLA Modules:
  0.0 32.0 jit_solution(13178565159978612679)
XLA Ops:
  0.6 1.4 %pack_rim.1 = (f32[1920,128]{1,0:T(8,128)S(1)}, f32[4,8,128]{2,1,0:T(8,128)S(1)}, f32[6,8,128]{2,1,0:T(8,128)S(1)}, f32[6,8,128]{2,1,0:T(8,128)S(1)}, f32[8,128]...) custom-call(bf16[1536,128]{1,0:T(8,128)(2,1)} %bitcast.7, ...), custom_call_target="tpu_custom_call" | custom-call | tf_op jit(solution)/shard_map/pack_rim/pallas_call | solution.py:579
  2.0 3.0 %collective-permute-start = (f32[200,128]{1,0:T(8,128)S(1)}, f32[200,128]{1,0:T(8,128)S(1)}, u32[]{:S(2)}, u32[]{:S(2)}) collective-permute-start(f32[200,128]{1,0:T(8,128)S(1)} %get-tuple-element.37.refs_7_), channel_id=1, source_target_pairs={{0,4},{1,5},{2,6},{3,7},{4,0},{5,1},{6,2},{7,3},{8,12},{9,13},{10,... | collective-permute-start | bytes 307208 | tf_op jit(solution)/shard_map/ppermute | solution.py:568
  5.1 0.0 collective-permute-start.1
  5.1 0.5 %collective-permute-start.2 = (f32[56,128]{1,0:T(8,128)S(1)}, f32[56,128]{1,0:T(8,128)S(1)}, u32[]{:S(2)}, u32[]{:S(2)}) collective-permute-start(f32[56,128]{1,0:T(8,128)S(1)} %get-tuple-element.39.refs_9_), channel_id=1, source_target_pairs={{0,1},{1,0},{2,3},{3,2},{4,5},{5,4},{6,7},{7,6},{8,9},{9,8},{10,11... | collective-permute-start | bytes 86024 | tf_op jit(solution)/shard_map/ppermute | solution.py:568
  5.6 1.1 %collective-permute-start.3 = (f32[56,128]{1,0:T(8,128)S(1)}, f32[56,128]{1,0:T(8,128)S(1)}, u32[]{:S(2)}, u32[]{:S(2)}) collective-permute-start(f32[56,128]{1,0:T(8,128)S(1)} %get-tuple-element.40.refs_10_), channel_id=1, source_target_pairs={{0,3},{1,2},{2,1},{3,0},{4,7},{5,6},{6,5},{7,4},{8,11},{9,10},{10,... | collective-permute-start | bytes 86024 | tf_op jit(solution)/shard_map/ppermute | solution.py:568
  6.7 0.0 copy-start
  6.7 1.3 %inner_load.1.refs_0_ = f32[1536,128]{1,0:T(8,128)S(1)} custom-call(f32[1920,128]{1,0:T(8,128)S(1)} %get-tuple-element.31.refs_0_, f32[4,8,128]{2,1,0:T(8,128)S(1)} %get-tuple-element.32.refs_1_, f32[6,8,128]{2,1,0:T(8,128)S(1)} %get-tuple-element.33.refs_2_, f32[6,8,128]{2,1,0:T(8,128)S(1)} %get-tuple-element.34.refs_3_, ...), custom_call_target="tpu_custom_call" | custom-call | tf_op jit(solution)/shard_map/inner_load/pallas_call | solution.py:579
  8.0 0.0 collective-permute-done.2.refs_13_
  8.0 1.0 %collective-permute-done.3.refs_14_ = f32[56,128]{1,0:T(8,128)S(1)} collective-permute-done((f32[56,128]{1,0:T(8,128)S(1)}, f32[56,128]{1,0:T(8,128)S(1)}, u32[]{:S(2)}, u32[]{:S(2)}) %collective-permute-start.3) | collective-permute-done | bytes 28704 | tf_op jit(solution)/shard_map/ppermute | solution.py:568
  9.0 0.4 %collective-permute-done.refs_11_ = f32[200,128]{1,0:T(8,128)S(1)} collective-permute-done((f32[200,128]{1,0:T(8,128)S(1)}, f32[200,128]{1,0:T(8,128)S(1)}, u32[]{:S(2)}, u32[]{:S(2)}) %collective-permute-start) | collective-permute-done | bytes 102432 | tf_op jit(solution)/shard_map/ppermute | solution.py:568
  9.4 0.0 collective-permute-done.1.refs_12_
  9.4 0.0 copy-done
  9.4 1.3 %load_and_first.1 = (f32[1536,128]{1,0:T(8,128)S(1)}, f32[1536,128]{1,0:T(8,128)S(1)}, f32[1536,128]{1,0:T(8,128)S(1)}, f32[72,8,128]{2,1,0:T(8,128)S(1)}, f32[7...) custom-call(f32[1536,128]{1,0:T(8,128)S(1)} %inner_load.1.refs_0_, ...), custom_call_target="tpu_custom_call" | custom-call | tf_op jit(solution)/shard_map/load_and_first/pallas_call | solution.py:579
  10.7 2.5 %collective-permute-start.4 = (f32[72,128]{1,0:T(8,128)S(1)}, f32[72,128]{1,0:T(8,128)S(1)}, u32[]{:S(2)}, u32[]{:S(2)}) collective-permute-start(f32[72,128]{1,0:T(8,128)S(1)} %get-tuple-element.48.refs_4_), channel_id=1, source_target_pairs={{0,4},{1,5},{2,6},{3,7},{4,0},{5,1},{6,2},{7,3},{8,12},{9,13},{10,... | collective-permute-start | bytes 110600 | tf_op jit(solution)/shard_map/ppermute | solution.py:568
  13.2 0.0 collective-permute-start.5
  13.2 0.5 %collective-permute-start.6 = (f32[24,128]{1,0:T(8,128)S(1)}, f32[24,128]{1,0:T(8,128)S(1)}, u32[]{:S(2)}, u32[]{:S(2)}) collective-permute-start(f32[24,128]{1,0:T(8,128)S(1)} %get-tuple-element.50.refs_6_), channel_id=1, source_target_pairs={{0,1},{1,0},{2,3},{3,2},{4,5},{5,4},{6,7},{7,6},{8,9},{9,8},{10,11... | collective-permute-start | bytes 36872 | tf_op jit(solution)/shard_map/ppermute | solution.py:568
  13.7 1.1 %collective-permute-start.7 = (f32[24,128]{1,0:T(8,128)S(1)}, f32[24,128]{1,0:T(8,128)S(1)}, u32[]{:S(2)}, u32[]{:S(2)}) collective-permute-start(f32[24,128]{1,0:T(8,128)S(1)} %get-tuple-element.51.refs_7_), channel_id=1, source_target_pairs={{0,3},{1,2},{2,1},{3,0},{4,7},{5,6},{6,5},{7,4},{8,11},{9,10},{10,... | collective-permute-start | bytes 36872 | tf_op jit(solution)/shard_map/ppermute | solution.py:568
  14.8 0.7 %solve_inner.1 = (f32[1536,128]{1,0:T(8,128)S(1)}, f32[96,128]{1,0:T(8,128)S(1)}, f32[1024,128]{1,0:T(8,128)S(1)}) custom-call(f32[1536,128]{1,0:T(8,128)S(1)} %get-tuple-element.41.refs_0_.refs_5_, f32[1536,128]{1,0:T(8,128)S(1)} %get-tuple-element.42.refs_1_.refs_6_, f32[1536,128]{1,0:T(8,128)S(1)} %get-tuple-element.43.refs_2_.refs_7_, ...), custom_call_target="tpu_custom_call" | custom-call | tf_op jit(solution)/shard_map/solve_inner/pallas_call | solution.py:579
  15.5 0.0 collective-permute-done.6.refs_10_
  15.5 1.3 %collective-permute-done.7.refs_11_ = f32[24,128]{1,0:T(8,128)S(1)} collective-permute-done((f32[24,128]{1,0:T(8,128)S(1)}, f32[24,128]{1,0:T(8,128)S(1)}, u32[]{:S(2)}, u32[]{:S(2)}) %collective-permute-start.7) | collective-permute-done | bytes 12320 | tf_op jit(solution)/shard_map/ppermute | solution.py:568
  16.8 0.0 collective-permute-done.4.refs_8_
  16.8 0.0 collective-permute-done.5.refs_9_
  16.8 0.9 %second_and_sums.1 = (f32[1536,128]{1,0:T(8,128)S(1)}, f32[1536,128]{1,0:T(8,128)S(1)}, f32[128,128]{1,0:T(8,128)S(1)}, f32[32,128]{1,0:T(8,128)S(1)}, f32[32,128]{1,0:T(8,128)S(1)}, /*index=5*/f32[8,128]{1,0:T(8,128)S(1)}) custom-call(f32[96,128]{1,0:T(8,128)S(1)} %get-tuple-element.45.refs_0_, f32[1024,128]{1,0:T(8,128)S(1)} %get-tuple-element.46.refs_1_, ...), custom_call_target="tpu_custom_call" | custom-call | tf_op jit(solution)/shard_map/second_and_sums/pallas_call | solution.py:579
  17.8 12.5 %all_to_all.5 = f32[32,4,128]{2,1,0:T(4,128)S(1)} all-to-all(f32[32,4,128]{2,1,0:T(4,128)S(1)} %bitcast.6), channel_id=1, replica_groups=mesh['slab'=8,'sub'=4] {'slab','sub'}, dimensions={0} | all-to-all | bytes 131072 | tf_op jit(solution)/shard_map/all_to_all | solution.py:622
  30.3 1.7 %combine.1 = (f32[1536,128]{1,0:T(8,128)}, f32[1536,128]{1,0:T(8,128)}) custom-call(f32[128,128]{1,0:T(8,128)S(1)} %bitcast.5, f32[72,8,128]{2,1,0:T(8,128)S(1)} %get-tuple-element.44.refs_3_.refs_1_, f32[32,128]{1,0:T(8,128)S(1)} %get-tuple-element.53.refs_2_, f32[32,128]{1,0:T(8,128)S(1)} %get-tuple-element.54.refs_3_, ...), custom_call_target="tpu_custom_call" | custom-call | tf_op jit(solution)/shard_map/combine/pallas_call | solution.py:579
Async XLA Ops:
  2.0 7.4 %collective-permute-start = (f32[200,128]{1,0:T(8,128)S(1)}, f32[200,128]{1,0:T(8,128)S(1)}, u32[]{:S(2)}, u32[]{:S(2)}) collective-permute-start(f32[200,128]{1,0:T(8,128)S(1)} %get-tuple-element.37.refs_7_), channel_id=1, source_target_pairs={{0,4},{1,5},{2,6},{3,7},{4,0},{5,1},{6,2},{7,3},{8,12},{9,13},{10,... | collective-permute-start | bytes 307208 | tf_op jit(solution)/shard_map/ppermute | solution.py:568
  5.1 4.3 %collective-permute-start.1 = (f32[200,128]{1,0:T(8,128)S(1)}, f32[200,128]{1,0:T(8,128)S(1)}, u32[]{:S(2)}, u32[]{:S(2)}) collective-permute-start(f32[200,128]{1,0:T(8,128)S(1)} %get-tuple-element.38.refs_8_), channel_id=1, source_target_pairs={{0,1},{1,0},{2,3},{3,2},{4,8},{5,9},{6,10},{7,11},{8,4},{9,5},{10,... | collective-permute-start | bytes 307208 | tf_op jit(solution)/shard_map/ppermute | solution.py:568
  5.1 2.9 %collective-permute-start.2 = (f32[56,128]{1,0:T(8,128)S(1)}, f32[56,128]{1,0:T(8,128)S(1)}, u32[]{:S(2)}, u32[]{:S(2)}) collective-permute-start(f32[56,128]{1,0:T(8,128)S(1)} %get-tuple-element.39.refs_9_), channel_id=1, source_target_pairs={{0,1},{1,0},{2,3},{3,2},{4,5},{5,4},{6,7},{7,6},{8,9},{9,8},{10,11... | collective-permute-start | bytes 86024 | tf_op jit(solution)/shard_map/ppermute | solution.py:568
  5.6 3.4 %collective-permute-start.3 = (f32[56,128]{1,0:T(8,128)S(1)}, f32[56,128]{1,0:T(8,128)S(1)}, u32[]{:S(2)}, u32[]{:S(2)}) collective-permute-start(f32[56,128]{1,0:T(8,128)S(1)} %get-tuple-element.40.refs_10_), channel_id=1, source_target_pairs={{0,3},{1,2},{2,1},{3,0},{4,7},{5,6},{6,5},{7,4},{8,11},{9,10},{10,... | collective-permute-start | bytes 86024 | tf_op jit(solution)/shard_map/ppermute | solution.py:568
  6.7 2.7 %copy-start = (f32[6,8,128]{2,1,0:T(8,128)S(1)}, f32[6,8,128]{2,1,0:T(8,128)}, u32[]{:S(2)}) copy-start(f32[6,8,128]{2,1,0:T(8,128)} %refs_6_.1) | copy-start | bytes 73732
  10.7 6.1 %collective-permute-start.4 = (f32[72,128]{1,0:T(8,128)S(1)}, f32[72,128]{1,0:T(8,128)S(1)}, u32[]{:S(2)}, u32[]{:S(2)}) collective-permute-start(f32[72,128]{1,0:T(8,128)S(1)} %get-tuple-element.48.refs_4_), channel_id=1, source_target_pairs={{0,4},{1,5},{2,6},{3,7},{4,0},{5,1},{6,2},{7,3},{8,12},{9,13},{10,... | collective-permute-start | bytes 110600 | tf_op jit(solution)/shard_map/ppermute | solution.py:568
  13.2 3.6 %collective-permute-start.5 = (f32[72,128]{1,0:T(8,128)S(1)}, f32[72,128]{1,0:T(8,128)S(1)}, u32[]{:S(2)}, u32[]{:S(2)}) collective-permute-start(f32[72,128]{1,0:T(8,128)S(1)} %get-tuple-element.49.refs_5_), channel_id=1, source_target_pairs={{0,1},{1,0},{2,3},{3,2},{4,8},{5,9},{6,10},{7,11},{8,4},{9,5},{10,... | collective-permute-start | bytes 110600 | tf_op jit(solution)/shard_map/ppermute | solution.py:568
  13.2 2.3 %collective-permute-start.6 = (f32[24,128]{1,0:T(8,128)S(1)}, f32[24,128]{1,0:T(8,128)S(1)}, u32[]{:S(2)}, u32[]{:S(2)}) collective-permute-start(f32[24,128]{1,0:T(8,128)S(1)} %get-tuple-element.50.refs_6_), channel_id=1, source_target_pairs={{0,1},{1,0},{2,3},{3,2},{4,5},{5,4},{6,7},{7,6},{8,9},{9,8},{10,11... | collective-permute-start | bytes 36872 | tf_op jit(solution)/shard_map/ppermute | solution.py:568
  13.7 3.1 %collective-permute-start.7 = (f32[24,128]{1,0:T(8,128)S(1)}, f32[24,128]{1,0:T(8,128)S(1)}, u32[]{:S(2)}, u32[]{:S(2)}) collective-permute-start(f32[24,128]{1,0:T(8,128)S(1)} %get-tuple-element.51.refs_7_), channel_id=1, source_target_pairs={{0,3},{1,2},{2,1},{3,0},{4,7},{5,6},{6,5},{7,4},{8,11},{9,10},{10,... | collective-permute-start | bytes 36872 | tf_op jit(solution)/shard_map/ppermute | solution.py:568
